TPU v7x, 32 devices: a whole 2x2x4 slice. The times are simulated.
32 devices in a mesh: replica: 16 (over z, y, core), shard: 2 (over x).
Axes of the slice: x: 2, y: 2, z: 4, core: 2. Of those that a mesh axis runs over, the one named last changes fastest.
Arguments:
- tokens: bfloat16 [16, 1024, 1088], P('replica', 'shard'), may hold values from -6 to 6
- qkv_weight: bfloat16 [1088, 3264], P('shard'), may hold values from -0.1875 to 0.1875
- out_weight: bfloat16 [1088, 1088], P('shard'), may hold values from -4 to 4
- up_weight: bfloat16 [1088, 4352], P('shard'), may hold values from -0.1875 to 0.1875
- down_weight: bfloat16 [4352, 1088], P('shard'), may hold values from -0.09375 to 0.09375
- attn_gain: bfloat16 [1088], P('shard'), may hold values from 0.099609375 to 1.8984375
- attn_shift: bfloat16 [1088], P('shard'), may hold values from -3 to 3
- query_bias: bfloat16 [1088], P('shard'), may hold values from -3 to 3
- value_bias: bfloat16 [1088], P('shard'), may hold values from -3 to 3
- out_bias: bfloat16 [1088], P('shard'), may hold values from -3 to 3
- mlp_gain: bfloat16 [1088], P('shard'), may hold values from 0.099609375 to 1.8984375
- mlp_shift: bfloat16 [1088], P('shard'), may hold values from -3 to 3
- up_bias: bfloat16 [4352], P('shard'), may hold values from -3 to 3
- down_bias: bfloat16 [1088], P('shard'), may hold values from -3 to 3
- cotangent: bfloat16 [16, 1024, 1088], P('replica', 'shard'), may hold values from -6 to 6
Outputs:
- block_out: bfloat16 [16, 1024, 1088], P('replica', 'shard')
- grad_tokens: bfloat16 [16, 1024, 1088], P('replica', 'shard')
- grad_qkv_weight: float32 [1088, 3264], P('shard')
- grad_out_weight: float32 [1088, 1088], P('shard')
- grad_up_weight: float32 [1088, 4352], P('shard')
- grad_down_weight: float32 [4352, 1088], P('shard')
- grad_attn_gain: float32 [1088], P('shard')
- grad_attn_shift: float32 [1088], P('shard')
- grad_query_bias: float32 [1088], P('shard')
- grad_value_bias: float32 [1088], P('shard')
- grad_out_bias: float32 [1088], P('shard')
- grad_mlp_gain: float32 [1088], P('shard')
- grad_mlp_shift: float32 [1088], P('shard')
- grad_up_bias: float32 [4352], P('shard')
- grad_down_bias: float32 [1088], P('shard')
All inputs are finite; a program needn't handle non-finite values.
Results may differ from a plain program's by a relative error of at most 0.019.
Values may be sent and summed in bfloat16 or wider, within the bound.
No kernel may reach another device: no remote copies, remote signals or barrier semaphores. Data moves between devices by JAX's collectives and lax.ppermute only.
A program may use at most 256 MiB of HBM per device.

v0:
```python
import jax
import jax.numpy as jnp
from jax import lax
from jax.sharding import PartitionSpec as P

HEADS = 17
HD = 64


EPSILON = 1e-05
SCALING = 0.125


def norm_rows(values, gain, shift):
    average = jnp.mean(values, axis=-1, keepdims=True)
    centered = values - average
    variance = jnp.mean(centered * centered, axis=-1, keepdims=True)
    return centered * lax.rsqrt(variance + EPSILON) * gain + shift


def gelu_curve(values):
    inner = 0.7978845608 * (values + 0.044715 * values * values * values)
    return 0.5 * values * (1.0 + jnp.tanh(inner))


def times_transposed(left, right):
    return lax.dot_general(
        left, right, (((1,), (1,)), ((), ())), preferred_element_type=jnp.float32
    )


def transposed_times(left, right):
    return lax.dot_general(
        left, right, (((0,), (0,)), ((), ())), preferred_element_type=jnp.float32
    )


def on_device(
    tokens,
    qkv_weight,
    out_weight,
    up_weight,
    down_weight,
    attn_gain,
    attn_shift,
    query_bias,
    value_bias,
    out_bias,
    mlp_gain,
    mlp_shift,
    up_bias,
    down_bias,
    cotangent,
):
    seqs, span, width = tokens.shape
    total_rows = seqs * span
    position = lax.axis_index("shard")
    length = span * lax.axis_size("shard")
    pieces = (
        qkv_weight,
        out_weight,
        up_weight,
        down_weight,
        attn_gain,
        attn_shift,
        query_bias,
        value_bias,
        out_bias,
        mlp_gain,
        mlp_shift,
        up_bias,
        down_bias,
    )
    gathered = (
        lax.all_gather(pieces[0], "shard", axis=0, tiled=True),
        lax.all_gather(pieces[1], "shard", axis=0, tiled=True),
        lax.all_gather(pieces[2], "shard", axis=0, tiled=True),
        lax.all_gather(pieces[3], "shard", axis=0, tiled=True),
        lax.all_gather(pieces[4], "shard", axis=0, tiled=True),
        lax.all_gather(pieces[5], "shard", axis=0, tiled=True),
        lax.all_gather(pieces[6], "shard", axis=0, tiled=True),
        lax.all_gather(pieces[7], "shard", axis=0, tiled=True),
        lax.all_gather(pieces[8], "shard", axis=0, tiled=True),
        lax.all_gather(pieces[9], "shard", axis=0, tiled=True),
        lax.all_gather(pieces[10], "shard", axis=0, tiled=True),
        lax.all_gather(pieces[11], "shard", axis=0, tiled=True),
        lax.all_gather(pieces[12], "shard", axis=0, tiled=True),
    )
    full_qkv, full_out, full_up, full_down = (gathered[0], gathered[1], gathered[2], gathered[3])
    vectors = [item.astype(jnp.float32) for item in gathered[4:]]
    gain_first, shift_first, bias_query, bias_value, bias_out = (
        vectors[0],
        vectors[1],
        vectors[2],
        vectors[3],
        vectors[4],
    )
    gain_second, shift_second, bias_up, bias_down = (vectors[5], vectors[6], vectors[7], vectors[8])
    flat = tokens.reshape(total_rows, width).astype(jnp.float32)
    normed = norm_rows(flat, gain_first, shift_first).astype(jnp.bfloat16)
    mixed = jnp.dot(normed, full_qkv, preferred_element_type=jnp.float32)
    queries = (mixed[:, :width] + bias_query).astype(jnp.bfloat16)
    keys = mixed[:, width : 2 * width].astype(jnp.bfloat16)
    values = (mixed[:, 2 * width :] + bias_value).astype(jnp.bfloat16)
    keys_all, values_all = (
        lax.all_gather(keys.reshape(seqs, span, width), "shard", axis=1, tiled=True),
        lax.all_gather(values.reshape(seqs, span, width), "shard", axis=1, tiled=True),
    )
    query_heads = queries.reshape(seqs, span, HEADS, HD)
    key_heads = keys_all.reshape(seqs, length, HEADS, HD)
    value_heads = values_all.reshape(seqs, length, HEADS, HD)
    query_pos = position * span + jnp.arange(span, dtype=jnp.int32)
    key_pos = jnp.arange(length, dtype=jnp.int32)
    allowed = (key_pos[None, :] <= query_pos[:, None])[None]

    def masked_scores(seq_query, seq_key):
        scores = (
            jnp.einsum("qhd,khd->hqk", seq_query, seq_key, preferred_element_type=jnp.float32)
            * SCALING
        )
        return jnp.where(allowed, scores, -1e30)

    def attend(items):
        seq_query, seq_key, seq_value = items
        scores = masked_scores(seq_query, seq_key)
        peak = jnp.max(scores, axis=-1, keepdims=True)
        expons = jnp.exp(scores - peak)
        totals = jnp.sum(expons, axis=-1, keepdims=True)
        probs = (expons / totals).astype(jnp.bfloat16)
        context = jnp.einsum("hqk,khd->qhd", probs, seq_value, preferred_element_type=jnp.float32)
        return (context.astype(jnp.bfloat16), peak + jnp.log(totals))

    contexts, log_totals = lax.map(attend, (query_heads, key_heads, value_heads))
    context = contexts.reshape(total_rows, width)
    branch = jnp.dot(context, full_out, preferred_element_type=jnp.float32) + bias_out
    middle = flat + branch
    normed_two = norm_rows(middle, gain_second, shift_second).astype(jnp.bfloat16)
    hidden = jnp.dot(normed_two, full_up, preferred_element_type=jnp.float32) + bias_up
    active = gelu_curve(hidden).astype(jnp.bfloat16)
    result = middle + jnp.dot(active, full_down, preferred_element_type=jnp.float32) + bias_down
    block_out = result.astype(jnp.bfloat16).reshape(seqs, span, width)
    regathered = (
        lax.all_gather(pieces[0], "shard", axis=0, tiled=True),
        lax.all_gather(pieces[1], "shard", axis=0, tiled=True),
        lax.all_gather(pieces[2], "shard", axis=0, tiled=True),
        lax.all_gather(pieces[3], "shard", axis=0, tiled=True),
        lax.all_gather(pieces[4], "shard", axis=0, tiled=True),
        lax.all_gather(pieces[5], "shard", axis=0, tiled=True),
        lax.all_gather(pieces[6], "shard", axis=0, tiled=True),
        lax.all_gather(pieces[7], "shard", axis=0, tiled=True),
        lax.all_gather(pieces[8], "shard", axis=0, tiled=True),
        lax.all_gather(pieces[9], "shard", axis=0, tiled=True),
        lax.all_gather(pieces[10], "shard", axis=0, tiled=True),
        lax.all_gather(pieces[11], "shard", axis=0, tiled=True),
        lax.all_gather(pieces[12], "shard", axis=0, tiled=True),
    )
    back_qkv, back_out, back_up, back_down = (
        regathered[0],
        regathered[1],
        regathered[2],
        regathered[3],
    )
    grad_out = cotangent.reshape(total_rows, width)
    grad_float = grad_out.astype(jnp.float32)
    grad_active = times_transposed(grad_out, back_down)
    unused_hidden, gelu_pull = jax.vjp(gelu_curve, hidden)
    grad_hidden = gelu_pull(grad_active)[0].astype(jnp.bfloat16)
    grad_normed_two = times_transposed(grad_hidden, back_up)
    unused_second, second_pull = jax.vjp(norm_rows, middle, gain_second, shift_second)
    grad_mid_norm, grad_gain_second, grad_shift_second = second_pull(grad_normed_two)
    grad_middle = grad_mid_norm + grad_float
    grad_branch = grad_middle.astype(jnp.bfloat16)
    grad_context = times_transposed(grad_branch, back_out).astype(jnp.bfloat16)
    grad_context_heads = grad_context.reshape(seqs, span, HEADS, HD)

    def attend_back(items):
        seq_query, seq_key, seq_value, seq_log, seq_grad = items
        scores = masked_scores(seq_query, seq_key)
        probs = jnp.exp(scores - seq_log)
        grad_probs = jnp.einsum(
            "qhd,khd->hqk", seq_grad, seq_value, preferred_element_type=jnp.float32
        )
        row_inner = jnp.sum(grad_probs * probs, axis=-1, keepdims=True)
        grad_scores = (probs * (grad_probs - row_inner)).astype(jnp.bfloat16)
        grad_query = (
            jnp.einsum("hqk,khd->qhd", grad_scores, seq_key, preferred_element_type=jnp.float32)
            * SCALING
        )
        grad_key = (
            jnp.einsum("hqk,qhd->khd", grad_scores, seq_query, preferred_element_type=jnp.float32)
            * SCALING
        )
        grad_value = jnp.einsum(
            "hqk,qhd->khd", probs.astype(jnp.bfloat16), seq_grad, preferred_element_type=jnp.float32
        )
        return (grad_query, grad_key, grad_value)

    grad_queries, grad_keys_all, grad_values_all = lax.map(
        attend_back, (query_heads, key_heads, value_heads, log_totals, grad_context_heads)
    )
    grad_keys, grad_values = (
        lax.psum_scatter(
            grad_keys_all.reshape(seqs, length, width), "shard", scatter_dimension=1, tiled=True
        ),
        lax.psum_scatter(
            grad_values_all.reshape(seqs, length, width), "shard", scatter_dimension=1, tiled=True
        ),
    )
    grad_query_low = grad_queries.reshape(total_rows, width).astype(jnp.bfloat16)
    grad_key_low = grad_keys.reshape(total_rows, width).astype(jnp.bfloat16)
    grad_value_low = grad_values.reshape(total_rows, width).astype(jnp.bfloat16)
    grad_mixed = jnp.concatenate([grad_query_low, grad_key_low, grad_value_low], axis=1)
    grad_normed = times_transposed(grad_mixed, back_qkv)
    unused_first, first_pull = jax.vjp(norm_rows, flat, gain_first, shift_first)
    grad_flat, grad_gain_first, grad_shift_first = first_pull(grad_normed)
    grad_tokens = (grad_flat + grad_middle).astype(jnp.bfloat16).reshape(seqs, span, width)
    part_qkv = transposed_times(normed, grad_mixed)
    part_out = transposed_times(context, grad_branch)
    owned = (
        lax.psum_scatter(
            part_qkv.astype(jnp.bfloat16), "shard", scatter_dimension=0, tiled=True
        ).astype(jnp.float32),
        lax.psum_scatter(
            part_out.astype(jnp.bfloat16), "shard", scatter_dimension=0, tiled=True
        ).astype(jnp.float32),
        lax.psum_scatter(
            grad_gain_first.astype(jnp.bfloat16), "shard", scatter_dimension=0, tiled=True
        ).astype(jnp.float32),
        lax.psum_scatter(
            grad_shift_first.astype(jnp.bfloat16), "shard", scatter_dimension=0, tiled=True
        ).astype(jnp.float32),
        lax.psum_scatter(
            jnp.sum(grad_query_low.astype(jnp.float32), axis=0).astype(jnp.bfloat16),
            "shard",
            scatter_dimension=0,
            tiled=True,
        ).astype(jnp.float32),
        lax.psum_scatter(
            jnp.sum(grad_value_low.astype(jnp.float32), axis=0).astype(jnp.bfloat16),
            "shard",
            scatter_dimension=0,
            tiled=True,
        ).astype(jnp.float32),
        lax.psum_scatter(
            jnp.sum(grad_branch.astype(jnp.float32), axis=0).astype(jnp.bfloat16),
            "shard",
            scatter_dimension=0,
            tiled=True,
        ).astype(jnp.float32),
        lax.psum_scatter(
            grad_gain_second.astype(jnp.bfloat16), "shard", scatter_dimension=0, tiled=True
        ).astype(jnp.float32),
        lax.psum_scatter(
            grad_shift_second.astype(jnp.bfloat16), "shard", scatter_dimension=0, tiled=True
        ).astype(jnp.float32),
        lax.psum_scatter(
            jnp.sum(grad_hidden.astype(jnp.float32), axis=0).astype(jnp.bfloat16),
            "shard",
            scatter_dimension=0,
            tiled=True,
        ).astype(jnp.float32),
        lax.psum_scatter(
            jnp.sum(grad_float, axis=0).astype(jnp.bfloat16),
            "shard",
            scatter_dimension=0,
            tiled=True,
        ).astype(jnp.float32),
    )
    piece = normed_two
    owned_up = lax.psum_scatter(
        transposed_times(piece, grad_hidden).astype(jnp.bfloat16),
        "shard",
        scatter_dimension=0,
        tiled=True,
    )
    piece = active
    owned_down = lax.psum_scatter(
        transposed_times(piece, grad_out).astype(jnp.bfloat16),
        "shard",
        scatter_dimension=0,
        tiled=True,
    )
    summed = (
        lax.psum(owned[0].astype(jnp.bfloat16), "replica").astype(jnp.float32),
        lax.psum(owned[1].astype(jnp.bfloat16), "replica").astype(jnp.float32),
        lax.psum(owned_up, "replica").astype(jnp.float32),
        lax.psum(owned_down, "replica").astype(jnp.float32),
        lax.psum(owned[2].astype(jnp.bfloat16), "replica").astype(jnp.float32),
        lax.psum(owned[3].astype(jnp.bfloat16), "replica").astype(jnp.float32),
        lax.psum(owned[4].astype(jnp.bfloat16), "replica").astype(jnp.float32),
        lax.psum(owned[5].astype(jnp.bfloat16), "replica").astype(jnp.float32),
        lax.psum(owned[6].astype(jnp.bfloat16), "replica").astype(jnp.float32),
        lax.psum(owned[7].astype(jnp.bfloat16), "replica").astype(jnp.float32),
        lax.psum(owned[8].astype(jnp.bfloat16), "replica").astype(jnp.float32),
        lax.psum(owned[9].astype(jnp.bfloat16), "replica").astype(jnp.float32),
        lax.psum(owned[10].astype(jnp.bfloat16), "replica").astype(jnp.float32),
    )
    return (
        block_out,
        grad_tokens,
        summed[0],
        summed[1],
        summed[2],
        summed[3],
        summed[4],
        summed[5],
        summed[6],
        summed[7],
        summed[8],
        summed[9],
        summed[10],
        summed[11],
        summed[12],
    )


def solution(mesh):
    placed = (
        P("replica", "shard", None),
        P("shard", None),
        P("shard", None),
        P("shard", None),
        P("shard", None),
        P("shard"),
        P("shard"),
        P("shard"),
        P("shard"),
        P("shard"),
        P("shard"),
        P("shard"),
        P("shard"),
        P("shard"),
        P("replica", "shard", None),
    )
    return jax.shard_map(
        on_device,
        mesh=mesh,
        in_specs=placed,
        out_specs=(
            P("replica", "shard", None),
            P("replica", "shard", None),
            P("shard", None),
            P("shard", None),
            P("shard", None),
            P("shard", None),
            P("shard"),
            P("shard"),
            P("shard"),
            P("shard"),
            P("shard"),
            P("shard"),
            P("shard"),
            P("shard"),
            P("shard"),
        ),
        check_vma=False,
    )
```

profile of v0, /device:TPU:27, one launch (start us, length us, event | category | flops | bytes accessed | tf_op | source)
XLA Modules:
  0.0 1331.7 jit_solution(11276808425965224734)
XLA Ops:
  11.0 5.4 all-reduce.20
  17.2 83.6 %all-gather.10.cloned.1.call-done = bf16[1088,3264]{1,0:T(8,128)(2,1)} async-done(((bf16[544,3264]{1,0:T(8,128)(2,1)}), bf16[1088,3264]{1,0:T(8,128)(2,1)}) %all-gather.10.cloned.1.call-update) | async-done | bytes 7102480 | tf_op jit(solution)/shard_map/all_gather | solution.py:75
  100.8 7.2 fusion.52
  108.1 2.8 copy-done.9
  112.2 3.6 fusion.31
  118.1 3.4 all-gather.2
  121.6 25.3 %all-gather.20.cloned.1.call-done = bf16[1024,1088]{0,1:T(8,128)(2,1)} async-done(((bf16[512,1088]{0,1:T(8,128)(2,1)}), bf16[1024,1088]{0,1:T(8,128)(2,1)}) %all-gather.20.cloned.1.call-update) | async-done | bytes 2228240 | tf_op jit(solution)/shard_map/all_gather | solution.py:106
  146.9 17.1 %fusion.6 = (f32[17,512]{1,0:T(8,128)S(1)}, f32[17,512,1024]{2,1,0:T(8,128)}) fusion(pred[512,1024]{1,0:T(8,128)(4,1)S(1)} %iota_compare_fusion, bf16[512,17,64]{0,2,1:T(8,128)(2,1)S(1)} %bitcast.102, bf16[1024,17,64]{0,2,1:T(8,128)(2,1)} %bitcast.100), kind=kOutput, calls=%fused_computation.15 | convolution fusion | flops 1167580672 | bytes 39553024 | tf_op jit(solution)/shard_map/while/body/eval_jaxpr/qhd,khd->hqk/dot_general | solution.py:118
  164.0 15.7 %fusion = f32[17,512]{1,0:T(8,128)S(1)} fusion(f32[17,512]{1,0:T(8,128)S(1)} %get-tuple-element.111, f32[17,512,1024]{2,1,0:T(8,128)} %get-tuple-element.112, pred[512,1024]{1,0:T(8,128)(4,1)S(1)} %iota_compare_fusion), kind=kLoop, calls=%fused_computation.6 | loop fusion | flops 35642880 | bytes 36245504 | tf_op jit(solution)/shard_map/while/body/eval_jaxpr/reduce_sum | solution.py:128
  179.7 3.9 all-gather.18.cloned.1.call-done
  183.6 17.8 %fusion.33 = bf16[17,64,512]{2,1,0:T(8,128)(2,1)} fusion(bf16[1024,17,64]{0,2,1:T(8,128)(2,1)} %bitcast.105, f32[17,512]{1,0:T(8,128)S(1)} %fusion, f32[17,512]{1,0:T(8,128)S(1)} %get-tuple-element.111, f32[17,512,1024]{2,1,0:T(8,128)} %get-tuple-element.112, pred[512,1024]{1,0:T(8,128)(4,1)S(1)} %iota_compare_fusion), kind=kOutput, calls=%fused_computation.66 | convolution fusion | flops 1185972224 | bytes 39587840 | tf_op jit(solution)/shard_map/while/body/eval_jaxpr/hqk,khd->qhd/dot_general | solution.py:130
  201.4 21.3 %all-gather.12.cloned.1.call-done = bf16[1088,1088]{1,0:T(8,128)(2,1)} async-done(((bf16[544,1088]{1,0:T(8,128)(2,1)}), bf16[1088,1088]{1,0:T(8,128)(2,1)}) %all-gather.12.cloned.1.call-update) | async-done | bytes 2367504 | tf_op jit(solution)/shard_map/all_gather | solution.py:76
  222.8 4.1 fusion.62
  227.2 115.4 %all-gather.14.cloned.1.call-done = bf16[1088,4352]{1,0:T(8,128)(2,1)} async-done(((bf16[544,4352]{1,0:T(8,128)(2,1)}), bf16[1088,4352]{1,0:T(8,128)(2,1)}) %all-gather.14.cloned.1.call-update) | async-done | bytes 9469968 | tf_op jit(solution)/shard_map/all_gather | solution.py:77
  342.6 12.7 fusion.54
  355.3 107.2 %all-gather.16.cloned.1.call-done = bf16[4352,1088]{0,1:T(8,128)(2,1)} async-done(((bf16[2176,1088]{0,1:T(8,128)(2,1)}), bf16[4352,1088]{0,1:T(8,128)(2,1)}) %all-gather.16.cloned.1.call-update) | async-done | bytes 9469968 | tf_op jit(solution)/shard_map/all_gather | solution.py:78
  462.4 18.9 %fusion.64 = (bf16[4352]{0:T(1024)(128)(2,1)}, bf16[512,4352]{1,0:T(8,128)(2,1)S(1)}) fusion(f32[512,4352]{1,0:T(8,128)} %fusion.54, f32[4352]{0:T(1024)S(1)} %reshape.218, bf16[4352,1088]{0,1:T(8,128)(2,1)} %all-gather.16.cloned.1.call-done, bf16[1,512,1088]{1,2,0:T(8,128)(2,1)} %param.29), kind=kOutput, calls=%fused_computation.104 | convolution fusion | flops 4906545152 | bytes 23979520 | tf_op jit(solution)/shard_map/dot_general | solution.py:27
  481.4 6.3 multiply_reduce_fusion.1
  490.8 1.6 convolution_convert_fusion.4
  492.4 26.9 %multiply_reduce_fusion = (f32[17,512]{1,0:T(8,128)S(1)}, f32[17,512,1024]{2,1,0:T(8,128)}) fusion(f32[17,512]{1,0:T(8,128)S(1)} %log_add_fusion, f32[17,512,1024]{2,1,0:T(8,128)} %get-tuple-element.112, pred[512,1024]{1,0:T(8,128)(4,1)S(1)} %iota_compare_fusion, bf16[512,17,64]{0,2,1:T(8,128)(2,1)S(1)} %bitcast.107, bf16[1024,17,64]{0,2,1:T(8,128)(2,1)S(1)} %bitcast.106), kind=kOutput, calls=%fused_computation.1 | convolution fusion | flops 1185406464 | bytes 75239424 | tf_op jit(solution)/shard_map/while/body/eval_jaxpr/qhd,khd->hqk/dot_general | solution.py:180
  519.3 29.5 %multiply_convert_fusion = bf16[17,512,1024]{2,1,0:T(8,128)(2,1)} fusion(f32[17,512,1024]{2,1,0:T(8,128)} %get-tuple-element.117, f32[17,512]{1,0:T(8,128)S(1)} %get-tuple-element.116, f32[17,512]{1,0:T(8,128)S(1)} %log_add_fusion, f32[17,512,1024]{2,1,0:T(8,128)} %get-tuple-element.112, pred[512,1024]{1,0:T(8,128)(4,1)S(1)} %iota_compare_fusion), kind=kLoop, calls=%fused_computation | loop fusion | flops 53477376 | bytes 89722880 | tf_op jit(solution)/shard_map/while/body/eval_jaxpr/convert_element_type | solution.py:184
  548.9 11.7 broadcast_multiply_fusion
  560.6 19.0 %fusion.2 = f32[17,64,1024]{2,1,0:T(8,128)} fusion(bf16[512,17,64]{0,2,1:T(8,128)(2,1)} %bitcast.108, f32[17,512]{1,0:T(8,128)S(1)} %log_add_fusion, f32[17,512,1024]{2,1,0:T(8,128)} %get-tuple-element.112, pred[512,1024]{1,0:T(8,128)(4,1)S(1)} %iota_compare_fusion), kind=kOutput, calls=%fused_computation.10 | convolution fusion | flops 1176502272 | bytes 41781248 | tf_op jit(solution)/shard_map/while/body/eval_jaxpr/hqk,qhd->khd/dot_general | solution.py:193
  580.9 12.8 convolution_convert_fusion
  593.7 14.0 %copy.30 = bf16[4352,1088]{1,0:T(8,128)(2,1)} copy(bf16[4352,1088]{0,1:T(8,128)(2,1)} %convolution_convert_fusion) | data formatting | bytes 18939904
  609.0 4.3 convolution_convert_fusion.3
  613.4 10.3 convolution_convert_fusion.1
  623.8 14.0 %fusion.63 = (bf16[17,64]{1,0:T(8,128)(2,1)S(1)}, bf16[17,64,512]{2,1,0:T(8,128)(2,1)}) fusion(bf16[1024,17,64]{0,2,1:T(8,128)(2,1)} %bitcast.101, bf16[17,512,1024]{2,1,0:T(8,128)(2,1)} %multiply_convert_fusion), kind=kOutput, calls=%fused_computation.103 | convolution fusion | flops 1142520832 | bytes 21170304 | tf_op jit(solution)/shard_map/while/body/eval_jaxpr/hqk,khd->qhd/dot_general | solution.py:186
  637.8 2.8 convert_bitcast_fusion.1
  640.6 37.4 %reduce-scatter.11.cloned.1.call-done = f32[1,512,1088]{1,2,0:T(8,128)} async-done(((f32[1,1024,1088]{1,2,0:T(8,128)}), f32[1,512,1088]{1,2,0:T(8,128)}) %reduce-scatter.11.cloned.1.call-update) | async-done | bytes 2228240 | tf_op jit(solution)/shard_map/reduce_scatter | solution.py:205
  678.0 1.9 convert_bitcast_fusion.2
  681.0 9.0 convolution_convert_fusion.2
  690.0 107.2 %reduce-scatter.19.cloned.1.call-done = bf16[2176,1088]{1,0:T(8,128)(2,1)} async-done(((bf16[4352,1088]{1,0:T(8,128)(2,1)}), bf16[2176,1088]{1,0:T(8,128)(2,1)}) %reduce-scatter.19.cloned.1.call-update) | async-done | bytes 4734992
  797.2 8.6 copy.31
  805.8 30.5 %reduce-scatter.15.cloned.1.call-done = bf16[544,1088]{1,0:T(8,128)(2,1)} async-done(((bf16[1088,1088]{1,0:T(8,128)(2,1)}), bf16[544,1088]{1,0:T(8,128)(2,1)}) %reduce-scatter.15.cloned.1.call-update) | async-done | bytes 1183760 | tf_op jit(solution)/shard_map/reduce_scatter | solution.py:223
  836.3 113.9 %reduce-scatter.17.cloned.1.call-done = bf16[544,4352]{1,0:T(8,128)(2,1)} async-done(((bf16[1088,4352]{1,0:T(8,128)(2,1)}), bf16[544,4352]{1,0:T(8,128)(2,1)}) %reduce-scatter.17.cloned.1.call-update) | async-done | bytes 4734992 | tf_op jit(solution)/shard_map/reduce_scatter | solution.py:270
  950.2 90.2 %reduce-scatter.13.cloned.1.call-done = bf16[544,3264]{1,0:T(8,128)(2,1)} async-done(((bf16[1088,3264]{1,0:T(8,128)(2,1)}), bf16[544,3264]{1,0:T(8,128)(2,1)}) %reduce-scatter.13.cloned.1.call-update) | async-done | bytes 3551248 | tf_op jit(solution)/shard_map/reduce_scatter | solution.py:220
  1043.7 2.0 convert_reduce_fusion.1
  1045.9 7.5 fusion.57
  1055.9 7.4 all-reduce.19
  1064.0 56.9 %all-reduce.17 = (bf16[544]{0:T(1024)(128)(2,1)S(1)}, bf16[544]{0:T(1024)(128)(2,1)S(1)}, bf16[544]{0:T(1024)(128)(2,1)S(1)}, bf16[544]{0:T(1024)(128)(2,1)S(1)}...) all-reduce(bf16[544]{0:T(1024)(128)(2,1)S(1)} %dynamic-slice.10, ...), channel_id=1, replica_groups=mesh['replica'=16,'shard'=2] {'replica'}, use_global_device_ids=true, to_apply=%region_23.24 | all-reduce | flops 6528 | bytes 26112 | tf_op jit(solution)/shard_map/psum | solution.py:288
  1126.4 4.6 fusion.36
  1131.0 12.8 fusion.23
  1143.8 164.4 %all-reduce.23.cloned.1.call-done = (bf16[544,3264]{1,0:T(8,128)(2,1)}, bf16[544,1088]{1,0:T(8,128)(2,1)}, bf16[544,4352]{1,0:T(8,128)(2,1)}, bf16[2176,1088]{0,1:T(8,128)(2,1)}) async-done(((bf16[544,3264]{1,0:T(8,128)(2,1)}, bf16[544,1088]{1,0:T(8,128)(2,1)}, bf16[544,4352]{1,0:T(8,128)(2,1)}, bf16[2176,1088]{0,1:T(8,128)(2,1)}), (bf16[544,3264]{1,0:T(8,128)(2,1)}, bf16[544,1088]{1,0:T(8,128)(2,1)}, ...) | async-done | bytes 14204944 | tf_op jit(solution)/shard_map/psum | solution.py:284
  1308.2 6.9 convert_element_type.242
  1315.2 4.4 convert_element_type.244
  1319.5 3.6 convert_element_type.238
  1323.1 1.6 convert_element_type.240
  (190 shorter events, 24.8 us)
Async XLA Ops:
  7.2 2.4 copy-start.40
  7.2 2.6 copy-start.41
  7.2 2.9 copy-start.42
  7.2 3.1 copy-start.43
  7.2 3.3 copy-start.44
  7.3 3.6 copy-start.45
  7.3 9.3 copy-start.2
  7.3 93.5 %all-gather.10.cloned.1.call-start = ((), (), s32[]{:S(2)}) async-start(), calls=%async_computation.6 | async-start | bytes 10862592 | tf_op jit(solution)/shard_map/all_gather | solution.py:75
  8.0 138.8 %all-gather.20.cloned.1.call-start = ((), (), s32[]{:S(2)}) async-start(), calls=%async_computation.16 | async-start | bytes 3342336 | tf_op jit(solution)/shard_map/all_gather | solution.py:106
  16.5 91.6 %copy-start.21 = (f32[1088]{0:T(1024)}, f32[1088]{0:T(1024)S(1)}, u32[]{:S(2)}) copy-start(f32[1088]{0:T(1024)S(1)} %convert_element_type.205) | copy-start | bytes 13060
  16.5 91.5 %copy-start.33 = (f32[1088]{0:T(1024)}, f32[1088]{0:T(1024)S(1)}, u32[]{:S(2)}) copy-start(f32[1088]{0:T(1024)S(1)} %convert_element_type.206) | copy-start | bytes 13060
  16.8 91.3 %copy-start.23 = (f32[512]{0:T(512)}, f32[512]{0:T(512)S(1)}, u32[]{:S(2)}) copy-start(f32[512]{0:T(512)S(1)} %broadcast_multiply_fusion.2) | copy-start | bytes 6148
  17.1 91.0 %copy-start.29 = (f32[512]{0:T(512)}, f32[512]{0:T(512)S(1)}, u32[]{:S(2)}) copy-start(f32[512]{0:T(512)S(1)} %fusion.29) | copy-start | bytes 6148
  17.2 91.0 %copy-start.25 = (f32[512]{0:T(512)}, f32[512]{0:T(512)S(1)}, u32[]{:S(2)}) copy-start(f32[512]{0:T(512)S(1)} %fusion.43) | copy-start | bytes 6148
  108.1 2.8 copy-start.9
  112.1 71.5 %all-gather.18.cloned.1.call-start = ((), (), s32[]{:S(2)}) async-start(), calls=%async_computation.15 | async-start | bytes 3342336 | tf_op jit(solution)/shard_map/all_gather | solution.py:107
  115.8 31.0 %copy-start.1 = (bf16[512,1088]{0,1:T(8,128)(2,1)}, bf16[512,1088]{0,1:T(8,128)(2,1)S(1)}, u32[]{:S(2)}) copy-start(bf16[512,1088]{0,1:T(8,128)(2,1)S(1)} %get-tuple-element.107) | copy-start | bytes 3342340
  115.8 106.9 %all-gather.12.cloned.1.call-start = ((), (), s32[]{:S(2)}) async-start(), calls=%async_computation.7 | async-start | bytes 3760128 | tf_op jit(solution)/shard_map/all_gather | solution.py:76
  116.4 226.2 %all-gather.14.cloned.1.call-start = ((), (), s32[]{:S(2)}) async-start(), calls=%async_computation.8 | async-start | bytes 14204928 | tf_op jit(solution)/shard_map/all_gather | solution.py:77
  117.0 345.4 %all-gather.16.cloned.1.call-start = ((), (), s32[]{:S(2)}) async-start(), calls=%async_computation.9 | async-start | bytes 14204928 | tf_op jit(solution)/shard_map/all_gather | solution.py:78
  117.6 520.2 %reduce-scatter.9.cloned.1.call-start = ((), (), s32[]{:S(2)}) async-start(), calls=%async_computation.10 | async-start | bytes 6684672 | tf_op jit(solution)/shard_map/reduce_scatter | solution.py:202
  462.4 18.9 %copy-start.4 = (bf16[1088,4352]{1,0:T(8,128)(2,1)S(1)}, bf16[1088,4352]{1,0:T(8,128)(2,1)}, u32[]{:S(2)}) copy-start(bf16[1088,4352]{1,0:T(8,128)(2,1)} %all-gather.14.cloned.1.call-done) | copy-start | bytes 28409860
  481.3 6.3 copy-start.48
  490.0 2.4 copy-start.19
  492.4 26.9 %copy-start.12 = (bf16[512,1088]{0,1:T(8,128)(2,1)}, bf16[512,1088]{0,1:T(8,128)(2,1)S(1)}, u32[]{:S(2)}) copy-start(bf16[512,1088]{0,1:T(8,128)(2,1)S(1)} %convolution_convert_fusion.4) | copy-start | bytes 3342340
  560.6 117.4 %reduce-scatter.11.cloned.1.call-start = ((), (), s32[]{:S(2)}) async-start(), calls=%async_computation.11 | async-start | bytes 6684672 | tf_op jit(solution)/shard_map/reduce_scatter | solution.py:205
  579.6 217.6 %reduce-scatter.19.cloned.1.call-start = ((), (), s32[]{:S(2)}) async-start(), calls=%async_computation.17 | async-start | bytes 15040512
  607.7 228.6 %reduce-scatter.15.cloned.1.call-start = ((), (), s32[]{:S(2)}) async-start(), calls=%async_computation.13 | async-start | bytes 3760128 | tf_op jit(solution)/shard_map/reduce_scatter | solution.py:223
  613.3 336.9 %reduce-scatter.17.cloned.1.call-start = ((), (), s32[]{:S(2)}) async-start(), calls=%async_computation.14 | async-start | bytes 14204928 | tf_op jit(solution)/shard_map/reduce_scatter | solution.py:270
  623.7 416.8 %reduce-scatter.13.cloned.1.call-start = ((), (), s32[]{:S(2)}) async-start(), calls=%async_computation.12 | async-start | bytes 10862592 | tf_op jit(solution)/shard_map/reduce_scatter | solution.py:220
  637.8 43.2 %copy-start.22 = (f32[1088]{0:T(1024)S(1)}, f32[1088]{0:T(1024)}, u32[]{:S(2)}) copy-start(f32[1088]{0:T(1024)} %copy-done.21) | copy-start | bytes 13060
  637.8 43.2 %copy-start.26 = (f32[512]{0:T(512)S(1)}, f32[512]{0:T(512)}, u32[]{:S(2)}) copy-start(f32[512]{0:T(512)} %copy-done.25) | copy-start | bytes 6148
  637.8 43.2 %copy-start.34 = (f32[1088]{0:T(1024)S(1)}, f32[1088]{0:T(1024)}, u32[]{:S(2)}) copy-start(f32[1088]{0:T(1024)} %copy-done.33) | copy-start | bytes 13060
  640.6 40.4 %copy-start.3 = (bf16[1,512,1088]{1,2,0:T(8,128)(2,1)S(1)}, bf16[1,512,1088]{1,2,0:T(8,128)(2,1)}, u32[]{:S(2)}) copy-start(bf16[1,512,1088]{1,2,0:T(8,128)(2,1)} %param.15) | copy-start | bytes 3342340
  640.6 40.4 %copy-start.24 = (f32[512]{0:T(512)S(1)}, f32[512]{0:T(512)}, u32[]{:S(2)}) copy-start(f32[512]{0:T(512)} %copy-done.23) | copy-start | bytes 6148
  678.0 2.9 copy-start.14
  678.0 3.0 copy-start.16
  690.0 618.3 %all-reduce.23.cloned.1.call-start = ((), (), s32[]{:S(2)}) async-start(), calls=%async_computation.18 | async-start | bytes 28688384 | tf_op jit(solution)/shard_map/psum | solution.py:284
  1040.5 2.8 copy-start.46
  1045.9 7.6 copy-start.30
  1053.5 2.4 copy-start.31
  1053.5 2.4 copy-start.32
  1053.5 2.4 copy-start.36
  1053.5 2.4 copy-start.37
  1053.5 72.8 %copy-start.28 = (f32[512]{0:T(512)S(1)}, f32[512]{0:T(512)}, u32[]{:S(2)}) copy-start(f32[512]{0:T(512)} %copy-done.27) | copy-start | bytes 6148
  1308.2 6.9 copy-start.8
  1315.2 4.4 copy-start.11
  1319.5 3.6 copy-start.13
  (14 other events, 21.3 us)
Sparse Core Ops, SparseCore 0:
  9.6 91.1 all-gather.9
  112.2 34.5 all-gather.19
  149.0 34.5 all-gather.17
  185.0 37.7 all-gather.11
  224.2 118.3 all-gather.13
  344.0 118.3 all-gather.15
  560.7 57.1 reduce-scatter.8
  620.8 57.1 reduce-scatter.10
  680.3 116.8 reduce-scatter.18
  799.9 36.3 reduce-scatter.14
  839.3 110.8 reduce-scatter.16
  953.1 87.3 reduce-scatter.12
  1045.7 262.4 all-reduce.22
where the time goes:
time: 1340 us; the launch traced here: 1330 us
  waiting for transfers between devices  903 us (67%)
  matrix products  214 us (16%)
  other arithmetic  87.6 us (7%)
  blocking collectives  73.2 us (5%)
  local copies, waits for them, and re-layouts  36.3 us (3%)
  between operations  16.9 us (1%)
    psum x1, waiting for transfers between devices, on_device(): lax.psum(owned[0].astype(jnp.bfloat16), 'replica').astype(jnp.float32)  164 us
    all_gather x1, waiting for transfers between devices, on_device(): lax.all_gather(pieces[2], 'shard', axis=0, tiled=True)  115 us
    reduce_scatter x1, waiting for transfers between devices, on_device(): lax.psum_scatter(transposed_times(piece, grad_hidden).astype(jnp.bfloat16...  114 us
    unnamed x14, waiting for transfers between devices  110 us
    all_gather x1, waiting for transfers between devices, on_device(): lax.all_gather(pieces[3], 'shard', axis=0, tiled=True)  107 us
    reduce_scatter x1, waiting for transfers between devices, on_device(): lax.psum_scatter(part_qkv.astype(jnp.bfloat16), 'shard', scatter_dimensio...  90.2 us
    all_gather x1, waiting for transfers between devices, on_device(): lax.all_gather(pieces[0], 'shard', axis=0, tiled=True)  83.6 us
    psum x1, blocking collectives, on_device(): lax.psum(owned[2].astype(jnp.bfloat16), 'replica').astype(jnp.float32)  56.9 us
  transfers between devices with their start and end apart: 13, of which 12 were waited for; matrix products, arithmetic and copies ran while one was open for 16% of the time, Pallas kernels for 0%

commit v1 on v0

v1 whole, which is shorter than its diff:
```python
import functools
import jax
import jax.numpy as jnp
from jax import lax
from jax.experimental import pallas as pl
from jax.experimental.pallas import tpu as pltpu
from jax.sharding import PartitionSpec as P

HD = 64
SCALING = 0.125
NEG = -1e30
LANES = 128


def _nt(a, b):
    return lax.dot_general(a, b, (((1,), (1,)), ((), ())), preferred_element_type=jnp.float32)


def _nn(a, b):
    return lax.dot_general(a, b, (((1,), (0,)), ((), ())), preferred_element_type=jnp.float32)


def _lane_valid(shape, width):
    left = width - pl.program_id(1) * LANES
    return lax.broadcasted_iota(jnp.int32, shape, 1) < left


def _clean(ref, width):
    block = ref[...]
    return jnp.where(_lane_valid(block.shape, width), block, jnp.zeros_like(block))


def _head_part(block, head):
    lane = lax.broadcasted_iota(jnp.int32, block.shape, 1)
    keep = (lane < HD) if head == 0 else (lane >= HD)
    return jnp.where(keep, block, jnp.zeros_like(block))


def _diag_mask(keys, rows, first):
    key_at = lax.broadcasted_iota(jnp.int32, (keys, rows), 0)
    row_at = lax.broadcasted_iota(jnp.int32, (keys, rows), 1) + first
    return key_at <= row_at


def forward_kernel(pos_ref, q_ref, k_ref, v_ref, ctx_ref, lse_ref, kc_ref, vt_ref, *, span, width):
    pos = pos_ref[0]
    block = min(256, span)
    queries = _clean(q_ref, width)
    kc_ref[...] = _clean(k_ref, width)
    length = k_ref.shape[0]
    for j in range(length // span):
        vt_ref[j] = _clean(v_ref.at[pl.ds(j * span, span), :], width).T
    chains = []
    for head in range(2):
        part = _head_part(queries, head)
        for at in range(0, span, block):
            chains.append((part[at : at + block], at))

    def update(state, scores, vt):
        peak, total, acc = state
        top = jnp.maximum(peak, jnp.max(scores, axis=0, keepdims=True))
        fade = jnp.exp(peak - top)
        expons = jnp.exp(scores - top)
        total = total * fade + jnp.sum(expons, axis=0, keepdims=True)
        acc = acc * fade + _nn(vt, expons.astype(jnp.bfloat16))
        return top, total, acc

    states = []
    own_vt = vt_ref[pos]
    for part, at in chains:
        keys = at + block
        own_k = kc_ref[pl.ds(pl.multiple_of(pos * span, span), keys), :]
        scores = jnp.where(_diag_mask(keys, block, at), _nt(own_k, part), NEG)
        peak = jnp.max(scores, axis=0, keepdims=True)
        expons = jnp.exp(scores - peak)
        total = jnp.sum(expons, axis=0, keepdims=True)
        acc = _nn(own_vt[:, :keys], expons.astype(jnp.bfloat16))
        states.append((peak, total, acc))

    def past(j, states):
        key_block = kc_ref[pl.ds(pl.multiple_of(j * span, span), span), :]
        vt = vt_ref[j]
        return tuple(
            update(state, _nt(key_block, part), vt) for state, (part, _) in zip(states, chains)
        )

    states = lax.fori_loop(0, pos, past, tuple(states))
    per_head = len(chains) // 2
    for i in range(per_head):
        at = i * block
        (peak0, total0, acc0), (peak1, total1, acc1) = states[i], states[per_head + i]
        row = lax.broadcasted_iota(jnp.int32, acc0.shape, 0)
        both = jnp.where(row < HD, acc0 / total0, acc1 / total1)
        ctx_ref[at : at + block, :] = both.T.astype(ctx_ref.dtype)
        lse_ref[0, 0:1, at : at + block] = peak0 + jnp.log(total0)
        lse_ref[0, 1:2, at : at + block] = peak1 + jnp.log(total1)


def backward_kernel(pos_ref, q_ref, k_ref, v_ref, g_ref, ctx_ref, lse_ref, dq_ref, dk_ref, dv_ref,
                    kc_ref, vc_ref, kt_ref, dk_acc, dv_acc, *, span, width):
    pos = pos_ref[0]
    block = min(256, span)
    queries = _clean(q_ref, width)
    grads = _clean(g_ref, width)
    context = _clean(ctx_ref, width)
    kc_ref[...] = _clean(k_ref, width)
    vc_ref[...] = _clean(v_ref, width)
    length = k_ref.shape[0]
    for j in range(length // span):
        kt_ref[j] = kc_ref[pl.ds(j * span, span), :].T
    dk_acc[...] = jnp.zeros_like(dk_acc)
    dv_acc[...] = jnp.zeros_like(dv_acc)
    product = (grads.astype(jnp.float32) * context.astype(jnp.float32)).T
    chains = []
    for head in range(2):
        q_part = _head_part(queries, head)
        g_part = _head_part(grads, head)
        inner = jnp.sum(product[head * HD : (head + 1) * HD], axis=0, keepdims=True)
        for at in range(0, span, block):
            chains.append((
                q_part[at : at + block], g_part[at : at + block], inner[:, at : at + block],
                lse_ref[0, head : head + 1, at : at + block], at,
            ))

    def piece(chain, key_block, value_block, kt, masked):
        q_part, g_part, inner, lse, at = chain
        scores = _nt(key_block, q_part)
        if masked:
            scores = jnp.where(_diag_mask(key_block.shape[0], q_part.shape[0], at), scores, NEG)
        probs = jnp.exp(scores - lse)
        grad_probs = _nt(value_block, g_part)
        grad_scores = (probs * (grad_probs - inner)).astype(jnp.bfloat16)
        dq = _nn(kt, grad_scores)
        dk = _nn(grad_scores, q_part)
        dv = _nn(probs.astype(jnp.bfloat16), g_part)
        return dq, dk, dv

    start = pl.multiple_of(pos * span, span)
    own_kt = kt_ref[pos]
    dqs = []
    for chain in chains:
        keys = chain[4] + block
        where = pl.ds(start, keys)
        dq, dk, dv = piece(chain, kc_ref[where, :], vc_ref[where, :], own_kt[:, :keys], True)
        dk_acc[where, :] += dk
        dv_acc[where, :] += dv
        dqs.append(dq)

    def past(j, dqs):
        where = pl.ds(pl.multiple_of(j * span, span), span)
        key_block, value_block, kt = kc_ref[where, :], vc_ref[where, :], kt_ref[j]
        out, dk_sum, dv_sum = [], None, None
        for chain, dq_old in zip(chains, dqs):
            dq, dk, dv = piece(chain, key_block, value_block, kt, False)
            dk_sum = dk if dk_sum is None else dk_sum + dk
            dv_sum = dv if dv_sum is None else dv_sum + dv
            out.append(dq_old + dq)
        dk_acc[where, :] = dk_sum
        dv_acc[where, :] = dv_sum
        return tuple(out)

    dqs = lax.fori_loop(0, pos, past, tuple(dqs))
    per_head = len(chains) // 2
    for i in range(per_head):
        at = i * block
        row = lax.broadcasted_iota(jnp.int32, dqs[0].shape, 0)
        both = jnp.where(row < HD, dqs[i], dqs[per_head + i]) * SCALING
        dq_ref[at : at + block, :] = both.T.astype(dq_ref.dtype)
    dk_ref[...] = dk_acc[...].astype(dk_ref.dtype)
    dv_ref[...] = dv_acc[...].astype(dv_ref.dtype)


def attention_forward(position, queries, keys, values, seqs, span):
    rows, width = queries.shape
    length = keys.shape[0] // seqs
    pairs = pl.cdiv(width, LANES)
    own = pl.BlockSpec((span, LANES), lambda s, h, p: (s, h))
    whole = pl.BlockSpec((length, LANES), lambda s, h, p: (s, h))
    lse = pl.BlockSpec((1, 2, span), lambda s, h, p: (s * pairs + h, 0, 0))
    return pl.pallas_call(
        functools.partial(forward_kernel, span=span, width=width),
        grid_spec=pltpu.PrefetchScalarGridSpec(
            num_scalar_prefetch=1,
            grid=(seqs, pairs),
            in_specs=[own, whole, whole],
            out_specs=[own, lse],
            scratch_shapes=[
                pltpu.VMEM((length, LANES), jnp.bfloat16),
                pltpu.VMEM((length // span, LANES, span), jnp.bfloat16),
            ],
        ),
        out_shape=[
            jax.ShapeDtypeStruct((rows, width), jnp.bfloat16),
            jax.ShapeDtypeStruct((seqs * pairs, 2, span), jnp.float32),
        ],
        compiler_params=pltpu.CompilerParams(vmem_limit_bytes=48 * 1024 * 1024),
        cost_estimate=pl.CostEstimate(flops=4 * rows * length * width * 2, bytes_accessed=8 * rows * width * 2, transcendentals=rows * length * 17),
        name="attention_forward",
    )(position, queries, keys, values)


def attention_backward(position, queries, keys, values, grads, context, lse_rows, seqs, span):
    rows, width = queries.shape
    length = keys.shape[0] // seqs
    pairs = pl.cdiv(width, LANES)
    own = pl.BlockSpec((span, LANES), lambda s, h, p: (s, h))
    whole = pl.BlockSpec((length, LANES), lambda s, h, p: (s, h))
    lse = pl.BlockSpec((1, 2, span), lambda s, h, p: (s * pairs + h, 0, 0))
    return pl.pallas_call(
        functools.partial(backward_kernel, span=span, width=width),
        grid_spec=pltpu.PrefetchScalarGridSpec(
            num_scalar_prefetch=1,
            grid=(seqs, pairs),
            in_specs=[own, whole, whole, own, own, lse],
            out_specs=[own, whole, whole],
            scratch_shapes=[
                pltpu.VMEM((length, LANES), jnp.bfloat16),
                pltpu.VMEM((length, LANES), jnp.bfloat16),
                pltpu.VMEM((length // span, LANES, span), jnp.bfloat16),
                pltpu.VMEM((length, LANES), jnp.float32),
                pltpu.VMEM((length, LANES), jnp.float32),
            ],
        ),
        out_shape=[
            jax.ShapeDtypeStruct((rows, width), jnp.bfloat16),
            jax.ShapeDtypeStruct(keys.shape, jnp.bfloat16),
            jax.ShapeDtypeStruct(keys.shape, jnp.bfloat16),
        ],
        compiler_params=pltpu.CompilerParams(vmem_limit_bytes=48 * 1024 * 1024),
        cost_estimate=pl.CostEstimate(flops=10 * rows * length * width * 2, bytes_accessed=12 * rows * width * 2, transcendentals=rows * length * 17),
        name="attention_backward",
    )(position, queries, keys, values, grads, context, lse_rows)


EPSILON = 1e-05
CORE_BIT = 1


def centred(values):
    average = jnp.mean(values, axis=-1, keepdims=True)
    off = values - average
    rstd = lax.rsqrt(jnp.mean(off * off, axis=-1, keepdims=True) + EPSILON)
    return off * rstd, rstd


def norm_pull(grad, unit, rstd, gain):
    scaled = grad * gain
    first = jnp.mean(scaled, axis=-1, keepdims=True)
    second = jnp.mean(scaled * unit, axis=-1, keepdims=True)
    return rstd * (scaled - first - unit * second)


def gelu_parts(values):
    square = values * values
    tanh = jnp.tanh(0.7978845608 * values * (1.0 + 0.044715 * square))
    half = 0.5 * (1.0 + tanh)
    slope = half + 0.5 * values * (1.0 - tanh * tanh) * (
        0.7978845608 * (1.0 + 3.0 * 0.044715 * square)
    )
    return values * half, slope


def dot(left, right):
    return jnp.dot(left, right, preferred_element_type=jnp.float32)


def dot_nt(left, right):
    return lax.dot_general(
        left, right, (((1,), (1,)), ((), ())), preferred_element_type=jnp.float32
    )


def dot_tn(left, right):
    return lax.dot_general(
        left, right, (((0,), (0,)), ((), ())), preferred_element_type=jnp.float32
    )


def low(values):
    return values.astype(jnp.bfloat16)


def swap(values, bit):
    size = lax.axis_size("replica")
    return lax.ppermute(values, "replica", [(i, i ^ bit) for i in range(size)])


def cross(values):
    return lax.ppermute(values, "shard", [(0, 1), (1, 0)])


def after(values, earlier):
    return lax.optimization_barrier((values, earlier))[0]


def has_bit(bit):
    return (lax.axis_index("replica") & bit) != 0


def choose(flag, left, right):
    return jnp.where(flag, left, right)


def in_order(bit, mine, other):
    flag = has_bit(bit)
    return jnp.concatenate([choose(flag, other, mine), choose(flag, mine, other)], axis=0)


def spread_start(weight, bits):
    rows = weight.shape[0]
    count = 2 ** len(bits)
    size = -(-rows // (8 * count)) * 8
    index = jnp.int32(0)
    for bit in bits:
        index = index * 2 + has_bit(bit).astype(jnp.int32)
    start = jnp.minimum(index * size, rows - size)
    return cross(lax.dynamic_slice_in_dim(weight, start, size, axis=0))


def spread_end(weight, got, bits):
    rows = weight.shape[0]
    count = 2 ** len(bits)
    size = got.shape[0]
    for bit in bits[::-1]:
        got = in_order(bit, got, swap(got, bit))
    extra = count * size - rows
    if extra:
        got = jnp.concatenate([got[: (count - 1) * size], got[(count - 1) * size + extra :]], axis=0)
    first = lax.axis_index("shard") == 0
    return jnp.concatenate([choose(first, weight, got), choose(first, got, weight)], axis=0)


def reduce_start(give, keep):
    return low(keep.astype(jnp.float32) + cross(low(give)).astype(jnp.float32))


def halves(values):
    rows = values.shape[0]
    size = -(-rows // 16) * 8
    return values[:size], values[rows - size :]


def reduce_rest(values, bits):
    stack = []
    for bit in bits[:-1]:
        lower, upper = halves(values)
        flag = has_bit(bit)
        sent = swap(choose(flag, lower, upper), bit)
        stack.append((bit, values.shape[0]))
        values = low(choose(flag, upper, lower).astype(jnp.float32) + sent.astype(jnp.float32))
    values = low(values.astype(jnp.float32) + swap(values, bits[-1]).astype(jnp.float32))
    for bit, rows in stack[::-1]:
        both = in_order(bit, values, swap(values, bit))
        size = values.shape[0]
        if 2 * size != rows:
            both = jnp.concatenate([both[: rows - size], both[size:]], axis=0)
        values = both
    return values


def columns_of(values, axis, index):
    size = values.shape[axis] // 2
    low_part = lax.slice_in_dim(values, 0, size, axis=axis)
    high_part = lax.slice_in_dim(values, size, 2 * size, axis=axis)
    return choose(index == 0, low_part, high_part)


def on_device(
    tokens, qkv_weight, out_weight, up_weight, down_weight, attn_gain, attn_shift, query_bias,
    value_bias, out_bias, mlp_gain, mlp_shift, up_bias, down_bias, cotangent,
):
    seqs, span, width = tokens.shape
    rows = seqs * span
    shards = lax.axis_size("shard")
    replicas = lax.axis_size("replica")
    position = lax.axis_index("shard")
    core = lax.axis_index("replica") & CORE_BIT
    length = span * shards
    hidden_units = up_weight.shape[1]
    pairwise = shards == 2
    bits = []
    bit = 2
    while bit < replicas:
        bits.append(bit)
        bit *= 2
    fast_bits = [CORE_BIT] + bits[:2]

    shards_of = (attn_gain, attn_shift, query_bias, value_bias, out_bias, mlp_gain, mlp_shift,
                 up_bias, down_bias)
    flat_vectors = jnp.concatenate(shards_of)
    all_vectors = lax.all_gather(flat_vectors, "shard", axis=0, tiled=False)
    vectors, at = [], 0
    for item in shards_of:
        size = item.shape[0]
        vectors.append(all_vectors[:, at : at + size].reshape(-1).astype(jnp.float32))
        at += size
    (gain_first, shift_first, bias_query, bias_value, bias_out, gain_second, shift_second, bias_up,
     bias_down) = vectors

    if pairwise:
        order = (0, 1)
        own_tokens = tokens.reshape(rows, width)
        got_qkv = spread_start(qkv_weight, fast_bits)
        got_out = spread_start(after(out_weight, got_qkv), fast_bits)
        other = cross(after(own_tokens, got_out))
        got_up = spread_start(after(up_weight, other), fast_bits)
        got_down = spread_start(after(down_weight, got_up), fast_bits)
        full_qkv = spread_end(qkv_weight, got_qkv, fast_bits)
        full_out = spread_end(out_weight, got_out, fast_bits)
        full_up = spread_end(up_weight, got_up, fast_bits)
        full_down = spread_end(down_weight, got_down, fast_bits)
        first = position == 0
        pair = tokens.shape[0], 1, span, width
        own_part, other_part = own_tokens.reshape(pair), other.reshape(pair)
        all_tokens = jnp.concatenate(
            [choose(first, own_part, other_part), choose(first, other_part, own_part)], axis=1
        ).reshape(seqs * length, width)
    else:
        full_qkv, full_out, full_up, full_down = [
            lax.all_gather(item, "shard", axis=0, tiled=True)
            for item in (qkv_weight, out_weight, up_weight, down_weight)
        ]
        all_tokens = lax.all_gather(tokens, "shard", axis=1, tiled=True).reshape(-1, width)

    def own_rows(values):
        per_seq = values.reshape(seqs, length, values.shape[-1])
        return lax.dynamic_slice_in_dim(per_seq, position * span, span, axis=1).reshape(rows, -1)

    grad_out = cotangent.reshape(rows, width)
    grad_out_both = jnp.concatenate([grad_out, swap(grad_out, CORE_BIT)], axis=0)

    flat = tokens.reshape(rows, width).astype(jnp.float32)
    unit_all, rstd_all = centred(all_tokens.astype(jnp.float32))
    normed_all = low(unit_all * gain_first + shift_first)
    normed_sib = swap(normed_all, CORE_BIT)
    normed = own_rows(normed_all)
    full_q, full_k, full_v = (full_qkv[:, i * width : (i + 1) * width] for i in range(3))
    queries = low(low(dot(normed, full_q) + bias_query) * SCALING)
    keys = low(dot(normed_all, full_k))
    values = low(dot(normed_all, full_v) + bias_value)
    spot = position.astype(jnp.int32).reshape(1)
    context, lse = attention_forward(spot, queries, keys, values, seqs, span)
    context_sib = swap(context, CORE_BIT)
    middle = flat + dot(context, full_out) + bias_out
    unit_second, rstd_second = centred(middle)
    normed_two = low(unit_second * gain_second + shift_second)
    normed_two_sib = swap(normed_two, CORE_BIT)
    active_float, slope = gelu_parts(dot(normed_two, full_up) + bias_up)
    active = low(active_float)
    slope = low(slope)

    def split_rows(lhs, rhs):
        if pairwise:
            give = dot_tn(columns_of(lhs, 1, 1 - position), rhs)
            keep = dot_tn(columns_of(lhs, 1, position), rhs)
            return reduce_start(low(give), low(keep))
        return lax.psum_scatter(low(dot_tn(lhs, rhs)), "shard", scatter_dimension=0, tiled=True)

    grouped = active.reshape(rows, shards, 2, -1)
    taken = jnp.where(core == 0, grouped[:, :, 0], grouped[:, :, 1]).reshape(rows, -1)
    given = jnp.where(core == 0, grouped[:, :, 1], grouped[:, :, 0]).reshape(rows, -1)
    active_both = jnp.concatenate([taken, swap(given, CORE_BIT)], axis=0)
    sum_down = split_rows(active_both, grad_out_both)
    sum_down = reduce_rest(sum_down, bits)
    sum_down = in_order(CORE_BIT, sum_down, swap(sum_down, CORE_BIT))

    result = middle + dot(active, full_down) + bias_down
    block_out = low(result).reshape(seqs, span, width)

    def by_columns(lhs_both, part):
        taken = columns_of(part, 1, core)
        given = columns_of(part, 1, 1 - core)
        return split_rows(lhs_both, jnp.concatenate([taken, swap(given, CORE_BIT)], axis=0))

    def join_columns(values):
        other = swap(values, CORE_BIT)
        left = choose(core == 0, values, other)
        right = choose(core == 0, other, values)
        return left, right

    grad_float = grad_out.astype(jnp.float32)
    grad_hidden = low(dot_nt(grad_out, full_down) * slope.astype(jnp.float32))
    normed_two_both = jnp.concatenate([normed_two, normed_two_sib], axis=0)
    sum_up = by_columns(normed_two_both, grad_hidden)
    sum_up = reduce_rest(sum_up, bits)
    sum_up = jnp.concatenate(join_columns(sum_up), axis=1)
    grad_normed_two = dot_nt(grad_hidden, full_up)
    grad_middle = norm_pull(grad_normed_two, unit_second, rstd_second, gain_second) + grad_float
    grad_branch = low(grad_middle)
    grad_context = low(dot_nt(grad_branch, full_out))
    context_both = jnp.concatenate([context, context_sib], axis=0)
    sum_out = by_columns(context_both, grad_branch)
    sum_out = reduce_rest(sum_out, bits)
    sum_out = jnp.concatenate(join_columns(sum_out), axis=1)

    grad_q, grad_k, grad_v = attention_backward(
        spot, queries, keys, values, grad_context, context, lse, seqs, span
    )
    normed_both = jnp.concatenate([normed_all, normed_sib], axis=0)
    own_both = jnp.concatenate([normed, own_rows(normed_sib)], axis=0)
    third = width // 2
    half_q, half_k, half_v = (
        jnp.concatenate(
            [columns_of(part, 1, core), swap(columns_of(part, 1, 1 - core), CORE_BIT)], axis=0
        )
        for part in (grad_q, grad_k, grad_v)
    )
    if pairwise:
        def three(index):
            left_own = columns_of(own_both, 1, index)
            left_all = columns_of(normed_both, 1, index)
            return low(jnp.concatenate(
                [dot_tn(left_own, half_q), dot_tn(left_all, half_k), dot_tn(left_all, half_v)],
                axis=1,
            ))
        sum_qkv = reduce_start(three(1 - position), three(position))
    else:
        sum_qkv = lax.psum_scatter(
            low(jnp.concatenate(
                [dot_tn(own_both, half_q), dot_tn(normed_both, half_k), dot_tn(normed_both, half_v)],
                axis=1,
            )),
            "shard", scatter_dimension=0, tiled=True,
        )
    sum_qkv = reduce_rest(sum_qkv, bits)
    left, right = join_columns(sum_qkv)
    sum_qkv = jnp.concatenate(
        [part[:, i * third : (i + 1) * third] for i in range(3) for part in (left, right)], axis=1
    )

    from_query = dot_nt(grad_q, full_q)
    from_rest = dot_nt(grad_k, full_k) + dot_nt(grad_v, full_v)
    if pairwise:
        halves_of = from_rest.reshape(seqs, 2, span, width)
        mine = choose(position == 0, halves_of[:, 0], halves_of[:, 1]).reshape(rows, width)
        theirs = choose(position == 0, halves_of[:, 1], halves_of[:, 0]).reshape(rows, width)
        grad_normed = from_query + mine + cross(low(theirs)).astype(jnp.float32)
    else:
        grad_normed = from_query + lax.psum_scatter(
            from_rest.reshape(seqs, length, width), "shard", scatter_dimension=1, tiled=True
        ).reshape(rows, width)
    unit_first, rstd_first = own_rows(unit_all), own_rows(rstd_all)
    grad_tokens = low(norm_pull(grad_normed, unit_first, rstd_first, gain_first) + grad_middle)

    def column_sum(values):
        return jnp.sum(values.astype(jnp.float32), axis=0)

    sums = (
        column_sum(grad_normed * unit_first),
        column_sum(grad_normed),
        column_sum(grad_q),
        column_sum(grad_v),
        column_sum(grad_branch),
        column_sum(grad_normed_two * unit_second),
        column_sum(grad_normed_two),
        column_sum(grad_hidden),
        column_sum(grad_float),
    )
    packed = jnp.concatenate([item.reshape(shards, -1) for item in sums], axis=1)
    packed = lax.psum(packed, ("replica", "shard"))
    packed = lax.dynamic_index_in_dim(packed, position, axis=0, keepdims=False)
    outs, at = [], 0
    for item in sums:
        size = item.shape[0] // shards
        outs.append(packed[at : at + size])
        at += size
    return (
        block_out,
        grad_tokens.reshape(seqs, span, width),
        sum_qkv.astype(jnp.float32),
        sum_out.astype(jnp.float32),
        sum_up.astype(jnp.float32),
        sum_down.astype(jnp.float32),
        *outs,
    )


def solution(mesh):
    vector, matrix, rows = P("shard"), P("shard", None), P("replica", "shard", None)
    return jax.shard_map(
        on_device,
        mesh=mesh,
        in_specs=(rows, *[matrix] * 4, *[vector] * 9, rows),
        out_specs=(rows, rows, *[matrix] * 4, *[vector] * 9),
        check_vma=False,
    )
```

time: 1340 us -> 832 us (0.62)
  waiting for transfers between devices: 903 us -> 215 us
  local copies, waits for them, and re-layouts: 36.3 us -> 148 us
  matrix products: 214 us -> 135 us
  starting transfers between devices: 0.52 us -> 79.2 us
  Pallas kernels: 0 us -> 69.1 us
  other arithmetic: 87.6 us -> 121 us
  blocking collectives: 73.2 us -> 45.2 us
  between operations: 16.9 us -> 2.39 us
    all_gather x6 -> x0, waiting for transfers between devices: 357 us -> none  [the longest x1 115 us: on_device(): lax.all_gather(pieces[2], 'shard', axis=0, tiled=True)]
    reduce_scatter x5 -> x0, waiting for transfers between devices: 272 us -> none  [the longest x1 114 us: on_device(): lax.psum_scatter(transposed_times(piece, grad_hidden).astype(jnp.bfloat16...]
    ppermute x0 -> x56, waiting for transfers between devices: none -> 215 us  [the longest x46 126 us: swap(): return lax.ppermute(values, 'replica', [(i, i ^ bit) for i in range(size)])]
    psum x1 -> x0, waiting for transfers between devices: 164 us -> none  [on_device(): lax.psum(owned[0].astype(jnp.bfloat16), 'replica').astype(jnp.float32)]
    unnamed x14 -> x0, waiting for transfers between devices: 110 us -> none
    ppermute x0 -> x56, starting transfers between devices: none -> 79.2 us  [the longest x46 75 us: swap(): return lax.ppermute(values, 'replica', [(i, i ^ bit) for i in range(size)])]
    dot_general x18 -> x24, matrix products: 214 us -> 135 us  [the longest x6 49.9 us: dot_nt(): lax.dot_general(left, right, (((1,), (1,)), ((), ())), preferred_element_...]
    pallas_call x0 -> x2, Pallas kernels: none -> 69.1 us  [the longest x1 37.4 us: attention_backward(): pl.pallas_call(functools.partial(backward_kernel, span=span, width=width)...]
  transfers between devices with their start and end apart: 13 -> 56, of which waited for: 12 -> 19; matrix products, arithmetic and copies ran while one was open for 16% -> 47% of each run, Pallas kernels for 0% -> 8%
where the time goes in v1:
time: 832 us; the launch traced here: 816 us
  waiting for transfers between devices  215 us (26%)
  local copies, waits for them, and re-layouts  148 us (18%)
  matrix products  135 us (16%)
  other arithmetic  121 us (15%)
  starting transfers between devices  79.2 us (10%)
  Pallas kernels  69.1 us (8%)
  blocking collectives  45.2 us (5%)
    ppermute x46, waiting for transfers between devices, swap(): return lax.ppermute(values, 'replica', [(i, i ^ bit) for i in range(size)])  126 us
    ppermute x10, waiting for transfers between devices, cross(): return lax.ppermute(values, 'shard', [(0, 1), (1, 0)])  89.8 us
    ppermute x46, starting transfers between devices, swap(): return lax.ppermute(values, 'replica', [(i, i ^ bit) for i in range(size)])  75 us
    select_n x42, other arithmetic, choose(): return jnp.where(flag, left, right)  55.8 us
    dot_general x6, matrix products, dot_nt(): lax.dot_general(left, right, (((1,), (1,)), ((), ())), preferred_element_...  49.9 us
    dot_general x12, matrix products, dot_tn(): lax.dot_general(left, right, (((0,), (0,)), ((), ())), preferred_element_...  46.6 us
    psum x1, blocking collectives, on_device(): packed = lax.psum(packed, ('replica', 'shard'))  41.9 us
    dot_general x6, matrix products, dot(): return jnp.dot(left, right, preferred_element_type=jnp.float32)  38.8 us
  transfers between devices with their start and end apart: 56, of which 19 were waited for; matrix products, arithmetic and copies ran while one was open for 47% of the time, Pallas kernels for 8%

profile of v1, /device:TPU:27, one launch (start us, length us, event | category | flops | bytes accessed | tf_op | source)
XLA Modules:
  0.0 816.0 jit_solution(10651981332331912845)
XLA Ops:
  2.3 11.7 %collective-permute-done = bf16[72,3264]{1,0:T(8,128)(2,1)} collective-permute-done((bf16[72,3264]{1,0:T(8,128)(2,1)S(1)}, bf16[72,3264]{1,0:T(8,128)(2,1)}, u32[]{:S(2)}, u32[]{:S(2)}) %collective-permute-start) | collective-permute-done | bytes 470048 | tf_op jit(solution)/shard_map/ppermute | solution.py:289
  22.4 6.2 concatenate.153
  35.7 8.7 %copy.117 = bf16[2176,1088]{1,0:T(8,128)(2,1)} copy(bf16[2176,1088]{0,1:T(8,128)(2,1)} %param.19) | data formatting | bytes 9469952 | tf_op args[4]
  53.8 4.4 collective-permute-done.3
  66.6 7.6 collective-permute-done.2
  92.2 8.2 %copy.116 = bf16[2176,1088]{1,0:T(8,128)(2,1)} copy(bf16[2176,1088]{0,1:T(8,128)(2,1)} %param.19) | data formatting | bytes 9469952 | tf_op jit(solution)/shard_map/optimization_barrier | solution.py:293
  108.1 5.8 collective-permute-done.13
  116.7 12.0 %collective-permute-done.14 = bf16[272,1088]{1,0:T(8,128)(2,1)S(1)} collective-permute-done((bf16[272,1088]{1,0:T(8,128)(2,1)S(1)}, bf16[272,1088]{1,0:T(8,128)(2,1)S(1)}, u32[]{:S(2)}, u32[]{:S(2)}) %collective-permute-start.14) | collective-permute-done | bytes 591904 | tf_op jit(solution)/shard_map/ppermute | solution.py:285
  138.1 4.7 add_convert_fusion.2.v_ref
  144.7 31.7 %attention_forward.1 = (bf16[512,1088]{1,0:T(8,128)(2,1)S(1)}, f32[9,2,512]{2,1,0:T(2,128)S(1)}) custom-call(s32[1]{0:T(128)} %bitcast.1.pos_ref, bf16[512,1088]{1,0:T(8,128)(2,1)S(1)} %fusion.19.q_ref, bf16[1024,1088]{1,0:T(8,128)(2,1)S(1)} %convolution_convert_fusion.4.k_ref, bf16[1024,1088]{1,0:T(8,128)(2,1)} %add_convert_fusion.2.v_ref), custom_call_target="tpu_custom_call" | custom-call | flops 4563402752 | bytes 8912896 | tf_op jit(solution)/shard_map/attention_forward/pallas_call | solution.py:180
  203.1 6.4 pad_maximum_fusion.18
  221.6 9.4 %broadcast_select_fusion.3 = (bf16[544,4352]{1,0:T(8,128)(2,1)S(1)}, bf16[544,4352]{1,0:T(8,128)(2,1)S(1)}) fusion(bf16[544,4352]{1,0:T(8,128)(2,1)} %param.18, pred[]{:T(512)S(6)} %eq.8, bf16[40,4352]{1,0:T(8,128)(2,1)S(1)} %slice.365, bf16[288,4352]{1,0:T(8,128)(2,1)S(1)} %get-tuple-element.124, bf16[288,4352]{1,0:T(8,128)(2,1)S(1)} %get-tuple-element.123), kind=kLoop, calls=%fused_computation.34 | loop fusion | flops 23674880 | bytes 19566592 | tf_op jit(solution)/shard_map/jit(_where)/select_n | solution.py:301
  231.1 11.0 %multiply_convert_fusion = (bf16[512,4352]{1,0:T(8,128)(2,1)}, f32[512,4352]{1,0:T(8,128)}) fusion(f32[4352]{0:T(1024)S(1)} %copy-done.84, bf16[512,1088]{1,0:T(8,128)(2,1)S(1)} %copy-done.37, bf16[544,4352]{1,0:T(8,128)(2,1)S(1)} %get-tuple-element.114, bf16[544,4352]{1,0:T(8,128)(2,1)S(1)} %get-tuple-element.113), kind=kOutput, calls=%fused_computation.8 | convolution fusion | flops 4889837568 | bytes 23970816 | tf_op jit(solution)/shard_map/dot_general | solution.py:264
  242.1 6.5 copy.142
  248.6 4.9 broadcast_select_fusion.17
  256.8 4.8 broadcast_select_fusion.1
  261.6 19.0 %convert_reduce_fusion = (f32[4352]{0:T(1024)}, bf16[512,4352]{1,0:T(8,128)(2,1)}) fusion(f32[512,4352]{1,0:T(8,128)} %get-tuple-element.207, f32[4352]{0:T(1024)S(1)} %copy-done.85, bf16[1,512,1088]{1,2,0:T(8,128)(2,1)S(1)} %copy-done.68, bf16[2176,1088]{1,0:T(8,128)(2,1)} %get-tuple-element.116, bf16[2176,1088]{1,0:T(8,128)(2,1)} %get-tuple-element.115), kind=kOutput, calls=%fused_computation.6 | convolution fusion | flops 4918800384 | bytes 23988224 | tf_op jit(solution)/shard_map/dot_general | solution.py:268
  280.6 12.2 %fusion.98 = (f32[1088]{0:T(1024)}, f32[512,1088]{0,1:T(8,128)}) fusion(bf16[512,4352]{1,0:T(8,128)(2,1)} %get-tuple-element.212, bf16[544,4352]{1,0:T(8,128)(2,1)} %copy-done.34, bf16[544,4352]{1,0:T(8,128)(2,1)} %copy-done.33), kind=kOutput, calls=%fused_computation.307 | convolution fusion | flops 4868111360 | bytes 16158976 | tf_op jit(solution)/shard_map/dot_general | solution.py:268
  311.2 37.4 %attention_backward.1 = (bf16[512,1088]{1,0:T(8,128)(2,1)S(1)}, bf16[1024,1088]{1,0:T(8,128)(2,1)}, bf16[1024,1088]{1,0:T(8,128)(2,1)}) custom-call(s32[1]{0:T(128)} %bitcast.1.pos_ref, bf16[512,1088]{1,0:T(8,128)(2,1)S(1)} %copy-done.1, bf16[1024,1088]{1,0:T(8,128)(2,1)} %copy-done.2, bf16[1024,1088]{1,0:T(8,128)(2,1)} %add_convert_fusion.2.v_ref, ...), custom_call_target="tpu_custom_call" | custom-call | flops 11408506880 | bytes 13369344 | tf_op jit(solution)/shard_map/attention_backward/pallas_call | solution.py:209
  350.7 4.9 fusion.89
  356.7 5.5 convolution_add_fusion
  362.2 5.8 copy.123
  384.2 13.0 %fusion.20 = bf16[1,512,1088]{2,1,0:T(8,128)(2,1)} fusion(f32[512,1088]{1,0:T(8,128)} %copy-done.5, bf16[512,4352]{1,0:T(8,128)(2,1)} %get-tuple-element.206, bf16[2176,1088]{1,0:T(8,128)(2,1)} %get-tuple-element.116, bf16[2176,1088]{1,0:T(8,128)(2,1)} %get-tuple-element.115, f32[1088]{0:T(1024)S(1)} %copy-done.87), kind=kOutput, calls=%fused_computation.67 | convolution fusion | flops 4869226496 | bytes 17273088 | tf_op jit(solution)/shard_map/dot_general | solution.py:264
  431.8 5.5 fusion.38
  446.3 5.5 fusion.37
  453.8 6.6 multiply_reduce_fusion.2
  462.7 4.5 collective-permute-done.33
  468.1 9.3 %collective-permute-done.34 = bf16[136,544]{1,0:T(8,128)(2,1)S(1)} collective-permute-done((bf16[136,544]{1,0:T(8,128)(2,1)S(1)}, bf16[136,544]{1,0:T(8,128)(2,1)S(1)}, u32[]{:S(2)}, u32[]{:S(2)}) %collective-permute-start.34) | collective-permute-done | bytes 148000 | tf_op jit(solution)/shard_map/ppermute | solution.py:285
  485.3 41.9 %psum.7 = f32[2,6528]{1,0:T(2,128)S(1)} all-reduce(f32[2,6528]{1,0:T(2,128)S(1)} %concatenate.198), channel_id=1, replica_groups=mesh['replica'=16,'shard'=2] {'replica','shard'}, use_global_device_ids=true, to_apply=%region_17.18 | all-reduce | flops 13056 | bytes 104448 | tf_op jit(solution)/shard_map/psum | solution.py:560
  529.7 5.7 convolution_convert_fusion
  543.3 4.7 convolution_convert_fusion.2
  548.2 4.7 convolution_convert_fusion.3
  553.0 10.6 %collective-permute-done.23 = bf16[272,1632]{1,0:T(8,128)(2,1)S(1)} collective-permute-done((bf16[272,1632]{1,0:T(8,128)(2,1)S(1)}, bf16[272,1632]{1,0:T(8,128)(2,1)S(1)}, u32[]{:S(2)}, u32[]{:S(2)}) %collective-permute-start.23) | collective-permute-done | bytes 887840 | tf_op jit(solution)/shard_map/ppermute | solution.py:285
  566.2 8.9 %collective-permute-done.24 = bf16[136,1632]{1,0:T(8,128)(2,1)S(1)} collective-permute-done((bf16[136,1632]{1,0:T(8,128)(2,1)S(1)}, bf16[136,1632]{1,0:T(8,128)(2,1)S(1)}, u32[]{:S(2)}, u32[]{:S(2)}) %collective-permute-start.24) | collective-permute-done | bytes 443936 | tf_op jit(solution)/shard_map/ppermute | solution.py:285
  575.7 13.6 %collective-permute-done.49 = bf16[1088,1088]{1,0:T(8,128)(2,1)S(1)} collective-permute-done((bf16[1088,1088]{1,0:T(8,128)(2,1)S(1)}, bf16[1088,1088]{1,0:T(8,128)(2,1)S(1)}, u32[]{:S(2)}, u32[]{:S(2)}) %collective-permute-start.49) | collective-permute-done | bytes 2367520 | tf_op jit(solution)/shard_map/ppermute | solution.py:289
  589.4 4.9 fusion.4
  594.6 45.5 %collective-permute-done.40 = bf16[544,2176]{1,0:T(8,128)(2,1)S(1)} collective-permute-done((bf16[544,2176]{1,0:T(8,128)(2,1)S(1)}, bf16[544,2176]{1,0:T(8,128)(2,1)S(1)}, u32[]{:S(2)}, u32[]{:S(2)}) %collective-permute-start.40) | collective-permute-done | bytes 2367520 | tf_op jit(solution)/shard_map/ppermute | solution.py:289
  641.3 8.6 %collective-permute-done.26 = bf16[136,1632]{1,0:T(8,128)(2,1)S(1)} collective-permute-done((bf16[136,1632]{1,0:T(8,128)(2,1)S(1)}, bf16[136,1632]{1,0:T(8,128)(2,1)S(1)}, u32[]{:S(2)}, u32[]{:S(2)}) %collective-permute-start.26) | collective-permute-done | bytes 443936 | tf_op jit(solution)/shard_map/ppermute | solution.py:285
  650.8 14.9 %collective-permute-done.41 = bf16[272,2176]{1,0:T(8,128)(2,1)S(1)} collective-permute-done((bf16[272,2176]{1,0:T(8,128)(2,1)S(1)}, bf16[272,2176]{1,0:T(8,128)(2,1)S(1)}, u32[]{:S(2)}, u32[]{:S(2)}) %collective-permute-start.41) | collective-permute-done | bytes 1183776 | tf_op jit(solution)/shard_map/ppermute | solution.py:285
  668.3 21.8 %collective-permute-done.42 = bf16[136,2176]{1,0:T(8,128)(2,1)S(1)} collective-permute-done((bf16[136,2176]{1,0:T(8,128)(2,1)S(1)}, bf16[136,2176]{1,0:T(8,128)(2,1)S(1)}, u32[]{:S(2)}, u32[]{:S(2)}) %collective-permute-start.42) | collective-permute-done | bytes 591904 | tf_op jit(solution)/shard_map/ppermute | solution.py:285
  693.3 28.4 %collective-permute-done.43 = bf16[136,2176]{1,0:T(8,128)(2,1)S(1)} collective-permute-done((bf16[136,2176]{1,0:T(8,128)(2,1)S(1)}, bf16[136,2176]{1,0:T(8,128)(2,1)S(1)}, u32[]{:S(2)}, u32[]{:S(2)}) %collective-permute-start.43) | collective-permute-done | bytes 591904 | tf_op jit(solution)/shard_map/ppermute | solution.py:285
  722.4 17.1 %collective-permute-start.28 = (bf16[544,1632]{1,0:T(8,128)(2,1)S(1)}, bf16[544,1632]{1,0:T(8,128)(2,1)S(1)}, u32[]{:S(2)}, u32[]{:S(2)}) collective-permute-start(bf16[544,1632]{1,0:T(8,128)(2,1)S(1)} %pad_maximum_fusion.30), channel_id=1, source_target_pairs={{0,2},{2,0},{4,6},{6,4},{8,10},{10,8},{12,14},{14,12},{16,18},{18,... | collective-permute-start | bytes 5326856 | tf_op jit(solution)/shard_map/ppermute | solution.py:285
  743.1 24.6 %collective-permute-start.55 = (bf16[1088,1088]{1,0:T(8,128)(2,1)}, bf16[1088,1088]{1,0:T(8,128)(2,1)}, u32[]{:S(2)}, u32[]{:S(2)}) collective-permute-start(bf16[1088,1088]{1,0:T(8,128)(2,1)} %pad_maximum_fusion.25), channel_id=1, source_target_pairs={{0,2},{2,0},{4,6},{6,4},{8,10},{10,8},{12,14},{14,12},{16,18},{18,... | collective-permute-start | bytes 7102472 | tf_op jit(solution)/shard_map/ppermute | solution.py:285
  772.4 7.4 concatenate.182
  779.8 5.6 convert_element_type.420
  792.0 4.5 maximum_convert_fusion
  796.5 12.3 %copy.148 = f32[2176,1088]{0,1:T(8,128)} copy(f32[2176,1088]{1,0:T(8,128)} %maximum_convert_fusion) | data formatting | bytes 18939904
  811.3 4.4 maximum_convert_fusion.1
  (459 shorter events, 250.4 us)
Async XLA Ops:
  2.0 12.0 %collective-permute-start = (bf16[72,3264]{1,0:T(8,128)(2,1)S(1)}, bf16[72,3264]{1,0:T(8,128)(2,1)}, u32[]{:S(2)}, u32[]{:S(2)}) collective-permute-start(bf16[72,3264]{1,0:T(8,128)(2,1)S(1)} %constant_dynamic-slice_fusion.6), channel_id=1, source_target_pairs={{0,1},{1,0},{2,3},{3,2},{4,5},{5,4},{6,7},{7,6},{8,9},{9,8},{10,11... | collective-permute-start | bytes 1410056 | tf_op jit(solution)/shard_map/ppermute | solution.py:289
  19.2 12.8 %collective-permute-start.6 = (bf16[72,1088]{1,0:T(8,128)(2,1)S(1)}, bf16[72,1088]{1,0:T(8,128)(2,1)S(1)}, u32[]{:S(2)}, u32[]{:S(2)}) collective-permute-start(bf16[72,1088]{1,0:T(8,128)(2,1)S(1)} %collective-permute-done.1), channel_id=1, source_target_pairs={{0,8},{2,10},{4,12},{6,14},{8,0},{10,2},{12,4},{14,6},{16,24},{18,... | collective-permute-start | bytes 470024 | tf_op jit(solution)/shard_map/ppermute | solution.py:285
  19.4 41.3 %collective-permute-start.48 = (bf16[512,1088]{0,1:T(8,128)(2,1)}, bf16[512,1088]{0,1:T(8,128)(2,1)}, u32[]{:S(2)}, u32[]{:S(2)}) collective-permute-start(bf16[512,1088]{0,1:T(8,128)(2,1)} %bitcast.82), channel_id=1, source_target_pairs={{0,2},{2,0},{4,6},{6,4},{8,10},{10,8},{12,14},{14,12},{16,18},{18,... | collective-permute-start | bytes 3342344 | tf_op jit(solution)/shard_map/ppermute | solution.py:285
  32.1 17.7 %collective-permute-start.7 = (bf16[144,1088]{1,0:T(8,128)(2,1)S(1)}, bf16[144,1088]{1,0:T(8,128)(2,1)}, u32[]{:S(2)}, u32[]{:S(2)}) collective-permute-start(bf16[144,1088]{1,0:T(8,128)(2,1)S(1)} %pad_maximum_fusion.65), channel_id=1, source_target_pairs={{0,4},{2,6},{4,0},{6,2},{8,12},{10,14},{12,8},{14,10},{16,20},{18,... | collective-permute-start | bytes 940040 | tf_op jit(solution)/shard_map/ppermute | solution.py:285
  46.9 11.3 %collective-permute-start.3 = (bf16[72,3264]{1,0:T(8,128)(2,1)}, bf16[72,3264]{1,0:T(8,128)(2,1)}, u32[]{:S(2)}, u32[]{:S(2)}) collective-permute-start(bf16[72,3264]{1,0:T(8,128)(2,1)} %collective-permute-done), channel_id=1, source_target_pairs={{0,8},{2,10},{4,12},{6,14},{8,0},{10,2},{12,4},{14,6},{16,24},{18,... | collective-permute-start | bytes 1410056 | tf_op jit(solution)/shard_map/ppermute | solution.py:285
  49.5 24.7 %collective-permute-start.2 = (bf16[512,1088]{0,1:T(8,128)(2,1)}, bf16[512,1088]{0,1:T(8,128)(2,1)}, u32[]{:S(2)}, u32[]{:S(2)}) collective-permute-start(bf16[512,1088]{0,1:T(8,128)(2,1)} %copy.109), channel_id=1, source_target_pairs={{0,1},{1,0},{2,3},{3,2},{4,5},{5,4},{6,7},{7,6},{8,9},{9,8},{10,11... | collective-permute-start | bytes 3342344 | tf_op jit(solution)/shard_map/ppermute | solution.py:289
  60.5 41.7 %collective-permute-start.4 = (bf16[144,3264]{1,0:T(8,128)(2,1)}, bf16[144,3264]{1,0:T(8,128)(2,1)}, u32[]{:S(2)}, u32[]{:S(2)}) collective-permute-start(bf16[144,3264]{1,0:T(8,128)(2,1)} %pad_maximum_fusion.56), channel_id=1, source_target_pairs={{0,4},{2,6},{4,0},{6,2},{8,12},{10,14},{12,8},{14,10},{16,20},{18,... | collective-permute-start | bytes 2820104 | tf_op jit(solution)/shard_map/ppermute | solution.py:285
  78.9 13.3 %collective-permute-start.9 = (bf16[72,4352]{1,0:T(8,128)(2,1)}, bf16[72,4352]{1,0:T(8,128)(2,1)}, u32[]{:S(2)}, u32[]{:S(2)}) collective-permute-start(bf16[72,4352]{1,0:T(8,128)(2,1)} %constant_dynamic-slice_fusion.3), channel_id=1, source_target_pairs={{0,1},{1,0},{2,3},{3,2},{4,5},{5,4},{6,7},{7,6},{8,9},{9,8},{10,11... | collective-permute-start | bytes 1880072 | tf_op jit(solution)/shard_map/ppermute | solution.py:289
  85.9 110.5 %collective-permute-start.18 = (bf16[1024,1088]{0,1:T(8,128)(2,1)}, bf16[1024,1088]{0,1:T(8,128)(2,1)}, u32[]{:S(2)}, u32[]{:S(2)}) collective-permute-start(bf16[1024,1088]{0,1:T(8,128)(2,1)} %copy.127), channel_id=1, source_target_pairs={{0,2},{2,0},{4,6},{6,4},{8,10},{10,8},{12,14},{14,12},{16,18},{18,... | collective-permute-start | bytes 6684680 | tf_op jit(solution)/shard_map/ppermute | solution.py:285
  101.7 12.1 %collective-permute-start.13 = (bf16[272,1088]{1,0:T(8,128)(2,1)S(1)}, bf16[272,1088]{1,0:T(8,128)(2,1)S(1)}, u32[]{:S(2)}, u32[]{:S(2)}) collective-permute-start(bf16[272,1088]{1,0:T(8,128)(2,1)S(1)} %constant_dynamic-slice_fusion.2), channel_id=1, source_target_pairs={{0,1},{1,0},{2,3},{3,2},{4,5},{5,4},{6,7},{7,6},{8,9},{9,8},{10,11... | collective-permute-start | bytes 1775624 | tf_op jit(solution)/shard_map/ppermute | solution.py:289
  102.0 12.0 %collective-permute-start.10 = (bf16[72,4352]{1,0:T(8,128)(2,1)}, bf16[72,4352]{1,0:T(8,128)(2,1)S(1)}, u32[]{:S(2)}, u32[]{:S(2)}) collective-permute-start(bf16[72,4352]{1,0:T(8,128)(2,1)} %collective-permute-done.9), channel_id=1, source_target_pairs={{0,8},{2,10},{4,12},{6,14},{8,0},{10,2},{12,4},{14,6},{16,24},{18,... | collective-permute-start | bytes 1880072 | tf_op jit(solution)/shard_map/ppermute | solution.py:285
  103.9 26.5 %collective-permute-start.5 = (bf16[288,3264]{1,0:T(8,128)(2,1)S(1)}, bf16[288,3264]{1,0:T(8,128)(2,1)S(1)}, u32[]{:S(2)}, u32[]{:S(2)}) collective-permute-start(bf16[288,3264]{1,0:T(8,128)(2,1)S(1)} %pad_maximum_fusion.29), channel_id=1, source_target_pairs={{0,2},{2,0},{4,6},{6,4},{8,10},{10,8},{12,14},{14,12},{16,18},{18,... | collective-permute-start | bytes 5640200 | tf_op jit(solution)/shard_map/ppermute | solution.py:285
  113.8 14.9 %collective-permute-start.14 = (bf16[272,1088]{1,0:T(8,128)(2,1)S(1)}, bf16[272,1088]{1,0:T(8,128)(2,1)S(1)}, u32[]{:S(2)}, u32[]{:S(2)}) collective-permute-start(bf16[272,1088]{1,0:T(8,128)(2,1)S(1)} %collective-permute-done.13), channel_id=1, source_target_pairs={{0,8},{2,10},{4,12},{6,14},{8,0},{10,2},{12,4},{14,6},{16,24},{18,... | collective-permute-start | bytes 1775624 | tf_op jit(solution)/shard_map/ppermute | solution.py:285
  116.5 66.3 %collective-permute-start.11 = (bf16[144,4352]{1,0:T(8,128)(2,1)}, bf16[144,4352]{1,0:T(8,128)(2,1)}, u32[]{:S(2)}, u32[]{:S(2)}) collective-permute-start(bf16[144,4352]{1,0:T(8,128)(2,1)} %pad_maximum_fusion.52), channel_id=1, source_target_pairs={{0,4},{2,6},{4,0},{6,2},{8,12},{10,14},{12,8},{14,10},{16,20},{18,... | collective-permute-start | bytes 3760136 | tf_op jit(solution)/shard_map/ppermute | solution.py:285
  130.2 79.3 %collective-permute-start.15 = (bf16[544,1088]{1,0:T(8,128)(2,1)}, bf16[544,1088]{1,0:T(8,128)(2,1)}, u32[]{:S(2)}, u32[]{:S(2)}) collective-permute-start(bf16[544,1088]{1,0:T(8,128)(2,1)} %pad_maximum_fusion.53), channel_id=1, source_target_pairs={{0,4},{2,6},{4,0},{6,2},{8,12},{10,14},{12,8},{14,10},{16,20},{18,... | collective-permute-start | bytes 3551240 | tf_op jit(solution)/shard_map/ppermute | solution.py:285
  188.5 29.8 %collective-permute-start.12 = (bf16[288,4352]{1,0:T(8,128)(2,1)}, bf16[288,4352]{1,0:T(8,128)(2,1)}, u32[]{:S(2)}, u32[]{:S(2)}) collective-permute-start(bf16[288,4352]{1,0:T(8,128)(2,1)} %pad_maximum_fusion.23), channel_id=1, source_target_pairs={{0,2},{2,0},{4,6},{6,4},{8,10},{10,8},{12,14},{14,12},{16,18},{18,... | collective-permute-start | bytes 7520264 | tf_op jit(solution)/shard_map/ppermute | solution.py:285
  195.8 17.8 %collective-permute-start.38 = (bf16[512,1088]{0,1:T(8,128)(2,1)}, bf16[512,1088]{0,1:T(8,128)(2,1)}, u32[]{:S(2)}, u32[]{:S(2)}) collective-permute-start(bf16[512,1088]{0,1:T(8,128)(2,1)} %copy.140), channel_id=1, source_target_pairs={{0,2},{2,0},{4,6},{6,4},{8,10},{10,8},{12,14},{14,12},{16,18},{18,... | collective-permute-start | bytes 3342344 | tf_op jit(solution)/shard_map/ppermute | solution.py:285
  195.8 20.1 %collective-permute-start.29 = (bf16[512,1088]{0,1:T(8,128)(2,1)}, bf16[512,1088]{0,1:T(8,128)(2,1)}, u32[]{:S(2)}, u32[]{:S(2)}) collective-permute-start(bf16[512,1088]{0,1:T(8,128)(2,1)} %copy.136), channel_id=1, source_target_pairs={{0,2},{2,0},{4,6},{6,4},{8,10},{10,8},{12,14},{14,12},{16,18},{18,... | collective-permute-start | bytes 3342344 | tf_op jit(solution)/shard_map/ppermute | solution.py:285
  213.6 40.4 %collective-permute-start.16 = (bf16[1088,1088]{1,0:T(8,128)(2,1)}, bf16[1088,1088]{1,0:T(8,128)(2,1)}, u32[]{:S(2)}, u32[]{:S(2)}) collective-permute-start(bf16[1088,1088]{1,0:T(8,128)(2,1)} %pad_maximum_fusion.24), channel_id=1, source_target_pairs={{0,2},{2,0},{4,6},{6,4},{8,10},{10,8},{12,14},{14,12},{16,18},{18,... | collective-permute-start | bytes 7102472 | tf_op jit(solution)/shard_map/ppermute | solution.py:285
  253.5 276.2 %collective-permute-start.47 = (bf16[512,2176]{0,1:T(8,128)(2,1)}, bf16[512,2176]{0,1:T(8,128)(2,1)}, u32[]{:S(2)}, u32[]{:S(2)}) collective-permute-start(bf16[512,2176]{0,1:T(8,128)(2,1)} %bitcast.15), channel_id=1, source_target_pairs={{0,2},{2,0},{4,6},{6,4},{8,10},{10,8},{12,14},{14,12},{16,18},{18,... | collective-permute-start | bytes 6684680 | tf_op jit(solution)/shard_map/ppermute | solution.py:285
  372.4 72.0 %collective-permute-start.17 = (bf16[512,1088]{0,1:T(8,128)(2,1)}, bf16[512,1088]{0,1:T(8,128)(2,1)}, u32[]{:S(2)}, u32[]{:S(2)}) collective-permute-start(bf16[512,1088]{0,1:T(8,128)(2,1)} %copy.125), channel_id=1, source_target_pairs={{0,1},{1,0},{2,3},{3,2},{4,5},{5,4},{6,7},{7,6},{8,9},{9,8},{10,11... | collective-permute-start | bytes 3342344 | tf_op jit(solution)/shard_map/ppermute | solution.py:289
  379.4 163.4 %collective-permute-start.39 = (bf16[512,2176]{1,0:T(8,128)(2,1)}, bf16[512,2176]{1,0:T(8,128)(2,1)}, u32[]{:S(2)}, u32[]{:S(2)}) collective-permute-start(bf16[512,2176]{1,0:T(8,128)(2,1)} %get-tuple-element.132), channel_id=1, source_target_pairs={{0,2},{2,0},{4,6},{6,4},{8,10},{10,8},{12,14},{14,12},{16,18},{18,... | collective-permute-start | bytes 6684680 | tf_op jit(solution)/shard_map/ppermute | solution.py:285
  381.6 28.9 %collective-permute-start.30 = (bf16[512,544]{0,1:T(8,128)(2,1)}, bf16[512,544]{0,1:T(8,128)(2,1)}, u32[]{:S(2)}, u32[]{:S(2)}) collective-permute-start(bf16[512,544]{0,1:T(8,128)(2,1)} %copy.138), channel_id=1, source_target_pairs={{0,2},{2,0},{4,6},{6,4},{8,10},{10,8},{12,14},{14,12},{16,18},{18,... | collective-permute-start | bytes 1671176 | tf_op jit(solution)/shard_map/ppermute | solution.py:285
  384.1 29.0 %collective-permute-start.19 = (bf16[512,544]{0,1:T(8,128)(2,1)}, bf16[512,544]{0,1:T(8,128)(2,1)}, u32[]{:S(2)}, u32[]{:S(2)}) collective-permute-start(bf16[512,544]{0,1:T(8,128)(2,1)} %copy.129), channel_id=1, source_target_pairs={{0,2},{2,0},{4,6},{6,4},{8,10},{10,8},{12,14},{14,12},{16,18},{18,... | collective-permute-start | bytes 1671176 | tf_op jit(solution)/shard_map/ppermute | solution.py:285
  410.5 14.7 %collective-permute-start.21 = (bf16[1024,544]{0,1:T(8,128)(2,1)}, bf16[1024,544]{0,1:T(8,128)(2,1)}, u32[]{:S(2)}, u32[]{:S(2)}) collective-permute-start(bf16[1024,544]{0,1:T(8,128)(2,1)} %copy.134), channel_id=1, source_target_pairs={{0,2},{2,0},{4,6},{6,4},{8,10},{10,8},{12,14},{14,12},{16,18},{18,... | collective-permute-start | bytes 3342344 | tf_op jit(solution)/shard_map/ppermute | solution.py:285
  413.2 16.2 %collective-permute-start.20 = (bf16[1024,544]{0,1:T(8,128)(2,1)}, bf16[1024,544]{0,1:T(8,128)(2,1)}, u32[]{:S(2)}, u32[]{:S(2)}) collective-permute-start(bf16[1024,544]{0,1:T(8,128)(2,1)} %copy.132), channel_id=1, source_target_pairs={{0,2},{2,0},{4,6},{6,4},{8,10},{10,8},{12,14},{14,12},{16,18},{18,... | collective-permute-start | bytes 3342344 | tf_op jit(solution)/shard_map/ppermute | solution.py:285
  425.1 26.7 %collective-permute-start.31 = (bf16[544,544]{1,0:T(8,128)(2,1)}, bf16[544,544]{1,0:T(8,128)(2,1)}, u32[]{:S(2)}, u32[]{:S(2)}) collective-permute-start(bf16[544,544]{1,0:T(8,128)(2,1)} %convolution_convert_fusion.6), channel_id=1, source_target_pairs={{0,1},{1,0},{2,3},{3,2},{4,5},{5,4},{6,7},{7,6},{8,9},{9,8},{10,11... | collective-permute-start | bytes 1775624 | tf_op jit(solution)/shard_map/ppermute | solution.py:289
  444.3 95.3 %collective-permute-start.22 = (bf16[544,1632]{1,0:T(8,128)(2,1)}, bf16[544,1632]{1,0:T(8,128)(2,1)}, u32[]{:S(2)}, u32[]{:S(2)}) collective-permute-start(bf16[544,1632]{1,0:T(8,128)(2,1)} %concatenate.179), channel_id=1, source_target_pairs={{0,1},{1,0},{2,3},{3,2},{4,5},{5,4},{6,7},{7,6},{8,9},{9,8},{10,11... | collective-permute-start | bytes 5326856 | tf_op jit(solution)/shard_map/ppermute | solution.py:289
  477.4 51.2 %collective-permute-start.35 = (bf16[136,544]{1,0:T(8,128)(2,1)S(1)}, bf16[136,544]{1,0:T(8,128)(2,1)S(1)}, u32[]{:S(2)}, u32[]{:S(2)}) collective-permute-start(bf16[136,544]{1,0:T(8,128)(2,1)S(1)} %add_convert_fusion.18), channel_id=1, source_target_pairs={{0,8},{2,10},{4,12},{6,14},{8,0},{10,2},{12,4},{14,6},{16,24},{18,... | collective-permute-start | bytes 443912 | tf_op jit(solution)/shard_map/ppermute | solution.py:285
  535.4 53.9 %collective-permute-start.49 = (bf16[1088,1088]{1,0:T(8,128)(2,1)S(1)}, bf16[1088,1088]{1,0:T(8,128)(2,1)S(1)}, u32[]{:S(2)}, u32[]{:S(2)}) collective-permute-start(bf16[1088,1088]{1,0:T(8,128)(2,1)S(1)} %convolution_convert_fusion), channel_id=1, source_target_pairs={{0,1},{1,0},{2,3},{3,2},{4,5},{5,4},{6,7},{7,6},{8,9},{9,8},{10,11... | collective-permute-start | bytes 7102472 | tf_op jit(solution)/shard_map/ppermute | solution.py:289
  536.5 27.5 %collective-permute-start.37 = (bf16[544,544]{1,0:T(8,128)(2,1)S(1)}, bf16[544,544]{1,0:T(8,128)(2,1)S(1)}, u32[]{:S(2)}, u32[]{:S(2)}) collective-permute-start(bf16[544,544]{1,0:T(8,128)(2,1)S(1)} %pad_maximum_fusion.62), channel_id=1, source_target_pairs={{0,2},{2,0},{4,6},{6,4},{8,10},{10,8},{12,14},{14,12},{16,18},{18,... | collective-permute-start | bytes 1775624 | tf_op jit(solution)/shard_map/ppermute | solution.py:285
  541.8 21.8 %collective-permute-start.23 = (bf16[272,1632]{1,0:T(8,128)(2,1)S(1)}, bf16[272,1632]{1,0:T(8,128)(2,1)S(1)}, u32[]{:S(2)}, u32[]{:S(2)}) collective-permute-start(bf16[272,1632]{1,0:T(8,128)(2,1)S(1)} %broadcast_select_fusion.48), channel_id=1, source_target_pairs={{0,4},{2,6},{4,0},{6,2},{8,12},{10,14},{12,8},{14,10},{16,20},{18,... | collective-permute-start | bytes 2663432 | tf_op jit(solution)/shard_map/ppermute | solution.py:285
  548.0 92.1 %collective-permute-start.40 = (bf16[544,2176]{1,0:T(8,128)(2,1)S(1)}, bf16[544,2176]{1,0:T(8,128)(2,1)S(1)}, u32[]{:S(2)}, u32[]{:S(2)}) collective-permute-start(bf16[544,2176]{1,0:T(8,128)(2,1)S(1)} %convolution_convert_fusion.2), channel_id=1, source_target_pairs={{0,1},{1,0},{2,3},{3,2},{4,5},{5,4},{6,7},{7,6},{8,9},{9,8},{10,11... | collective-permute-start | bytes 7102472 | tf_op jit(solution)/shard_map/ppermute | solution.py:289
  575.3 65.4 %collective-permute-start.25 = (bf16[136,1632]{1,0:T(8,128)(2,1)S(1)}, bf16[136,1632]{1,0:T(8,128)(2,1)S(1)}, u32[]{:S(2)}, u32[]{:S(2)}) collective-permute-start(bf16[136,1632]{1,0:T(8,128)(2,1)S(1)} %add_convert_fusion.16), channel_id=1, source_target_pairs={{0,16},{2,18},{4,20},{6,22},{8,24},{10,26},{12,28},{14,30},{16,0},... | collective-permute-start | bytes 1331720 | tf_op jit(solution)/shard_map/ppermute | solution.py:285
  594.4 55.5 %collective-permute-start.50 = (bf16[544,1088]{1,0:T(8,128)(2,1)S(1)}, bf16[544,1088]{1,0:T(8,128)(2,1)S(1)}, u32[]{:S(2)}, u32[]{:S(2)}) collective-permute-start(bf16[544,1088]{1,0:T(8,128)(2,1)S(1)} %broadcast_select_fusion.30), channel_id=1, source_target_pairs={{0,4},{2,6},{4,0},{6,2},{8,12},{10,14},{12,8},{14,10},{16,20},{18,... | collective-permute-start | bytes 3551240 | tf_op jit(solution)/shard_map/ppermute | solution.py:285
  641.0 24.7 %collective-permute-start.41 = (bf16[272,2176]{1,0:T(8,128)(2,1)S(1)}, bf16[272,2176]{1,0:T(8,128)(2,1)S(1)}, u32[]{:S(2)}, u32[]{:S(2)}) collective-permute-start(bf16[272,2176]{1,0:T(8,128)(2,1)S(1)} %broadcast_select_fusion.39), channel_id=1, source_target_pairs={{0,4},{2,6},{4,0},{6,2},{8,12},{10,14},{12,8},{14,10},{16,20},{18,... | collective-permute-start | bytes 3551240 | tf_op jit(solution)/shard_map/ppermute | solution.py:285
  650.5 17.1 %collective-permute-start.51 = (bf16[272,1088]{1,0:T(8,128)(2,1)S(1)}, bf16[272,1088]{1,0:T(8,128)(2,1)S(1)}, u32[]{:S(2)}, u32[]{:S(2)}) collective-permute-start(bf16[272,1088]{1,0:T(8,128)(2,1)S(1)} %broadcast_select_fusion.59), channel_id=1, source_target_pairs={{0,8},{2,10},{4,12},{6,14},{8,0},{10,2},{12,4},{14,6},{16,24},{18,... | collective-permute-start | bytes 1775624 | tf_op jit(solution)/shard_map/ppermute | solution.py:285
  666.2 23.9 %collective-permute-start.42 = (bf16[136,2176]{1,0:T(8,128)(2,1)S(1)}, bf16[136,2176]{1,0:T(8,128)(2,1)S(1)}, u32[]{:S(2)}, u32[]{:S(2)}) collective-permute-start(bf16[136,2176]{1,0:T(8,128)(2,1)S(1)} %broadcast_select_fusion.66), channel_id=1, source_target_pairs={{0,8},{2,10},{4,12},{6,14},{8,0},{10,2},{12,4},{14,6},{16,24},{18,... | collective-permute-start | bytes 1775624 | tf_op jit(solution)/shard_map/ppermute | solution.py:285
  667.5 23.0 %collective-permute-start.27 = (bf16[272,1632]{1,0:T(8,128)(2,1)S(1)}, bf16[272,1632]{1,0:T(8,128)(2,1)S(1)}, u32[]{:S(2)}, u32[]{:S(2)}) collective-permute-start(bf16[272,1632]{1,0:T(8,128)(2,1)S(1)} %pad_maximum_fusion.57), channel_id=1, source_target_pairs={{0,4},{2,6},{4,0},{6,2},{8,12},{10,14},{12,8},{14,10},{16,20},{18,... | collective-permute-start | bytes 2663432 | tf_op jit(solution)/shard_map/ppermute | solution.py:285
  667.9 23.0 %collective-permute-start.52 = (bf16[272,1088]{1,0:T(8,128)(2,1)S(1)}, bf16[272,1088]{1,0:T(8,128)(2,1)S(1)}, u32[]{:S(2)}, u32[]{:S(2)}) collective-permute-start(bf16[272,1088]{1,0:T(8,128)(2,1)S(1)} %add_convert_fusion.12), channel_id=1, source_target_pairs={{0,16},{2,18},{4,20},{6,22},{8,24},{10,26},{12,28},{14,30},{16,0},... | collective-permute-start | bytes 1775624 | tf_op jit(solution)/shard_map/ppermute | solution.py:285
  690.4 31.3 %collective-permute-start.43 = (bf16[136,2176]{1,0:T(8,128)(2,1)S(1)}, bf16[136,2176]{1,0:T(8,128)(2,1)S(1)}, u32[]{:S(2)}, u32[]{:S(2)}) collective-permute-start(bf16[136,2176]{1,0:T(8,128)(2,1)S(1)} %add_convert_fusion.14), channel_id=1, source_target_pairs={{0,16},{2,18},{4,20},{6,22},{8,24},{10,26},{12,28},{14,30},{16,0},... | collective-permute-start | bytes 1775624 | tf_op jit(solution)/shard_map/ppermute | solution.py:285
  691.0 30.9 %collective-permute-start.53 = (bf16[272,1088]{1,0:T(8,128)(2,1)S(1)}, bf16[272,1088]{1,0:T(8,128)(2,1)S(1)}, u32[]{:S(2)}, u32[]{:S(2)}) collective-permute-start(bf16[272,1088]{1,0:T(8,128)(2,1)S(1)} %add_convert_fusion.11), channel_id=1, source_target_pairs={{0,8},{2,10},{4,12},{6,14},{8,0},{10,2},{12,4},{14,6},{16,24},{18,... | collective-permute-start | bytes 1775624 | tf_op jit(solution)/shard_map/ppermute | solution.py:285
  721.8 17.7 %collective-permute-start.44 = (bf16[136,2176]{1,0:T(8,128)(2,1)S(1)}, bf16[136,2176]{1,0:T(8,128)(2,1)S(1)}, u32[]{:S(2)}, u32[]{:S(2)}) collective-permute-start(bf16[136,2176]{1,0:T(8,128)(2,1)S(1)} %add_convert_fusion.13), channel_id=1, source_target_pairs={{0,8},{2,10},{4,12},{6,14},{8,0},{10,2},{12,4},{14,6},{16,24},{18,... | collective-permute-start | bytes 1775624 | tf_op jit(solution)/shard_map/ppermute | solution.py:285
  722.1 18.8 %collective-permute-start.54 = (bf16[544,1088]{1,0:T(8,128)(2,1)S(1)}, bf16[544,1088]{1,0:T(8,128)(2,1)S(1)}, u32[]{:S(2)}, u32[]{:S(2)}) collective-permute-start(bf16[544,1088]{1,0:T(8,128)(2,1)S(1)} %pad_maximum_fusion.54), channel_id=1, source_target_pairs={{0,4},{2,6},{4,0},{6,2},{8,12},{10,14},{12,8},{14,10},{16,20},{18,... | collective-permute-start | bytes 3551240 | tf_op jit(solution)/shard_map/ppermute | solution.py:285
  722.4 45.3 %collective-permute-start.28 = (bf16[544,1632]{1,0:T(8,128)(2,1)S(1)}, bf16[544,1632]{1,0:T(8,128)(2,1)S(1)}, u32[]{:S(2)}, u32[]{:S(2)}) collective-permute-start(bf16[544,1632]{1,0:T(8,128)(2,1)S(1)} %pad_maximum_fusion.30), channel_id=1, source_target_pairs={{0,2},{2,0},{4,6},{6,4},{8,10},{10,8},{12,14},{14,12},{16,18},{18,... | collective-permute-start | bytes 5326856 | tf_op jit(solution)/shard_map/ppermute | solution.py:285
  740.9 44.5 %collective-permute-start.45 = (bf16[272,2176]{1,0:T(8,128)(2,1)}, bf16[272,2176]{1,0:T(8,128)(2,1)}, u32[]{:S(2)}, u32[]{:S(2)}) collective-permute-start(bf16[272,2176]{1,0:T(8,128)(2,1)} %pad_maximum_fusion.55), channel_id=1, source_target_pairs={{0,4},{2,6},{4,0},{6,2},{8,12},{10,14},{12,8},{14,10},{16,20},{18,... | collective-permute-start | bytes 3551240 | tf_op jit(solution)/shard_map/ppermute | solution.py:285
  743.1 46.1 %collective-permute-start.55 = (bf16[1088,1088]{1,0:T(8,128)(2,1)}, bf16[1088,1088]{1,0:T(8,128)(2,1)}, u32[]{:S(2)}, u32[]{:S(2)}) collective-permute-start(bf16[1088,1088]{1,0:T(8,128)(2,1)} %pad_maximum_fusion.25), channel_id=1, source_target_pairs={{0,2},{2,0},{4,6},{6,4},{8,10},{10,8},{12,14},{14,12},{16,18},{18,... | collective-permute-start | bytes 7102472 | tf_op jit(solution)/shard_map/ppermute | solution.py:285
  789.2 19.5 %collective-permute-start.46 = (bf16[544,2176]{1,0:T(8,128)(2,1)}, bf16[544,2176]{1,0:T(8,128)(2,1)}, u32[]{:S(2)}, u32[]{:S(2)}) collective-permute-start(bf16[544,2176]{1,0:T(8,128)(2,1)} %pad_maximum_fusion.26), channel_id=1, source_target_pairs={{0,2},{2,0},{4,6},{6,4},{8,10},{10,8},{12,14},{14,12},{16,18},{18,... | collective-permute-start | bytes 7102472 | tf_op jit(solution)/shard_map/ppermute | solution.py:285
  (104 other events, 984.0 us)

commit v2 on v1

--- a/solution.py
+++ b/solution.py
@@ -42,7 +42,7 @@
     return key_at <= row_at
 
 
-def forward_kernel(pos_ref, q_ref, k_ref, v_ref, ctx_ref, lse_ref, kc_ref, vt_ref, *, span, width):
+def forward_kernel(pos_ref, q_ref, k_ref, v_ref, ctx_ref, ctx_t_ref, lse_ref, kc_ref, vt_ref, *, span, width):
     pos = pos_ref[0]
     block = min(256, span)
     queries = _clean(q_ref, width)
@@ -92,6 +92,7 @@
         row = lax.broadcasted_iota(jnp.int32, acc0.shape, 0)
         both = jnp.where(row < HD, acc0 / total0, acc1 / total1)
         ctx_ref[at : at + block, :] = both.T.astype(ctx_ref.dtype)
+        ctx_t_ref[:, at : at + block] = both.astype(ctx_t_ref.dtype)
         lse_ref[0, 0:1, at : at + block] = peak0 + jnp.log(total0)
         lse_ref[0, 1:2, at : at + block] = peak1 + jnp.log(total1)
 
@@ -183,7 +184,7 @@
             num_scalar_prefetch=1,
             grid=(seqs, pairs),
             in_specs=[own, whole, whole],
-            out_specs=[own, lse],
+            out_specs=[own, pl.BlockSpec((LANES, span), lambda s, h, p: (h, s)), lse],
             scratch_shapes=[
                 pltpu.VMEM((length, LANES), jnp.bfloat16),
                 pltpu.VMEM((length // span, LANES, span), jnp.bfloat16),
@@ -191,6 +192,7 @@
         ),
         out_shape=[
             jax.ShapeDtypeStruct((rows, width), jnp.bfloat16),
+            jax.ShapeDtypeStruct((width, rows), jnp.bfloat16),
             jax.ShapeDtypeStruct((seqs * pairs, 2, span), jnp.float32),
         ],
         compiler_params=pltpu.CompilerParams(vmem_limit_bytes=48 * 1024 * 1024),
@@ -289,10 +291,6 @@
     return lax.ppermute(values, "shard", [(0, 1), (1, 0)])
 
 
-def after(values, earlier):
-    return lax.optimization_barrier((values, earlier))[0]
-
-
 def has_bit(bit):
     return (lax.axis_index("replica") & bit) != 0
 
@@ -306,32 +304,17 @@
     return jnp.concatenate([choose(flag, other, mine), choose(flag, mine, other)], axis=0)
 
 
-def spread_start(weight, bits):
-    rows = weight.shape[0]
-    count = 2 ** len(bits)
-    size = -(-rows // (8 * count)) * 8
-    index = jnp.int32(0)
-    for bit in bits:
-        index = index * 2 + has_bit(bit).astype(jnp.int32)
-    start = jnp.minimum(index * size, rows - size)
-    return cross(lax.dynamic_slice_in_dim(weight, start, size, axis=0))
-
-
-def spread_end(weight, got, bits):
-    rows = weight.shape[0]
-    count = 2 ** len(bits)
-    size = got.shape[0]
-    for bit in bits[::-1]:
-        got = in_order(bit, got, swap(got, bit))
-    extra = count * size - rows
-    if extra:
-        got = jnp.concatenate([got[: (count - 1) * size], got[(count - 1) * size + extra :]], axis=0)
+def both_halves(weight, got):
     first = lax.axis_index("shard") == 0
     return jnp.concatenate([choose(first, weight, got), choose(first, got, weight)], axis=0)
 
 
-def reduce_start(give, keep):
-    return low(keep.astype(jnp.float32) + cross(low(give)).astype(jnp.float32))
+def all_bits():
+    bits, bit = [], 2
+    while bit < lax.axis_size("replica"):
+        bits.append(bit)
+        bit *= 2
+    return bits
 
 
 def halves(values):
@@ -365,25 +348,544 @@
     return choose(index == 0, low_part, high_part)
 
 
-def on_device(
+VMEM_LIMIT = 60 * 1024 * 1024
+CHUNK = 256
+
+
+def _vmem(count):
+    return [pl.BlockSpec(memory_space=pltpu.VMEM)] * count
+
+
+def _call(kernel, name, in_specs, out_shapes, scratch, flops, moved):
+    return pl.pallas_call(
+        kernel,
+        grid_spec=pltpu.PrefetchScalarGridSpec(
+            num_scalar_prefetch=1, grid=(1,), in_specs=in_specs,
+            out_specs=[pl.BlockSpec(memory_space=pltpu.VMEM)] * len(out_shapes),
+            scratch_shapes=scratch,
+        ),
+        out_shape=out_shapes,
+        compiler_params=pltpu.CompilerParams(vmem_limit_bytes=VMEM_LIMIT),
+        cost_estimate=pl.CostEstimate(flops=flops, bytes_accessed=moved, transcendentals=0),
+        name=name,
+    )
+
+
+def _fetch(own_ref, got_ref, full_ref, sems, pos, at, width):
+    rows = own_ref.shape[0]
+    cols = pl.ds(at, width)
+    mine = pl.ds(pl.multiple_of(pos * rows, 16), rows)
+    theirs = pl.ds(pl.multiple_of((1 - pos) * rows, 16), rows)
+    return (
+        pltpu.make_async_copy(own_ref.at[:, cols], full_ref.at[mine, cols], sems.at[0]),
+        pltpu.make_async_copy(got_ref.at[:, cols], full_ref.at[theirs, cols], sems.at[1]),
+    )
+
+
+def up_kernel(pos_ref, nt_ref, bias_ref, own_ref, got_ref, act_ref, slope_ref, full_ref, sems):
+    pos = pos_ref[0]
+    units = own_ref.shape[1]
+    count = units // CHUNK
+    copies = [_fetch(own_ref, got_ref, full_ref, sems.at[j], pos, j * CHUNK, CHUNK) for j in range(count)]
+    for pair in copies:
+        for copy in pair:
+            copy.start()
+    normed = nt_ref[...]
+    early = min(3, count)
+    for j in range(early):
+        for copy in copies[j]:
+            copy.wait()
+
+    for j in range(count):
+        if j == early:
+            for later in copies[early:]:
+                for copy in later:
+                    copy.wait()
+        cols = pl.ds(j * CHUNK, CHUNK)
+        hidden = _nn(normed, full_ref[:, cols]) + bias_ref[:, cols]
+        value, slope = gelu_parts(hidden)
+        value = value.astype(jnp.bfloat16)
+        act_ref[:, cols] = value
+        slope_ref[:, cols] = slope.astype(jnp.bfloat16)
+
+
+def mlp_up(spot, normed, bias, own, got):
+    rows, width = normed.shape
+    units = own.shape[1]
+    any_spec = pl.BlockSpec(memory_space=pl.ANY)
+    return _call(
+        up_kernel, "mlp_up", _vmem(2) + [any_spec] * 2,
+        [
+            jax.ShapeDtypeStruct((rows, units), jnp.bfloat16),
+            jax.ShapeDtypeStruct((rows, units), jnp.bfloat16),
+        ],
+        [pltpu.VMEM((width, units), jnp.bfloat16), pltpu.SemaphoreType.DMA((units // CHUNK, 2))],
+        2 * rows * width * units, 2 * units * (width + 3 * rows),
+    )(spot, normed, bias, own, got)
+
+
+def down_kernel(pos_ref, act_ref, own_ref, got_ref, middle_ref, bias_ref, out_ref):
+    pos = pos_ref[0]
+    half = own_ref.shape[1]
+    mine = pl.ds(pl.multiple_of(pos * half, 128), half)
+    theirs = pl.ds(pl.multiple_of((1 - pos) * half, 128), half)
+    total = _nt(own_ref[...], act_ref[:, mine]) + _nt(got_ref[...], act_ref[:, theirs])
+    out_ref[...] = (middle_ref[...] + total + bias_ref[...]).astype(out_ref.dtype)
+
+
+def mlp_down(spot, active, own, got, middle, bias):
+    width, rows = middle.shape
+    half = own.shape[1]
+    tile = width // 4
+    return pl.pallas_call(
+        down_kernel,
+        grid_spec=pltpu.PrefetchScalarGridSpec(
+            num_scalar_prefetch=1, grid=(width // tile,),
+            in_specs=[
+                pl.BlockSpec((rows, 2 * half), lambda i, p: (0, 0)),
+                pl.BlockSpec((tile, half), lambda i, p: (i, 0)),
+                pl.BlockSpec((tile, half), lambda i, p: (i, 0)),
+                pl.BlockSpec((tile, rows), lambda i, p: (i, 0)),
+                pl.BlockSpec((tile, 1), lambda i, p: (i, 0)),
+            ],
+            out_specs=pl.BlockSpec((tile, rows), lambda i, p: (i, 0)),
+        ),
+        out_shape=jax.ShapeDtypeStruct((width, rows), jnp.bfloat16),
+        compiler_params=pltpu.CompilerParams(vmem_limit_bytes=VMEM_LIMIT),
+        cost_estimate=pl.CostEstimate(flops=4 * rows * width * half, bytes_accessed=4 * half * (width + rows), transcendentals=0),
+        name="mlp_down",
+    )(spot, active, own, got, middle, bias)
+
+
+def back_kernel(pos_ref, grad_ref, slope_ref, down_own, down_got, up_own, up_got,
+                hidden_ref, normed_ref, sum_ref, down_full, up_full, sems):
+    pos = pos_ref[0]
+    half = down_own.shape[1]
+    units = up_own.shape[1]
+    mine = pl.ds(pl.multiple_of(pos * half, 128), half)
+    theirs = pl.ds(pl.multiple_of((1 - pos) * half, 128), half)
+    first = pltpu.make_async_copy(down_own, down_full.at[:, mine], sems.at[0])
+    second = pltpu.make_async_copy(down_got, down_full.at[:, theirs], sems.at[1])
+    first.start()
+    second.start()
+    rows_up = up_own.shape[0]
+    third = pltpu.make_async_copy(up_own, up_full.at[pl.ds(pl.multiple_of(pos * rows_up, 16), rows_up), :], sems.at[2])
+    fourth = pltpu.make_async_copy(up_got, up_full.at[pl.ds(pl.multiple_of((1 - pos) * rows_up, 16), rows_up), :], sems.at[3])
+    third.start()
+    fourth.start()
+    first.wait()
+    second.wait()
+    grad = grad_ref[...]
+    for j in range(units // CHUNK):
+        cols = pl.ds(j * CHUNK, CHUNK)
+        active = _nn(grad, down_full[:, cols])
+        hidden = (active * slope_ref[:, cols].astype(jnp.float32)).astype(jnp.bfloat16)
+        hidden_ref[:, cols] = hidden
+        sum_ref[:, cols] = jnp.sum(hidden.astype(jnp.float32), axis=0, keepdims=True)
+    third.wait()
+    fourth.wait()
+    hidden = hidden_ref[...]
+    for at in range(0, rows_up * 2, CHUNK):
+        size = min(CHUNK, rows_up * 2 - at)
+        normed_ref[:, at : at + size] = _nt(hidden, up_full[at : at + size, :])
+
+
+def mlp_back(spot, grad, slope, down_own, down_got, up_own, up_got):
+    rows, width = grad.shape
+    units = up_own.shape[1]
+    any_spec = pl.BlockSpec(memory_space=pl.ANY)
+    return _call(
+        back_kernel, "mlp_back", _vmem(2) + [any_spec] * 4,
+        [
+            jax.ShapeDtypeStruct((rows, units), jnp.bfloat16),
+            jax.ShapeDtypeStruct((rows, width), jnp.float32),
+            jax.ShapeDtypeStruct((1, units), jnp.float32),
+        ],
+        [
+            pltpu.VMEM((width, units), jnp.bfloat16),
+            pltpu.VMEM((width, units), jnp.bfloat16),
+            pltpu.SemaphoreType.DMA((4,)),
+        ],
+        4 * rows * width * units, 4 * units * (width + rows),
+    )(spot, grad, slope, down_own, down_got, up_own, up_got)
+
+
+def weight_kernel(pos_ref, left_own, left_sib, right_own, right_sib, give_ref, keep_ref, total_ref):
+    pos = pos_ref[0]
+    _, rows, tokens = left_own.shape
+    own = left_own[...].reshape(2 * rows, tokens)
+    sib = left_sib[...].reshape(2 * rows, tokens)
+    total = _nn(own, right_own[...]) + _nn(sib, right_sib[...])
+    total_ref[...] = total.astype(total_ref.dtype).reshape(total_ref.shape)
+    give_ref[...] = total_ref[1 - pos]
+    keep_ref[...] = total_ref[pos]
+
+
+def weight_grads(spot, left_own, left_sib, right_own, right_sib, tile_rows, tile_cols, name):
+    _, rows, tokens = left_own.shape
+    columns = right_own.shape[1]
+    left = pl.BlockSpec((2, tile_rows, tokens), lambda i, j, p: (0, i, 0))
+    right = pl.BlockSpec((tokens, tile_cols), lambda i, j, p: (0, j))
+    out = pl.BlockSpec((tile_rows, tile_cols), lambda i, j, p: (i, j))
+    return pl.pallas_call(
+        weight_kernel,
+        grid_spec=pltpu.PrefetchScalarGridSpec(
+            num_scalar_prefetch=1, grid=(rows // tile_rows, pl.cdiv(columns, tile_cols)),
+            in_specs=[left, left, right, right], out_specs=[out, out],
+            scratch_shapes=[pltpu.VMEM((2, tile_rows, tile_cols), jnp.bfloat16)],
+        ),
+        out_shape=[jax.ShapeDtypeStruct((rows, columns), jnp.bfloat16)] * 2,
+        compiler_params=pltpu.CompilerParams(vmem_limit_bytes=VMEM_LIMIT),
+        cost_estimate=pl.CostEstimate(flops=8 * rows * tokens * columns, bytes_accessed=4 * rows * columns + 4 * tokens * columns, transcendentals=0),
+        name=name,
+    )(spot, left_own, left_sib, right_own, right_sib)
+
+
+def turned_kernel(pos_ref, left_own, left_sib, right_own, right_sib, give_ref, keep_ref):
+    total = _nn(left_own[...], right_own[...]) + _nn(left_sib[...], right_sib[...])
+    total = total.astype(give_ref.dtype)
+
+    @pl.when(pl.program_id(0) == 0)
+    def _():
+        give_ref[...] = total
+
+    @pl.when(pl.program_id(0) == 1)
+    def _():
+        keep_ref[...] = total
+
+
+def turned_weight_grads(spot, left_own, left_sib, right_own, right_sib, tile_rows, name):
+    rows, tokens = left_own.shape
+    columns = right_own.shape[1] // 2
+    last = rows // tile_rows - 1
+    left = pl.BlockSpec((tile_rows, tokens), lambda i, j, p: (j, 0))
+    right = pl.BlockSpec((tokens, columns), lambda i, j, p: (0, jnp.where(i == 0, 1 - p[0], p[0])))
+    return pl.pallas_call(
+        turned_kernel,
+        grid_spec=pltpu.PrefetchScalarGridSpec(
+            num_scalar_prefetch=1, grid=(2, last + 1),
+            in_specs=[left, left, right, right],
+            out_specs=[
+                pl.BlockSpec((tile_rows, columns), lambda i, j, p: (jnp.where(i == 0, j, last), 0)),
+                pl.BlockSpec((tile_rows, columns), lambda i, j, p: (jnp.where(i == 0, 0, j), 0)),
+            ],
+        ),
+        out_shape=[jax.ShapeDtypeStruct((rows, columns), jnp.bfloat16)] * 2,
+        compiler_params=pltpu.CompilerParams(vmem_limit_bytes=VMEM_LIMIT),
+        cost_estimate=pl.CostEstimate(flops=8 * rows * tokens * columns, bytes_accessed=4 * rows * columns + 8 * tokens * columns, transcendentals=0),
+        name=name,
+    )(spot, left_own, left_sib, right_own, right_sib)
+
+
+def qkv_weight_kernel(pos_ref, left_own, left_sib, q_own, q_sib, k_own, k_sib, v_own, v_sib,
+                      give_ref, keep_ref, total_ref):
+    pos = pos_ref[0]
+    _, rows, length = left_own.shape
+    span, width = q_own.shape
+    mine = pl.ds(pl.multiple_of(pos * span, 128), span)
+
+    def rows_of(ref, cols):
+        return ref[:, :, cols].reshape(2 * rows, -1)
+
+    whole = pl.ds(0, length)
+    for at, cols, own, sib in ((0, mine, q_own, q_sib), (1, whole, k_own, k_sib), (2, whole, v_own, v_sib)):
+        total = _nn(rows_of(left_own, cols), own[...]) + _nn(rows_of(left_sib, cols), sib[...])
+        total_ref[...] = total.astype(total_ref.dtype).reshape(total_ref.shape)
+        give_ref[:, at * width : (at + 1) * width] = total_ref[1 - pos]
+        keep_ref[:, at * width : (at + 1) * width] = total_ref[pos]
+
+
+def qkv_weight_grads(spot, left_own, left_sib, *rights):
+    rows = left_own.shape[1]
+    length = left_own.shape[2]
+    width = rights[0].shape[1]
+    return _call(
+        qkv_weight_kernel, "qkv_weight_grads", _vmem(8),
+        [jax.ShapeDtypeStruct((rows, 3 * width), jnp.bfloat16)] * 2,
+        [pltpu.VMEM((2, rows, width), jnp.bfloat16)],
+        8 * rows * width * length * 5 // 2, 2 * (rows * width * 6 + 10 * length // 2 * width),
+    )(spot, left_own, left_sib, *rights)
+
+
+def input_kernel(pos_ref, wq_ref, wk_ref, wv_ref, gq_ref, gk_ref, gv_ref, mine_ref, theirs_ref):
+    pos = pos_ref[0]
+    span = gq_ref.shape[0]
+    mine = pl.ds(pl.multiple_of(pos * span, 16), span)
+    theirs = pl.ds(pl.multiple_of((1 - pos) * span, 16), span)
+    wk, wv = wk_ref[...], wv_ref[...]
+    theirs_ref[...] = (_nt(wk, gk_ref[theirs, :]) + _nt(wv, gv_ref[theirs, :])).astype(theirs_ref.dtype)
+    mine_ref[...] = _nt(wq_ref[...], gq_ref[...]) + _nt(wk, gk_ref[mine, :]) + _nt(wv, gv_ref[mine, :])
+
+
+def input_grads(spot, wq, wk, wv, gq, gk, gv):
+    span, width = gq.shape
+    return _call(
+        input_kernel, "input_grads", _vmem(6),
+        [
+            jax.ShapeDtypeStruct((width, span), jnp.float32),
+            jax.ShapeDtypeStruct((width, span), jnp.bfloat16),
+        ],
+        [], 10 * span * width * width, 2 * (3 * width * width + 8 * span * width),
+    )(spot, wq, wk, wv, gq, gk, gv)
+
+
+def tie(values, *earlier):
+    return lax.optimization_barrier((values, *earlier))[0]
+
+
+def row_sum(values):
+    return jnp.sum(values.astype(jnp.float32), axis=0)
+
+
+def pick(values, index, axis):
+    return lax.dynamic_index_in_dim(values, index, axis, keepdims=False)
+
+
+def plus(left, right):
+    return low(left.astype(jnp.float32) + right.astype(jnp.float32))
+
+
+def total_of(packed):
+    position = lax.axis_index("shard")
+    kept = pick(packed, position, 0) + cross(pick(packed, 1 - position, 0))
+    bit = 1
+    while bit < lax.axis_size("replica"):
+        kept = kept + swap(kept, bit)
+        bit *= 2
+    return kept
+
+
+def spread(weight, bits):
+    rows = weight.shape[0]
+    count = 2 ** len(bits)
+    size = -(-rows // (8 * count)) * 8
+    index = jnp.int32(0)
+    for bit in bits:
+        index = index * 2 + has_bit(bit).astype(jnp.int32)
+    piece = lax.dynamic_slice_in_dim(weight, jnp.minimum(index * size, rows - size), size, axis=0)
+    got = yield cross(piece), piece
+    for bit in bits[::-1]:
+        other = yield swap(got, bit), got
+        got = in_order(bit, got, other)
+    extra = count * size - rows
+    if extra:
+        got = jnp.concatenate([got[: (count - 1) * size], got[(count - 1) * size + extra :]], axis=0)
+    return got
+
+
+def reduced(keep, give, bits):
+    got = yield cross(give), give
+    values = plus(keep, got)
+    stack = []
+    for bit in bits[:-1]:
+        lower, upper = halves(values)
+        flag = has_bit(bit)
+        got = yield swap(choose(flag, lower, upper), bit), values
+        stack.append((bit, values.shape[0]))
+        values = plus(choose(flag, upper, lower), got)
+    got = yield swap(values, bits[-1]), values
+    values = plus(values, got)
+    for bit, rows in stack[::-1]:
+        got = yield swap(values, bit), values
+        both = in_order(bit, values, got)
+        size = values.shape[0]
+        if 2 * size != rows:
+            both = jnp.concatenate([both[: rows - size], both[size:]], axis=0)
+        values = both
+    got = yield swap(values, CORE_BIT), values
+    return in_order(CORE_BIT, values, got).astype(jnp.float32)
+
+
+class Steps:
+    def __init__(self, chain):
+        self.chain = chain
+        self.got, self.latest = next(chain)
+
+    def step(self, *gates):
+        got = tie(self.got, *gates) if gates else self.got
+        self.got, self.latest = self.chain.send(got)
+
+    def finish(self):
+        while True:
+            try:
+                self.step()
+            except StopIteration as end:
+                return end.value
+
+
+def centred_down(values):
+    off = values - jnp.mean(values, axis=0, keepdims=True)
+    rstd = lax.rsqrt(jnp.mean(off * off, axis=0, keepdims=True) + EPSILON)
+    return off * rstd, rstd
+
+
+def on_device_pair(
+    tokens, qkv_weight, out_weight, up_weight, down_weight, attn_gain, attn_shift, query_bias,
+    value_bias, out_bias, mlp_gain, mlp_shift, up_bias, down_bias, cotangent,
+):
+    _, span, width = tokens.shape
+    position = lax.axis_index("shard")
+    spot = position.astype(jnp.int32).reshape(1)
+    core = lax.axis_index("replica") & CORE_BIT
+    bits = all_bits()
+    fast_bits = [CORE_BIT] + bits[:2]
+    turned_bits = [CORE_BIT] + bits[:2][::-1]
+    first = position == 0
+
+    own_turned = tokens.reshape(span, width).T
+    down_turned = down_weight.T
+    singles = (attn_gain, attn_shift, query_bias, value_bias, out_bias, mlp_gain, mlp_shift, down_bias)
+    flat_vectors = jnp.concatenate(
+        [item.reshape(1, -1) for item in singles] + [up_bias.reshape(-1, singles[0].shape[0])], axis=0
+    )
+    way_qkv = Steps(spread(qkv_weight, fast_bits))
+    other_vectors = cross(flat_vectors)
+    way_out = Steps(spread(out_weight, turned_bits))
+    other_turned = cross(tie(own_turned, way_qkv.got))
+    way_qkv.step()
+    way_out.step()
+    way_up = Steps(spread(tie(up_weight, other_turned), turned_bits))
+    way_down = Steps(spread(tie(down_turned, way_up.got), turned_bits))
+    grad_turned = cotangent.reshape(span, width).T
+    grad_out = grad_turned.T
+    grad_halves = grad_turned.reshape(2, width // 2, span)
+    grad_left = pick(grad_halves, core, 0), swap(pick(grad_halves, 1 - core, 0), CORE_BIT)
+
+    lower = choose(first, flat_vectors, other_vectors).astype(jnp.float32)
+    upper = choose(first, other_vectors, flat_vectors).astype(jnp.float32)
+    both = jnp.concatenate([lower, upper], axis=1)
+    (gain_first, shift_first, bias_query, bias_value, bias_out, gain_second, shift_second,
+     bias_down) = (both[i] for i in range(8))
+    bias_up = jnp.concatenate([lower[8:].reshape(1, -1), upper[8:].reshape(1, -1)], axis=1)
+
+    all_turned = jnp.concatenate(
+        [choose(first, own_turned, other_turned), choose(first, other_turned, own_turned)], axis=1
+    )
+    unit_all, _ = centred_down(all_turned.astype(jnp.float32))
+    normed_turned = low(unit_all * gain_first[:, None] + shift_first[:, None])
+    normed_all = normed_turned.T
+    normed = lax.dynamic_slice_in_dim(normed_all, position * span, span, axis=0)
+
+    def for_cores(turned):
+        parts = turned.reshape(2, 2, turned.shape[0] // 4, turned.shape[1])
+        return pick(parts, core, 1), swap(pick(parts, 1 - core, 1), CORE_BIT)
+
+    way_up.step(normed_all)
+    full_qkv = both_halves(qkv_weight, way_qkv.finish())
+    full_q, full_k, full_v = (full_qkv[:, i * width : (i + 1) * width] for i in range(3))
+    full_out = both_halves(out_weight, way_out.finish())
+    normed_all = tie(normed_all, way_up.latest)
+    keys = low(dot(normed_all, full_k))
+    values = low(dot(normed_all, full_v) + bias_value)
+    queries = low(low(dot(normed, full_q) + bias_query) * SCALING)
+    way_up.step(keys, values, queries)
+    way_down.step(keys, values, queries)
+    queries = tie(queries, way_up.latest, way_down.latest, full_out)
+    context, context_t, lse = attention_forward(spot, queries, keys, values, 1, span)
+    way_up.step(context)
+    way_down.step(context)
+    context = tie(context, way_up.latest, way_down.latest)
+    normed_left = for_cores(normed_turned)
+    flat = own_turned.T.astype(jnp.float32)
+    middle = flat + dot(context, full_out) + bias_out
+    unit_second, rstd_second = centred(middle)
+    normed_two = low(unit_second * gain_second + shift_second)
+    part_up = way_up.finish()
+    active, slope = mlp_up(spot, normed_two, bias_up, up_weight, part_up)
+    active_sib = swap(active, CORE_BIT)
+    way_down.step(active)
+    part_down = way_down.finish()
+    block_out = mlp_down(spot, active, down_turned, part_down, middle.T, bias_down.reshape(-1, 1))
+
+    give, keep_down = turned_weight_grads(
+        spot, *grad_left, active, tie(active_sib, block_out), width // 4, "down_grads"
+    )
+    sum_down = Steps(reduced(keep_down, give, bits))
+
+    grad_hidden, grad_normed_two, sum_hidden = mlp_back(
+        spot, tie(grad_out, give), slope, down_turned, part_down, up_weight, part_up
+    )
+    hidden_sib = swap(grad_hidden, CORE_BIT)
+    grad_middle = norm_pull(grad_normed_two, unit_second, rstd_second, gain_second)
+    grad_middle = grad_middle + grad_out.astype(jnp.float32)
+    grad_branch = low(grad_middle)
+    branch_sib = swap(grad_branch, CORE_BIT)
+    grad_context = low(dot_nt(grad_branch, full_out))
+    two_left = for_cores(normed_two.T)
+    give, keep_up = weight_grads(
+        spot, *two_left, grad_hidden, hidden_sib, two_left[0].shape[1], 2 * CHUNK, "up_grads"
+    )
+    sum_up = Steps(reduced(keep_up, give, bits))
+    context_left = for_cores(context_t)
+    give_out, keep_out = weight_grads(
+        spot, *context_left, grad_branch, branch_sib, context_left[0].shape[1], width, "out_grads"
+    )
+    sum_down.step(give, give_out, grad_context)
+    grad_context = tie(grad_context, give, give_out, sum_down.latest)
+
+    grad_q, grad_k, grad_v = attention_backward(
+        spot, queries, keys, values, grad_context, context, lse, 1, span
+    )
+    sum_down.step(grad_q)
+    rights = []
+    for part in (grad_q, grad_k, grad_v):
+        rights += [part, swap(part, CORE_BIT)]
+    rights[0] = tie(grad_q, sum_down.latest)
+    give, keep_qkv = qkv_weight_grads(spot, *normed_left, *rights)
+    sum_down.step(give)
+    sum_up.step(give)
+    sum_qkv = Steps(reduced(keep_qkv, give, bits))
+
+    mine, theirs = input_grads(
+        spot, full_q, full_k, full_v, tie(grad_q, give, sum_down.latest, sum_up.latest), grad_k, grad_v
+    )
+    sum_out = Steps(reduced(keep_out, tie(give_out, mine), bits))
+    grad_normed = mine + cross(theirs).astype(jnp.float32)
+    unit_first, rstd_first = centred_down(own_turned.astype(jnp.float32))
+    scaled = grad_normed * gain_first[:, None]
+    pulled = rstd_first * (
+        scaled - jnp.mean(scaled, axis=0, keepdims=True)
+        - unit_first * jnp.mean(scaled * unit_first, axis=0, keepdims=True)
+    )
+    grad_tokens = low(pulled + grad_middle.T)
+
+    sums = (
+        jnp.sum(grad_normed * unit_first, axis=1),
+        jnp.sum(grad_normed, axis=1),
+        row_sum(grad_q),
+        row_sum(grad_v),
+        row_sum(grad_branch),
+        row_sum(grad_normed_two * unit_second),
+        row_sum(grad_normed_two),
+        sum_hidden.reshape(-1),
+        row_sum(grad_out),
+    )
+    packed = total_of(jnp.concatenate([item.reshape(2, -1) for item in sums], axis=1))
+    outs, at = [], 0
+    for item in sums:
+        size = item.shape[0] // 2
+        outs.append(packed[at : at + size])
+        at += size
+
+    return (
+        block_out.T.reshape(1, span, width),
+        grad_tokens.T.reshape(1, span, width),
+        sum_qkv.finish(), sum_out.finish(), sum_up.finish(), sum_down.finish().T,
+        *outs,
+    )
+
+
+def on_device_general(
     tokens, qkv_weight, out_weight, up_weight, down_weight, attn_gain, attn_shift, query_bias,
     value_bias, out_bias, mlp_gain, mlp_shift, up_bias, down_bias, cotangent,
 ):
     seqs, span, width = tokens.shape
     rows = seqs * span
     shards = lax.axis_size("shard")
-    replicas = lax.axis_size("replica")
     position = lax.axis_index("shard")
     core = lax.axis_index("replica") & CORE_BIT
     length = span * shards
-    hidden_units = up_weight.shape[1]
-    pairwise = shards == 2
-    bits = []
-    bit = 2
-    while bit < replicas:
-        bits.append(bit)
-        bit *= 2
-    fast_bits = [CORE_BIT] + bits[:2]
+    bits = all_bits()
 
     shards_of = (attn_gain, attn_shift, query_bias, value_bias, out_bias, mlp_gain, mlp_shift,
                  up_bias, down_bias)
@@ -397,30 +899,11 @@
     (gain_first, shift_first, bias_query, bias_value, bias_out, gain_second, shift_second, bias_up,
      bias_down) = vectors
 
-    if pairwise:
-        order = (0, 1)
-        own_tokens = tokens.reshape(rows, width)
-        got_qkv = spread_start(qkv_weight, fast_bits)
-        got_out = spread_start(after(out_weight, got_qkv), fast_bits)
-        other = cross(after(own_tokens, got_out))
-        got_up = spread_start(after(up_weight, other), fast_bits)
-        got_down = spread_start(after(down_weight, got_up), fast_bits)
-        full_qkv = spread_end(qkv_weight, got_qkv, fast_bits)
-        full_out = spread_end(out_weight, got_out, fast_bits)
-        full_up = spread_end(up_weight, got_up, fast_bits)
-        full_down = spread_end(down_weight, got_down, fast_bits)
-        first = position == 0
-        pair = tokens.shape[0], 1, span, width
-        own_part, other_part = own_tokens.reshape(pair), other.reshape(pair)
-        all_tokens = jnp.concatenate(
-            [choose(first, own_part, other_part), choose(first, other_part, own_part)], axis=1
-        ).reshape(seqs * length, width)
-    else:
-        full_qkv, full_out, full_up, full_down = [
-            lax.all_gather(item, "shard", axis=0, tiled=True)
-            for item in (qkv_weight, out_weight, up_weight, down_weight)
-        ]
-        all_tokens = lax.all_gather(tokens, "shard", axis=1, tiled=True).reshape(-1, width)
+    full_qkv, full_out, full_up, full_down = [
+        lax.all_gather(item, "shard", axis=0, tiled=True)
+        for item in (qkv_weight, out_weight, up_weight, down_weight)
+    ]
+    all_tokens = lax.all_gather(tokens, "shard", axis=1, tiled=True).reshape(-1, width)
 
     def own_rows(values):
         per_seq = values.reshape(seqs, length, values.shape[-1])
@@ -439,7 +922,7 @@
     keys = low(dot(normed_all, full_k))
     values = low(dot(normed_all, full_v) + bias_value)
     spot = position.astype(jnp.int32).reshape(1)
-    context, lse = attention_forward(spot, queries, keys, values, seqs, span)
+    context, context_t, lse = attention_forward(spot, queries, keys, values, seqs, span)
     context_sib = swap(context, CORE_BIT)
     middle = flat + dot(context, full_out) + bias_out
     unit_second, rstd_second = centred(middle)
@@ -450,10 +933,6 @@
     slope = low(slope)
 
     def split_rows(lhs, rhs):
-        if pairwise:
-            give = dot_tn(columns_of(lhs, 1, 1 - position), rhs)
-            keep = dot_tn(columns_of(lhs, 1, position), rhs)
-            return reduce_start(low(give), low(keep))
         return lax.psum_scatter(low(dot_tn(lhs, rhs)), "shard", scatter_dimension=0, tiled=True)
 
     grouped = active.reshape(rows, shards, 2, -1)
@@ -505,23 +984,13 @@
         )
         for part in (grad_q, grad_k, grad_v)
     )
-    if pairwise:
-        def three(index):
-            left_own = columns_of(own_both, 1, index)
-            left_all = columns_of(normed_both, 1, index)
-            return low(jnp.concatenate(
-                [dot_tn(left_own, half_q), dot_tn(left_all, half_k), dot_tn(left_all, half_v)],
-                axis=1,
-            ))
-        sum_qkv = reduce_start(three(1 - position), three(position))
-    else:
-        sum_qkv = lax.psum_scatter(
-            low(jnp.concatenate(
-                [dot_tn(own_both, half_q), dot_tn(normed_both, half_k), dot_tn(normed_both, half_v)],
-                axis=1,
-            )),
-            "shard", scatter_dimension=0, tiled=True,
-        )
+    sum_qkv = lax.psum_scatter(
+        low(jnp.concatenate(
+            [dot_tn(own_both, half_q), dot_tn(normed_both, half_k), dot_tn(normed_both, half_v)],
+            axis=1,
+        )),
+        "shard", scatter_dimension=0, tiled=True,
+    )
     sum_qkv = reduce_rest(sum_qkv, bits)
     left, right = join_columns(sum_qkv)
     sum_qkv = jnp.concatenate(
@@ -530,15 +999,9 @@
 
     from_query = dot_nt(grad_q, full_q)
     from_rest = dot_nt(grad_k, full_k) + dot_nt(grad_v, full_v)
-    if pairwise:
-        halves_of = from_rest.reshape(seqs, 2, span, width)
-        mine = choose(position == 0, halves_of[:, 0], halves_of[:, 1]).reshape(rows, width)
-        theirs = choose(position == 0, halves_of[:, 1], halves_of[:, 0]).reshape(rows, width)
-        grad_normed = from_query + mine + cross(low(theirs)).astype(jnp.float32)
-    else:
-        grad_normed = from_query + lax.psum_scatter(
-            from_rest.reshape(seqs, length, width), "shard", scatter_dimension=1, tiled=True
-        ).reshape(rows, width)
+    grad_normed = from_query + lax.psum_scatter(
+        from_rest.reshape(seqs, length, width), "shard", scatter_dimension=1, tiled=True
+    ).reshape(rows, width)
     unit_first, rstd_first = own_rows(unit_all), own_rows(rstd_all)
     grad_tokens = low(norm_pull(grad_normed, unit_first, rstd_first, gain_first) + grad_middle)
 
@@ -575,6 +1038,12 @@
     )
 
 
+def on_device(tokens, *rest):
+    if lax.axis_size("shard") == 2 and lax.axis_size("replica") >= 8 and tokens.shape[0] == 1:
+        return on_device_pair(tokens, *rest)
+    return on_device_general(tokens, *rest)
+
+
 def solution(mesh):
     vector, matrix, rows = P("shard"), P("shard", None), P("replica", "shard", None)
     return jax.shard_map(

time: 832 us -> 645 us (0.78)
  matrix products: 135 us -> 17.3 us
  Pallas kernels: 69.1 us -> 177 us
  local copies, waits for them, and re-layouts: 148 us -> 64.9 us
  blocking collectives: 45.2 us -> 0 us
  other arithmetic: 121 us -> 97.7 us
  waiting for transfers between devices: 215 us -> 200 us
    pallas_call x0 -> x8, Pallas kernels: none -> 107 us  [the longest x1 22 us: mlp_back(): _call(back_kernel, 'mlp_back', _vmem(2) + [any_spec] * 4, [jax.ShapeDtype...]
    dot_general x12 -> x0, matrix products: 46.6 us -> none  [dot_tn(): lax.dot_general(left, right, (((0,), (0,)), ((), ())), preferred_element_...]
    dot_general x6 -> x1, matrix products: 49.9 us -> 4.99 us  [dot_nt(): lax.dot_general(left, right, (((1,), (1,)), ((), ())), preferred_element_...]
    psum x1 -> x0, blocking collectives: 41.9 us -> none  [on_device(): packed = lax.psum(packed, ('replica', 'shard'))]
    select_n x42 -> x38, other arithmetic: 55.8 us -> 23.7 us  [choose(): return jnp.where(flag, left, right)]
    unnamed x203 -> x130, local copies, waits for them, and re-layouts: 35.4 us -> 5.69 us
    dot_general x6 -> x4, matrix products: 38.8 us -> 12.3 us  [dot(): return jnp.dot(left, right, preferred_element_type=jnp.float32)]
    concatenate x5 -> x2, local copies, waits for them, and re-layouts: 21 us -> 0.23 us  [the longest x1 0.16 us: on_device_pair(): jnp.concatenate([item.reshape(2, -1) for item in sums], axis=1)]
  transfers between devices with their start and end apart: 56 -> 62, of which waited for: 19 -> 29; matrix products, arithmetic and copies ran while one was open for 47% -> 24% of each run, Pallas kernels for 8% -> 22%
where the time goes in v2:
time: 645 us; the launch traced here: 635 us
  waiting for transfers between devices  200 us (31%)
  Pallas kernels  177 us (27%)
  other arithmetic  97.7 us (15%)
  starting transfers between devices  76.2 us (12%)
  local copies, waits for them, and re-layouts  64.9 us (10%)
  matrix products  17.3 us (3%)
    ppermute x50, waiting for transfers between devices, swap(): return lax.ppermute(values, 'replica', [(i, i ^ bit) for i in range(size)])  118 us
    ppermute x12, waiting for transfers between devices, cross(): return lax.ppermute(values, 'shard', [(0, 1), (1, 0)])  82 us
    ppermute x50, starting transfers between devices, swap(): return lax.ppermute(values, 'replica', [(i, i ^ bit) for i in range(size)])  69.2 us
    pallas_call x1, Pallas kernels, attention_backward(): pl.pallas_call(functools.partial(backward_kernel, span=span, width=width)...  37.2 us
    pallas_call x1, Pallas kernels, attention_forward(): pl.pallas_call(functools.partial(forward_kernel, span=span, width=width),...  32.2 us
    select_n x38, other arithmetic, choose(): return jnp.where(flag, left, right)  23.7 us
    pallas_call x1, Pallas kernels, mlp_back(): _call(back_kernel, 'mlp_back', _vmem(2) + [any_spec] * 4, [jax.ShapeDtype...  22 us
    convert_element_type x19, other arithmetic, low(): return values.astype(jnp.bfloat16)  20 us
  transfers between devices with their start and end apart: 62, of which 29 were waited for; matrix products, arithmetic and copies ran while one was open for 24% of the time, Pallas kernels for 22%

profile of v2, /device:TPU:27, one launch (start us, length us, event | category | flops | bytes accessed | tf_op | source)
XLA Modules:
  0.0 634.9 jit_solution(230374465808836214)
XLA Ops:
  15.3 8.5 %collective-permute-done = bf16[72,3264]{1,0:T(8,128)(2,1)S(1)} collective-permute-done((bf16[72,3264]{1,0:T(8,128)(2,1)S(1)}, bf16[72,3264]{1,0:T(8,128)(2,1)S(1)}, u32[]{:S(2)}, u32[]{:S(2)}) %collective-permute-start) | collective-permute-done | bytes 470048 | tf_op jit(solution)/shard_map/ppermute | solution.py:291
  26.3 8.4 %collective-permute-done.3 = bf16[72,3264]{1,0:T(8,128)(2,1)S(1)} collective-permute-done((bf16[72,3264]{1,0:T(8,128)(2,1)S(1)}, bf16[72,3264]{1,0:T(8,128)(2,1)S(1)}, u32[]{:S(2)}, u32[]{:S(2)}) %collective-permute-start.3) | collective-permute-done | bytes 470048 | tf_op jit(solution)/shard_map/ppermute | solution.py:287
  36.1 5.7 collective-permute-done.11
  44.6 4.8 collective-permute-done.1
  53.5 5.6 collective-permute-start.5
  69.1 3.2 pad_maximum_fusion.1
  74.6 4.8 add_convert_fusion.2.v_ref
  79.4 3.8 convolution_convert_fusion.k_ref
  85.9 32.2 %attention_forward.1 = (bf16[512,1088]{1,0:T(8,128)(2,1)S(1)}, bf16[1088,512]{1,0:T(8,128)(2,1)S(1)}, f32[9,2,512]{2,1,0:T(2,128)S(1)}) custom-call(s32[1]{0:T(128)} %bitcast.pos_ref, bf16[512,1088]{1,0:T(8,128)(2,1)S(1)} %fusion.14.q_ref, bf16[1024,1088]{1,0:T(8,128)(2,1)S(1)} %convolution_convert_fusion.k_ref, bf16[1024,1088]{1,0:T(8,128)(2,1)} %add_convert_fusion.2.v_ref), custom_call_target="tpu_custom_call" | custom-call | flops 4563402752 | bytes 8912896 | tf_op jit(solution)/shard_map/attention_forward/pallas_call | solution.py:181
  121.0 4.3 collective-permute-start.15
  140.4 17.4 %mlp_up.1 = (bf16[512,4352]{1,0:T(8,128)(2,1)}, bf16[512,4352]{1,0:T(8,128)(2,1)}) custom-call(s32[1]{0:T(128)} %bitcast.pos_ref, bf16[512,1088]{1,0:T(8,128)(2,1)} %copy.58.nt_ref, f32[1,4352]{1,0:T(1,128)} %pad_maximum_fusion.20.bias_ref, bf16[544,4352]{1,0:T(8,128)(2,1)} %up_own.1, bf16[544,4352]{1,0:T(8,128)(2,1)} %fusion.5.got_ref.up_got), custom_call_target="tpu_custom_call" | custom-call | flops 4848615424 | bytes 22839296 | tf_op jit(solution)/shard_map/mlp_up/pallas_call | solution.py:416
  172.5 11.3 %mlp_down.1 = bf16[1088,512]{1,0:T(8,128)(2,1)} custom-call(s32[1]{0:T(128)} %bitcast.pos_ref, bf16[512,4352]{1,0:T(8,128)(2,1)} %get-tuple-element.70.act_ref.right_own, bf16[1088,2176]{1,0:T(8,128)(2,1)} %bitcast.86, bf16[1088,2176]{1,0:T(8,128)(2,1)} %pad_maximum_fusion.got_ref.down_got, f32[1088,512]{1,0:T(8,128)} %bitcast.76, f32[1088,1]{1,0:T(8,128)} %copy.59.bias_ref), custom_call_target="tpu_custom_call" | custom-call | flops 4848615424 | bytes 13926400 | tf_op jit(solution)/shard_map/mlp_down/pallas_call | solution.py:440
  183.8 11.8 %down_grads.1 = (bf16[544,2176]{1,0:T(8,128)(2,1)}, bf16[544,2176]{1,0:T(8,128)(2,1)}) custom-call(s32[1]{0:T(128)} %bitcast.pos_ref, bf16[544,512]{1,0:T(8,128)(2,1)} %get-tuple-element.170.left_own, bf16[544,512]{1,0:T(8,128)(2,1)} %collective-permute-done.18.left_sib, bf16[512,4352]{1,0:T(8,128)(2,1)} %get-tuple-element.70.act_ref.right_own, ...), custom_call_target="tpu_custom_call" | custom-call | flops 4848615424 | bytes 13647872 | tf_op jit(solution)/shard_map/down_grads/pallas_call | solution.py:563
  198.0 22.0 %mlp_back.1 = (bf16[512,4352]{1,0:T(8,128)(2,1)}, f32[512,1088]{1,0:T(8,128)}, f32[1,4352]{1,0:T(1,128)}) custom-call(s32[1]{0:T(128)} %bitcast.pos_ref, bf16[512,1088]{1,0:T(8,128)(2,1)} %copy.60.grad_ref, bf16[512,4352]{1,0:T(8,128)(2,1)} %get-tuple-element.75.slope_ref, bf16[1088,2176]{1,0:T(8,128)(2,1)} %bitcast.87, ...), custom_call_target="tpu_custom_call" | custom-call | flops 9697230848 | bytes 27852800 | tf_op jit(solution)/shard_map/mlp_back/pallas_call | solution.py:497
  221.8 3.5 copy.61
  225.3 3.9 multiply_reduce_fusion
  229.2 3.9 convert_reduce_fusion.5
  240.6 5.0 convolution_convert_fusion.1.g_ref
  248.0 4.7 out_grads.1
  253.5 11.8 %up_grads.1 = (bf16[272,4352]{1,0:T(8,128)(2,1)}, bf16[272,4352]{1,0:T(8,128)(2,1)}) custom-call(s32[1]{0:T(128)} %bitcast.pos_ref, bf16[2,272,512]{2,1,0:T(8,128)(2,1)} %get-tuple-element.168.left_own, bf16[2,272,512]{2,1,0:T(8,128)(2,1)} %copy-done.64, bf16[512,4352]{1,0:T(8,128)(2,1)} %get-tuple-element.77.right_own, ...), custom_call_target="tpu_custom_call" | custom-call | flops 4848615424 | bytes 13647872 | tf_op jit(solution)/shard_map/up_grads/pallas_call | solution.py:530
  265.3 9.5 %collective-permute-done.24 = bf16[544,2176]{1,0:T(8,128)(2,1)} collective-permute-done((bf16[544,2176]{1,0:T(8,128)(2,1)}, bf16[544,2176]{1,0:T(8,128)(2,1)}, u32[]{:S(2)}, u32[]{:S(2)}) %collective-permute-start.24) | collective-permute-done | bytes 2367520 | tf_op jit(solution)/shard_map/ppermute | solution.py:291
  280.2 37.2 %attention_backward.1 = (bf16[512,1088]{1,0:T(8,128)(2,1)S(1)}, bf16[1024,1088]{1,0:T(8,128)(2,1)}, bf16[1024,1088]{1,0:T(8,128)(2,1)}) custom-call(s32[1]{0:T(128)} %bitcast.pos_ref, bf16[512,1088]{1,0:T(8,128)(2,1)S(1)} %fusion.14.q_ref, bf16[1024,1088]{1,0:T(8,128)(2,1)} %copy-done.2, bf16[1024,1088]{1,0:T(8,128)(2,1)} %add_convert_fusion.2.v_ref, ...), custom_call_target="tpu_custom_call" | custom-call | flops 11408506880 | bytes 13369344 | tf_op jit(solution)/shard_map/attention_backward/pallas_call | solution.py:211
  317.4 4.7 copy.68
  322.1 4.4 copy.69
  346.3 4.2 copy.72.v_sib
  350.5 4.3 copy.71.k_sib
  354.8 14.4 %qkv_weight_grads.1 = (bf16[272,3264]{1,0:T(8,128)(2,1)}, bf16[272,3264]{1,0:T(8,128)(2,1)}) custom-call(s32[1]{0:T(128)} %bitcast.pos_ref, bf16[2,272,1024]{2,1,0:T(8,128)(2,1)} %get-tuple-element.147.left_own, bf16[2,272,1024]{2,1,0:T(8,128)(2,1)} %collective-permute-done.25.left_sib, bf16[512,1088]{1,0:T(8,128)(2,1)} %copy-done, ...), custom_call_target="tpu_custom_call" | custom-call | flops 6060769280 | bytes 14692352 | tf_op jit(solution)/shard_map/qkv_weight_grads/pallas_call | solution.py:602
  372.1 18.9 %collective-permute-done.31 = bf16[272,4352]{1,0:T(8,128)(2,1)} collective-permute-done((bf16[272,4352]{1,0:T(8,128)(2,1)}, bf16[272,4352]{1,0:T(8,128)(2,1)}, u32[]{:S(2)}, u32[]{:S(2)}) %collective-permute-start.31) | collective-permute-done | bytes 2367520 | tf_op jit(solution)/shard_map/ppermute | solution.py:291
  390.9 3.6 add_convert_fusion
  394.6 13.7 %input_grads.1 = (f32[1088,512]{1,0:T(8,128)}, bf16[1088,512]{1,0:T(8,128)(2,1)}) custom-call(s32[1]{0:T(128)} %bitcast.pos_ref, bf16[1088,1088]{1,0:T(8,128)(2,1)} %copy-done.36, bf16[1088,1088]{1,0:T(8,128)(2,1)} %copy-done.37, bf16[1088,1088]{1,0:T(8,128)(2,1)} %copy-done.35, bf16[512,1088]{1,0:T(8,128)(2,1)} %copy-done, ...), custom_call_target="tpu_custom_call" | custom-call | flops 6060769280 | bytes 16015360 | tf_op jit(solution)/shard_map/input_grads/pallas_call | solution.py:622
  413.2 29.9 %collective-permute-done.40 = bf16[272,1088]{1,0:T(8,128)(2,1)S(1)} collective-permute-done((bf16[272,1088]{1,0:T(8,128)(2,1)S(1)}, bf16[272,1088]{1,0:T(8,128)(2,1)S(1)}, u32[]{:S(2)}, u32[]{:S(2)}) %collective-permute-start.40) | collective-permute-done | bytes 591904 | tf_op jit(solution)/shard_map/ppermute | solution.py:291
  444.5 6.5 %collective-permute-done.41 = bf16[136,1088]{1,0:T(8,128)(2,1)S(1)} collective-permute-done((bf16[136,1088]{1,0:T(8,128)(2,1)S(1)}, bf16[136,1088]{1,0:T(8,128)(2,1)S(1)}, u32[]{:S(2)}, u32[]{:S(2)}) %collective-permute-start.41) | collective-permute-done | bytes 295968 | tf_op jit(solution)/shard_map/ppermute | solution.py:287
  451.6 6.0 collective-permute-done.54
  462.0 5.1 collective-permute-done.32
  474.5 4.7 fusion.32
  487.9 6.3 collective-permute-done.61
  495.6 3.6 collective-permute-done.44
  505.3 10.2 %collective-permute-start.46 = (bf16[272,1088]{1,0:T(8,128)(2,1)S(1)}, bf16[272,1088]{1,0:T(8,128)(2,1)S(1)}, u32[]{:S(2)}, u32[]{:S(2)}) collective-permute-start(bf16[272,1088]{1,0:T(8,128)(2,1)S(1)} %pad_maximum_fusion.17), channel_id=1, source_target_pairs={{0,2},{2,0},{4,6},{6,4},{8,10},{10,8},{12,14},{14,12},{16,18},{18,... | collective-permute-start | bytes 1775624 | tf_op jit(solution)/shard_map/ppermute | solution.py:287
  523.0 22.9 %collective-permute-done.49 = bf16[72,4352]{1,0:T(8,128)(2,1)S(1)} collective-permute-done((bf16[72,4352]{1,0:T(8,128)(2,1)S(1)}, bf16[72,4352]{1,0:T(8,128)(2,1)S(1)}, u32[]{:S(2)}, u32[]{:S(2)}) %collective-permute-start.49) | collective-permute-done | bytes 626720 | tf_op jit(solution)/shard_map/ppermute | solution.py:287
  547.5 21.1 %collective-permute-done.50 = bf16[72,4352]{1,0:T(8,128)(2,1)S(1)} collective-permute-done((bf16[72,4352]{1,0:T(8,128)(2,1)S(1)}, bf16[72,4352]{1,0:T(8,128)(2,1)S(1)}, u32[]{:S(2)}, u32[]{:S(2)}) %collective-permute-start.50) | collective-permute-done | bytes 626720 | tf_op jit(solution)/shard_map/ppermute | solution.py:287
  572.5 9.9 %collective-permute-done.37 = bf16[72,3264]{1,0:T(8,128)(2,1)S(1)} collective-permute-done((bf16[72,3264]{1,0:T(8,128)(2,1)S(1)}, bf16[72,3264]{1,0:T(8,128)(2,1)S(1)}, u32[]{:S(2)}, u32[]{:S(2)}) %collective-permute-start.37) | collective-permute-done | bytes 470048 | tf_op jit(solution)/shard_map/ppermute | solution.py:287
  583.2 10.5 %collective-permute-done.51 = bf16[136,4352]{1,0:T(8,128)(2,1)S(1)} collective-permute-done((bf16[136,4352]{1,0:T(8,128)(2,1)S(1)}, bf16[136,4352]{1,0:T(8,128)(2,1)S(1)}, u32[]{:S(2)}, u32[]{:S(2)}) %collective-permute-start.51) | collective-permute-done | bytes 1183776 | tf_op jit(solution)/shard_map/ppermute | solution.py:287
  594.4 12.2 %collective-permute-start.52 = (bf16[272,4352]{1,0:T(8,128)(2,1)S(1)}, bf16[272,4352]{1,0:T(8,128)(2,1)S(1)}, u32[]{:S(2)}, u32[]{:S(2)}) collective-permute-start(bf16[272,4352]{1,0:T(8,128)(2,1)S(1)} %pad_maximum_fusion.5), channel_id=1, source_target_pairs={{0,2},{2,0},{4,6},{6,4},{8,10},{10,8},{12,14},{14,12},{16,18},{18,... | collective-permute-start | bytes 7102472 | tf_op jit(solution)/shard_map/ppermute | solution.py:287
  606.5 6.6 %collective-permute-done.38 = bf16[136,3264]{1,0:T(8,128)(2,1)S(1)} collective-permute-done((bf16[136,3264]{1,0:T(8,128)(2,1)S(1)}, bf16[136,3264]{1,0:T(8,128)(2,1)S(1)}, u32[]{:S(2)}, u32[]{:S(2)}) %collective-permute-start.38) | collective-permute-done | bytes 887840 | tf_op jit(solution)/shard_map/ppermute | solution.py:287
  613.6 6.3 collective-permute-start.39
  620.9 4.4 convert_bitcast_fusion
  625.9 3.5 maximum_convert_fusion.1
  630.3 4.4 maximum_convert_fusion
  (383 shorter events, 167.1 us)
Async XLA Ops:
  10.8 13.0 %collective-permute-start = (bf16[72,3264]{1,0:T(8,128)(2,1)S(1)}, bf16[72,3264]{1,0:T(8,128)(2,1)S(1)}, u32[]{:S(2)}, u32[]{:S(2)}) collective-permute-start(bf16[72,3264]{1,0:T(8,128)(2,1)S(1)} %constant_dynamic-slice_fusion.3), channel_id=1, source_target_pairs={{0,1},{1,0},{2,3},{3,2},{4,5},{5,4},{6,7},{7,6},{8,9},{9,8},{10,11... | collective-permute-start | bytes 1410056 | tf_op jit(solution)/shard_map/ppermute | solution.py:291
  24.1 17.7 %collective-permute-start.11 = (bf16[144,1088]{1,0:T(8,128)(2,1)S(1)}, bf16[144,1088]{1,0:T(8,128)(2,1)S(1)}, u32[]{:S(2)}, u32[]{:S(2)}) collective-permute-start(bf16[144,1088]{1,0:T(8,128)(2,1)S(1)} %pad_maximum_fusion.18), channel_id=1, source_target_pairs={{0,8},{2,10},{4,12},{6,14},{8,0},{10,2},{12,4},{14,6},{16,24},{18,... | collective-permute-start | bytes 940040 | tf_op jit(solution)/shard_map/ppermute | solution.py:287
  25.5 23.9 %collective-permute-start.1 = (bf16[1088,512]{1,0:T(8,128)(2,1)S(1)}, bf16[1088,512]{1,0:T(8,128)(2,1)S(1)}, u32[]{:S(2)}, u32[]{:S(2)}) collective-permute-start(bf16[1088,512]{1,0:T(8,128)(2,1)S(1)} %bitcast.79), channel_id=1, source_target_pairs={{0,1},{1,0},{2,3},{3,2},{4,5},{5,4},{6,7},{7,6},{8,9},{9,8},{10,11... | collective-permute-start | bytes 3342344 | tf_op jit(solution)/shard_map/ppermute | solution.py:291
  34.9 18.2 %collective-permute-start.4 = (bf16[144,3264]{1,0:T(8,128)(2,1)S(1)}, bf16[144,3264]{1,0:T(8,128)(2,1)S(1)}, u32[]{:S(2)}, u32[]{:S(2)}) collective-permute-start(bf16[144,3264]{1,0:T(8,128)(2,1)S(1)} %pad_maximum_fusion.14), channel_id=1, source_target_pairs={{0,4},{2,6},{4,0},{6,2},{8,12},{10,14},{12,8},{14,10},{16,20},{18,... | collective-permute-start | bytes 2820104 | tf_op jit(solution)/shard_map/ppermute | solution.py:287
  42.0 41.8 %collective-permute-start.12 = (bf16[288,1088]{1,0:T(8,128)(2,1)S(1)}, bf16[288,1088]{1,0:T(8,128)(2,1)S(1)}, u32[]{:S(2)}, u32[]{:S(2)}) collective-permute-start(bf16[288,1088]{1,0:T(8,128)(2,1)S(1)} %pad_maximum_fusion.16), channel_id=1, source_target_pairs={{0,2},{2,0},{4,6},{6,4},{8,10},{10,8},{12,14},{14,12},{16,18},{18,... | collective-permute-start | bytes 1880072 | tf_op jit(solution)/shard_map/ppermute | solution.py:287
  50.6 12.6 %collective-permute-start.6 = (bf16[72,4352]{1,0:T(8,128)(2,1)S(1)}, bf16[72,4352]{1,0:T(8,128)(2,1)S(1)}, u32[]{:S(2)}, u32[]{:S(2)}) collective-permute-start(bf16[72,4352]{1,0:T(8,128)(2,1)S(1)} %constant_dynamic-slice_fusion.2), channel_id=1, source_target_pairs={{0,1},{1,0},{2,3},{3,2},{4,5},{5,4},{6,7},{7,6},{8,9},{9,8},{10,11... | collective-permute-start | bytes 1880072 | tf_op jit(solution)/shard_map/ppermute | solution.py:291
  53.5 12.5 %collective-permute-start.5 = (bf16[288,3264]{1,0:T(8,128)(2,1)S(1)}, bf16[288,3264]{1,0:T(8,128)(2,1)S(1)}, u32[]{:S(2)}, u32[]{:S(2)}) collective-permute-start(bf16[288,3264]{1,0:T(8,128)(2,1)S(1)} %pad_maximum_fusion.8), channel_id=1, source_target_pairs={{0,2},{2,0},{4,6},{6,4},{8,10},{10,8},{12,14},{14,12},{16,18},{18,... | collective-permute-start | bytes 5640200 | tf_op jit(solution)/shard_map/ppermute | solution.py:287
  63.2 20.0 %collective-permute-start.7 = (bf16[72,4352]{1,0:T(8,128)(2,1)S(1)}, bf16[72,4352]{1,0:T(8,128)(2,1)S(1)}, u32[]{:S(2)}, u32[]{:S(2)}) collective-permute-start(bf16[72,4352]{1,0:T(8,128)(2,1)S(1)} %collective-permute-done.6), channel_id=1, source_target_pairs={{0,4},{2,6},{4,0},{6,2},{8,12},{10,14},{12,8},{14,10},{16,20},{18,... | collective-permute-start | bytes 1880072 | tf_op jit(solution)/shard_map/ppermute | solution.py:287
  65.6 18.5 %collective-permute-start.8 = (bf16[136,2176]{1,0:T(8,128)(2,1)S(1)}, bf16[136,2176]{1,0:T(8,128)(2,1)S(1)}, u32[]{:S(2)}, u32[]{:S(2)}) collective-permute-start(bf16[136,2176]{1,0:T(8,128)(2,1)S(1)} %constant_dynamic-slice_fusion.1), channel_id=1, source_target_pairs={{0,1},{1,0},{2,3},{3,2},{4,5},{5,4},{6,7},{7,6},{8,9},{9,8},{10,11... | collective-permute-start | bytes 1775624 | tf_op jit(solution)/shard_map/ppermute | solution.py:291
  83.5 34.7 %collective-permute-start.13 = (bf16[144,4352]{1,0:T(8,128)(2,1)S(1)}, bf16[144,4352]{1,0:T(8,128)(2,1)S(1)}, u32[]{:S(2)}, u32[]{:S(2)}) collective-permute-start(bf16[144,4352]{1,0:T(8,128)(2,1)S(1)} %pad_maximum_fusion.10), channel_id=1, source_target_pairs={{0,8},{2,10},{4,12},{6,14},{8,0},{10,2},{12,4},{14,6},{16,24},{18,... | collective-permute-start | bytes 3760136 | tf_op jit(solution)/shard_map/ppermute | solution.py:287
  84.1 34.0 %collective-permute-start.14 = (bf16[136,2176]{1,0:T(8,128)(2,1)S(1)}, bf16[136,2176]{1,0:T(8,128)(2,1)S(1)}, u32[]{:S(2)}, u32[]{:S(2)}) collective-permute-start(bf16[136,2176]{1,0:T(8,128)(2,1)S(1)} %collective-permute-done.8), channel_id=1, source_target_pairs={{0,4},{2,6},{4,0},{6,2},{8,12},{10,14},{12,8},{14,10},{16,20},{18,... | collective-permute-start | bytes 1775624 | tf_op jit(solution)/shard_map/ppermute | solution.py:287
  121.0 13.3 %collective-permute-start.15 = (bf16[288,4352]{1,0:T(8,128)(2,1)}, bf16[288,4352]{1,0:T(8,128)(2,1)}, u32[]{:S(2)}, u32[]{:S(2)}) collective-permute-start(bf16[288,4352]{1,0:T(8,128)(2,1)} %pad_maximum_fusion.3), channel_id=1, source_target_pairs={{0,2},{2,0},{4,6},{6,4},{8,10},{10,8},{12,14},{14,12},{16,18},{18,... | collective-permute-start | bytes 7520264 | tf_op jit(solution)/shard_map/ppermute | solution.py:287
  126.6 31.1 %collective-permute-start.16 = (bf16[272,2176]{1,0:T(8,128)(2,1)}, bf16[272,2176]{1,0:T(8,128)(2,1)}, u32[]{:S(2)}, u32[]{:S(2)}) collective-permute-start(bf16[272,2176]{1,0:T(8,128)(2,1)} %pad_maximum_fusion.11), channel_id=1, source_target_pairs={{0,8},{2,10},{4,12},{6,14},{8,0},{10,2},{12,4},{14,6},{16,24},{18,... | collective-permute-start | bytes 3551240 | tf_op jit(solution)/shard_map/ppermute | solution.py:287
  162.1 21.7 %collective-permute-start.19 = (bf16[512,4352]{1,0:T(8,128)(2,1)}, bf16[512,4352]{1,0:T(8,128)(2,1)}, u32[]{:S(2)}, u32[]{:S(2)}) collective-permute-start(bf16[512,4352]{1,0:T(8,128)(2,1)} %get-tuple-element.70.act_ref.right_own), channel_id=1, source_target_pairs={{0,2},{2,0},{4,6},{6,4},{8,10},{10,8},{12,14},{14,12},{16,18},{18,... | collective-permute-start | bytes 13369352 | tf_op jit(solution)/shard_map/ppermute | solution.py:287
  164.7 19.1 %collective-permute-start.18 = (bf16[544,512]{1,0:T(8,128)(2,1)}, bf16[544,512]{1,0:T(8,128)(2,1)}, u32[]{:S(2)}, u32[]{:S(2)}) collective-permute-start(bf16[544,512]{1,0:T(8,128)(2,1)} %get-tuple-element.169), channel_id=1, source_target_pairs={{0,2},{2,0},{4,6},{6,4},{8,10},{10,8},{12,14},{14,12},{16,18},{18,... | collective-permute-start | bytes 1671176 | tf_op jit(solution)/shard_map/ppermute | solution.py:287
  220.0 32.7 %collective-permute-start.21 = (bf16[512,4352]{1,0:T(8,128)(2,1)}, bf16[512,4352]{1,0:T(8,128)(2,1)}, u32[]{:S(2)}, u32[]{:S(2)}) collective-permute-start(bf16[512,4352]{1,0:T(8,128)(2,1)} %get-tuple-element.77.right_own), channel_id=1, source_target_pairs={{0,2},{2,0},{4,6},{6,4},{8,10},{10,8},{12,14},{14,12},{16,18},{18,... | collective-permute-start | bytes 13369352 | tf_op jit(solution)/shard_map/ppermute | solution.py:287
  221.7 53.1 %collective-permute-start.24 = (bf16[544,2176]{1,0:T(8,128)(2,1)}, bf16[544,2176]{1,0:T(8,128)(2,1)}, u32[]{:S(2)}, u32[]{:S(2)}) collective-permute-start(bf16[544,2176]{1,0:T(8,128)(2,1)} %get-tuple-element.73), channel_id=1, source_target_pairs={{0,1},{1,0},{2,3},{3,2},{4,5},{5,4},{6,7},{7,6},{8,9},{9,8},{10,11... | collective-permute-start | bytes 7102472 | tf_op jit(solution)/shard_map/ppermute | solution.py:291
  233.2 12.4 %collective-permute-start.23 = (bf16[512,1088]{0,1:T(8,128)(2,1)}, bf16[512,1088]{0,1:T(8,128)(2,1)}, u32[]{:S(2)}, u32[]{:S(2)}) collective-permute-start(bf16[512,1088]{0,1:T(8,128)(2,1)} %get-tuple-element.118), channel_id=1, source_target_pairs={{0,2},{2,0},{4,6},{6,4},{8,10},{10,8},{12,14},{14,12},{16,18},{18,... | collective-permute-start | bytes 3342344 | tf_op jit(solution)/shard_map/ppermute | solution.py:287
  234.9 13.0 %collective-permute-start.22 = (bf16[2,272,512]{2,1,0:T(8,128)(2,1)}, bf16[2,272,512]{2,1,0:T(8,128)(2,1)}, u32[]{:S(2)}, u32[]{:S(2)}) collective-permute-start(bf16[2,272,512]{2,1,0:T(8,128)(2,1)} %get-tuple-element.165), channel_id=1, source_target_pairs={{0,2},{2,0},{4,6},{6,4},{8,10},{10,8},{12,14},{14,12},{16,18},{18,... | collective-permute-start | bytes 1671176 | tf_op jit(solution)/shard_map/ppermute | solution.py:287
  236.0 16.7 %collective-permute-start.20 = (bf16[2,272,512]{2,1,0:T(8,128)(2,1)S(1)}, bf16[2,272,512]{2,1,0:T(8,128)(2,1)S(1)}, u32[]{:S(2)}, u32[]{:S(2)}) collective-permute-start(bf16[2,272,512]{2,1,0:T(8,128)(2,1)S(1)} %get-tuple-element.167), channel_id=1, source_target_pairs={{0,2},{2,0},{4,6},{6,4},{8,10},{10,8},{12,14},{14,12},{16,18},{18,... | collective-permute-start | bytes 1671176 | tf_op jit(solution)/shard_map/ppermute | solution.py:287
  279.0 62.2 %collective-permute-start.26 = (bf16[272,2176]{1,0:T(8,128)(2,1)}, bf16[272,2176]{1,0:T(8,128)(2,1)}, u32[]{:S(2)}, u32[]{:S(2)}) collective-permute-start(bf16[272,2176]{1,0:T(8,128)(2,1)} %broadcast_select_fusion.23), channel_id=1, source_target_pairs={{0,4},{2,6},{4,0},{6,2},{8,12},{10,14},{12,8},{14,10},{16,20},{18,... | collective-permute-start | bytes 3551240 | tf_op jit(solution)/shard_map/ppermute | solution.py:287
  326.6 19.7 %collective-permute-start.29 = (bf16[1024,1088]{0,1:T(8,128)(2,1)}, bf16[1024,1088]{0,1:T(8,128)(2,1)}, u32[]{:S(2)}, u32[]{:S(2)}) collective-permute-start(bf16[1024,1088]{0,1:T(8,128)(2,1)} %copy.69), channel_id=1, source_target_pairs={{0,2},{2,0},{4,6},{6,4},{8,10},{10,8},{12,14},{14,12},{16,18},{18,... | collective-permute-start | bytes 6684680 | tf_op jit(solution)/shard_map/ppermute | solution.py:287
  328.0 22.5 %collective-permute-start.28 = (bf16[1024,1088]{0,1:T(8,128)(2,1)}, bf16[1024,1088]{0,1:T(8,128)(2,1)}, u32[]{:S(2)}, u32[]{:S(2)}) collective-permute-start(bf16[1024,1088]{0,1:T(8,128)(2,1)} %copy.68), channel_id=1, source_target_pairs={{0,2},{2,0},{4,6},{6,4},{8,10},{10,8},{12,14},{14,12},{16,18},{18,... | collective-permute-start | bytes 6684680 | tf_op jit(solution)/shard_map/ppermute | solution.py:287
  330.5 24.2 %collective-permute-start.25 = (bf16[2,272,1024]{2,1,0:T(8,128)(2,1)}, bf16[2,272,1024]{2,1,0:T(8,128)(2,1)}, u32[]{:S(2)}, u32[]{:S(2)}) collective-permute-start(bf16[2,272,1024]{2,1,0:T(8,128)(2,1)} %get-tuple-element.146), channel_id=1, source_target_pairs={{0,2},{2,0},{4,6},{6,4},{8,10},{10,8},{12,14},{14,12},{16,18},{18,... | collective-permute-start | bytes 3342344 | tf_op jit(solution)/shard_map/ppermute | solution.py:287
  337.6 53.4 %collective-permute-start.31 = (bf16[272,4352]{1,0:T(8,128)(2,1)}, bf16[272,4352]{1,0:T(8,128)(2,1)}, u32[]{:S(2)}, u32[]{:S(2)}) collective-permute-start(bf16[272,4352]{1,0:T(8,128)(2,1)} %get-tuple-element.78), channel_id=1, source_target_pairs={{0,1},{1,0},{2,3},{3,2},{4,5},{5,4},{6,7},{7,6},{8,9},{9,8},{10,11... | collective-permute-start | bytes 7102472 | tf_op jit(solution)/shard_map/ppermute | solution.py:291
  344.2 26.4 %collective-permute-start.30 = (bf16[136,2176]{1,0:T(8,128)(2,1)}, bf16[136,2176]{1,0:T(8,128)(2,1)}, u32[]{:S(2)}, u32[]{:S(2)}) collective-permute-start(bf16[136,2176]{1,0:T(8,128)(2,1)} %broadcast_select_fusion.43), channel_id=1, source_target_pairs={{0,8},{2,10},{4,12},{6,14},{8,0},{10,2},{12,4},{14,6},{16,24},{18,... | collective-permute-start | bytes 1775624 | tf_op jit(solution)/shard_map/ppermute | solution.py:287
  369.2 130.9 %collective-permute-start.33 = (bf16[272,3264]{1,0:T(8,128)(2,1)}, bf16[272,3264]{1,0:T(8,128)(2,1)}, u32[]{:S(2)}, u32[]{:S(2)}) collective-permute-start(bf16[272,3264]{1,0:T(8,128)(2,1)} %get-tuple-element.90), channel_id=1, source_target_pairs={{0,1},{1,0},{2,3},{3,2},{4,5},{5,4},{6,7},{7,6},{8,9},{9,8},{10,11... | collective-permute-start | bytes 5326856 | tf_op jit(solution)/shard_map/ppermute | solution.py:291
  372.0 72.0 %collective-permute-start.53 = (bf16[136,2176]{1,0:T(8,128)(2,1)S(1)}, bf16[136,2176]{1,0:T(8,128)(2,1)S(1)}, u32[]{:S(2)}, u32[]{:S(2)}) collective-permute-start(bf16[136,2176]{1,0:T(8,128)(2,1)S(1)} %add_convert_fusion.13), channel_id=1, source_target_pairs={{0,16},{2,18},{4,20},{6,22},{8,24},{10,26},{12,28},{14,30},{16,0},... | collective-permute-start | bytes 1775624 | tf_op jit(solution)/shard_map/ppermute | solution.py:287
  408.3 34.8 %collective-permute-start.40 = (bf16[272,1088]{1,0:T(8,128)(2,1)S(1)}, bf16[272,1088]{1,0:T(8,128)(2,1)S(1)}, u32[]{:S(2)}, u32[]{:S(2)}) collective-permute-start(bf16[272,1088]{1,0:T(8,128)(2,1)S(1)} %copy-done.63), channel_id=1, source_target_pairs={{0,1},{1,0},{2,3},{3,2},{4,5},{5,4},{6,7},{7,6},{8,9},{9,8},{10,11... | collective-permute-start | bytes 1775624 | tf_op jit(solution)/shard_map/ppermute | solution.py:291
  411.5 55.6 %collective-permute-start.32 = (bf16[1088,512]{1,0:T(8,128)(2,1)S(1)}, bf16[1088,512]{1,0:T(8,128)(2,1)S(1)}, u32[]{:S(2)}, u32[]{:S(2)}) collective-permute-start(bf16[1088,512]{1,0:T(8,128)(2,1)S(1)} %copy-done.62), channel_id=1, source_target_pairs={{0,1},{1,0},{2,3},{3,2},{4,5},{5,4},{6,7},{7,6},{8,9},{9,8},{10,11... | collective-permute-start | bytes 3342344 | tf_op jit(solution)/shard_map/ppermute | solution.py:291
  412.6 67.3 %collective-permute-start.47 = (bf16[136,4352]{1,0:T(8,128)(2,1)}, bf16[136,4352]{1,0:T(8,128)(2,1)}, u32[]{:S(2)}, u32[]{:S(2)}) collective-permute-start(bf16[136,4352]{1,0:T(8,128)(2,1)} %broadcast_select_fusion.20), channel_id=1, source_target_pairs={{0,4},{2,6},{4,0},{6,2},{8,12},{10,14},{12,8},{14,10},{16,20},{18,... | collective-permute-start | bytes 3551240 | tf_op jit(solution)/shard_map/ppermute | solution.py:287
  444.1 13.4 %collective-permute-start.54 = (bf16[136,2176]{1,0:T(8,128)(2,1)S(1)}, bf16[136,2176]{1,0:T(8,128)(2,1)S(1)}, u32[]{:S(2)}, u32[]{:S(2)}) collective-permute-start(bf16[136,2176]{1,0:T(8,128)(2,1)S(1)} %add_convert_fusion.12), channel_id=1, source_target_pairs={{0,8},{2,10},{4,12},{6,14},{8,0},{10,2},{12,4},{14,6},{16,24},{18,... | collective-permute-start | bytes 1775624 | tf_op jit(solution)/shard_map/ppermute | solution.py:287
  458.9 58.4 %collective-permute-start.55 = (bf16[272,2176]{1,0:T(8,128)(2,1)}, bf16[272,2176]{1,0:T(8,128)(2,1)}, u32[]{:S(2)}, u32[]{:S(2)}) collective-permute-start(bf16[272,2176]{1,0:T(8,128)(2,1)} %pad_maximum_fusion.13), channel_id=1, source_target_pairs={{0,4},{2,6},{4,0},{6,2},{8,12},{10,14},{12,8},{14,10},{16,20},{18,... | collective-permute-start | bytes 3551240 | tf_op jit(solution)/shard_map/ppermute | solution.py:287
  461.9 24.6 %collective-permute-start.43 = (bf16[72,1088]{1,0:T(8,128)(2,1)}, bf16[72,1088]{1,0:T(8,128)(2,1)}, u32[]{:S(2)}, u32[]{:S(2)}) collective-permute-start(bf16[72,1088]{1,0:T(8,128)(2,1)} %add_convert_fusion.18), channel_id=1, source_target_pairs={{0,16},{2,18},{4,20},{6,22},{8,24},{10,26},{12,28},{14,30},{16,0},... | collective-permute-start | bytes 470024 | tf_op jit(solution)/shard_map/ppermute | solution.py:287
  483.7 31.8 %collective-permute-start.48 = (bf16[72,4352]{1,0:T(8,128)(2,1)S(1)}, bf16[72,4352]{1,0:T(8,128)(2,1)S(1)}, u32[]{:S(2)}, u32[]{:S(2)}) collective-permute-start(bf16[72,4352]{1,0:T(8,128)(2,1)S(1)} %broadcast_select_fusion.36), channel_id=1, source_target_pairs={{0,8},{2,10},{4,12},{6,14},{8,0},{10,2},{12,4},{14,6},{16,24},{18,... | collective-permute-start | bytes 1880072 | tf_op jit(solution)/shard_map/ppermute | solution.py:287
  487.5 11.7 %collective-permute-start.44 = (bf16[72,1088]{1,0:T(8,128)(2,1)S(1)}, bf16[72,1088]{1,0:T(8,128)(2,1)S(1)}, u32[]{:S(2)}, u32[]{:S(2)}) collective-permute-start(bf16[72,1088]{1,0:T(8,128)(2,1)S(1)} %add_convert_fusion.17), channel_id=1, source_target_pairs={{0,8},{2,10},{4,12},{6,14},{8,0},{10,2},{12,4},{14,6},{16,24},{18,... | collective-permute-start | bytes 470024 | tf_op jit(solution)/shard_map/ppermute | solution.py:287
  502.2 19.9 %collective-permute-start.34 = (bf16[136,3264]{1,0:T(8,128)(2,1)S(1)}, bf16[136,3264]{1,0:T(8,128)(2,1)S(1)}, u32[]{:S(2)}, u32[]{:S(2)}) collective-permute-start(bf16[136,3264]{1,0:T(8,128)(2,1)S(1)} %broadcast_select_fusion.32), channel_id=1, source_target_pairs={{0,4},{2,6},{4,0},{6,2},{8,12},{10,14},{12,8},{14,10},{16,20},{18,... | collective-permute-start | bytes 2663432 | tf_op jit(solution)/shard_map/ppermute | solution.py:287
  505.3 14.3 %collective-permute-start.46 = (bf16[272,1088]{1,0:T(8,128)(2,1)S(1)}, bf16[272,1088]{1,0:T(8,128)(2,1)S(1)}, u32[]{:S(2)}, u32[]{:S(2)}) collective-permute-start(bf16[272,1088]{1,0:T(8,128)(2,1)S(1)} %pad_maximum_fusion.17), channel_id=1, source_target_pairs={{0,2},{2,0},{4,6},{6,4},{8,10},{10,8},{12,14},{14,12},{16,18},{18,... | collective-permute-start | bytes 1775624 | tf_op jit(solution)/shard_map/ppermute | solution.py:287
  515.7 30.2 %collective-permute-start.49 = (bf16[72,4352]{1,0:T(8,128)(2,1)S(1)}, bf16[72,4352]{1,0:T(8,128)(2,1)S(1)}, u32[]{:S(2)}, u32[]{:S(2)}) collective-permute-start(bf16[72,4352]{1,0:T(8,128)(2,1)S(1)} %add_convert_fusion.10), channel_id=1, source_target_pairs={{0,16},{2,18},{4,20},{6,22},{8,24},{10,26},{12,28},{14,30},{16,0},... | collective-permute-start | bytes 1880072 | tf_op jit(solution)/shard_map/ppermute | solution.py:287
  519.3 100.7 %collective-permute-start.56 = (bf16[544,2176]{1,0:T(8,128)(2,1)S(1)}, bf16[544,2176]{1,0:T(8,128)(2,1)S(1)}, u32[]{:S(2)}, u32[]{:S(2)}) collective-permute-start(bf16[544,2176]{1,0:T(8,128)(2,1)S(1)} %pad_maximum_fusion.6), channel_id=1, source_target_pairs={{0,2},{2,0},{4,6},{6,4},{8,10},{10,8},{12,14},{14,12},{16,18},{18,... | collective-permute-start | bytes 7102472 | tf_op jit(solution)/shard_map/ppermute | solution.py:287
  522.5 23.7 %collective-permute-start.35 = (bf16[72,3264]{1,0:T(8,128)(2,1)S(1)}, bf16[72,3264]{1,0:T(8,128)(2,1)S(1)}, u32[]{:S(2)}, u32[]{:S(2)}) collective-permute-start(bf16[72,3264]{1,0:T(8,128)(2,1)S(1)} %broadcast_select_fusion.47), channel_id=1, source_target_pairs={{0,8},{2,10},{4,12},{6,14},{8,0},{10,2},{12,4},{14,6},{16,24},{18,... | collective-permute-start | bytes 1410056 | tf_op jit(solution)/shard_map/ppermute | solution.py:287
  546.1 22.5 %collective-permute-start.50 = (bf16[72,4352]{1,0:T(8,128)(2,1)S(1)}, bf16[72,4352]{1,0:T(8,128)(2,1)S(1)}, u32[]{:S(2)}, u32[]{:S(2)}) collective-permute-start(bf16[72,4352]{1,0:T(8,128)(2,1)S(1)} %add_convert_fusion.9), channel_id=1, source_target_pairs={{0,8},{2,10},{4,12},{6,14},{8,0},{10,2},{12,4},{14,6},{16,24},{18,... | collective-permute-start | bytes 1880072 | tf_op jit(solution)/shard_map/ppermute | solution.py:287
  546.4 23.0 %collective-permute-start.36 = (bf16[72,3264]{1,0:T(8,128)(2,1)S(1)}, bf16[72,3264]{1,0:T(8,128)(2,1)S(1)}, u32[]{:S(2)}, u32[]{:S(2)}) collective-permute-start(bf16[72,3264]{1,0:T(8,128)(2,1)S(1)} %add_convert_fusion.15), channel_id=1, source_target_pairs={{0,16},{2,18},{4,20},{6,22},{8,24},{10,26},{12,28},{14,30},{16,0},... | collective-permute-start | bytes 1410056 | tf_op jit(solution)/shard_map/ppermute | solution.py:287
  569.5 12.9 %collective-permute-start.37 = (bf16[72,3264]{1,0:T(8,128)(2,1)S(1)}, bf16[72,3264]{1,0:T(8,128)(2,1)S(1)}, u32[]{:S(2)}, u32[]{:S(2)}) collective-permute-start(bf16[72,3264]{1,0:T(8,128)(2,1)S(1)} %add_convert_fusion.14), channel_id=1, source_target_pairs={{0,8},{2,10},{4,12},{6,14},{8,0},{10,2},{12,4},{14,6},{16,24},{18,... | collective-permute-start | bytes 1410056 | tf_op jit(solution)/shard_map/ppermute | solution.py:287
  571.5 22.3 %collective-permute-start.51 = (bf16[136,4352]{1,0:T(8,128)(2,1)S(1)}, bf16[136,4352]{1,0:T(8,128)(2,1)S(1)}, u32[]{:S(2)}, u32[]{:S(2)}) collective-permute-start(bf16[136,4352]{1,0:T(8,128)(2,1)S(1)} %pad_maximum_fusion.12), channel_id=1, source_target_pairs={{0,4},{2,6},{4,0},{6,2},{8,12},{10,14},{12,8},{14,10},{16,20},{18,... | collective-permute-start | bytes 3551240 | tf_op jit(solution)/shard_map/ppermute | solution.py:287
  582.6 30.6 %collective-permute-start.38 = (bf16[136,3264]{1,0:T(8,128)(2,1)S(1)}, bf16[136,3264]{1,0:T(8,128)(2,1)S(1)}, u32[]{:S(2)}, u32[]{:S(2)}) collective-permute-start(bf16[136,3264]{1,0:T(8,128)(2,1)S(1)} %pad_maximum_fusion.15), channel_id=1, source_target_pairs={{0,4},{2,6},{4,0},{6,2},{8,12},{10,14},{12,8},{14,10},{16,20},{18,... | collective-permute-start | bytes 2663432 | tf_op jit(solution)/shard_map/ppermute | solution.py:287
  594.4 35.1 %collective-permute-start.52 = (bf16[272,4352]{1,0:T(8,128)(2,1)S(1)}, bf16[272,4352]{1,0:T(8,128)(2,1)S(1)}, u32[]{:S(2)}, u32[]{:S(2)}) collective-permute-start(bf16[272,4352]{1,0:T(8,128)(2,1)S(1)} %pad_maximum_fusion.5), channel_id=1, source_target_pairs={{0,2},{2,0},{4,6},{6,4},{8,10},{10,8},{12,14},{14,12},{16,18},{18,... | collective-permute-start | bytes 7102472 | tf_op jit(solution)/shard_map/ppermute | solution.py:287
  613.6 11.6 %collective-permute-start.39 = (bf16[272,3264]{1,0:T(8,128)(2,1)S(1)}, bf16[272,3264]{1,0:T(8,128)(2,1)S(1)}, u32[]{:S(2)}, u32[]{:S(2)}) collective-permute-start(bf16[272,3264]{1,0:T(8,128)(2,1)S(1)} %pad_maximum_fusion.9), channel_id=1, source_target_pairs={{0,2},{2,0},{4,6},{6,4},{8,10},{10,8},{12,14},{14,12},{16,18},{18,... | collective-permute-start | bytes 5326856 | tf_op jit(solution)/shard_map/ppermute | solution.py:287
  (79 other events, 812.6 us)

commit v3 on v2

--- a/solution.py
+++ b/solution.py
@@ -10,6 +10,7 @@
 SCALING = 0.125
 NEG = -1e30
 LANES = 128
+QUICK = pl.CostEstimate(flops=1, bytes_accessed=1, transcendentals=0)
 
 
 def _nt(a, b):
@@ -196,7 +197,7 @@
             jax.ShapeDtypeStruct((seqs * pairs, 2, span), jnp.float32),
         ],
         compiler_params=pltpu.CompilerParams(vmem_limit_bytes=48 * 1024 * 1024),
-        cost_estimate=pl.CostEstimate(flops=4 * rows * length * width * 2, bytes_accessed=8 * rows * width * 2, transcendentals=rows * length * 17),
+        cost_estimate=QUICK,
         name="attention_forward",
     )(position, queries, keys, values)
 
@@ -224,12 +225,12 @@
             ],
         ),
         out_shape=[
-            jax.ShapeDtypeStruct((rows, width), jnp.bfloat16),
-            jax.ShapeDtypeStruct(keys.shape, jnp.bfloat16),
-            jax.ShapeDtypeStruct(keys.shape, jnp.bfloat16),
+            jax.ShapeDtypeStruct((rows, pairs * LANES), jnp.bfloat16),
+            jax.ShapeDtypeStruct((keys.shape[0], pairs * LANES), jnp.bfloat16),
+            jax.ShapeDtypeStruct((keys.shape[0], pairs * LANES), jnp.bfloat16),
         ],
         compiler_params=pltpu.CompilerParams(vmem_limit_bytes=48 * 1024 * 1024),
-        cost_estimate=pl.CostEstimate(flops=10 * rows * length * width * 2, bytes_accessed=12 * rows * width * 2, transcendentals=rows * length * 17),
+        cost_estimate=QUICK,
         name="attention_backward",
     )(position, queries, keys, values, grads, context, lse_rows)
 
@@ -366,7 +367,7 @@
         ),
         out_shape=out_shapes,
         compiler_params=pltpu.CompilerParams(vmem_limit_bytes=VMEM_LIMIT),
-        cost_estimate=pl.CostEstimate(flops=flops, bytes_accessed=moved, transcendentals=0),
+        cost_estimate=QUICK,
         name=name,
     )
 
@@ -382,7 +383,8 @@
     )
 
 
-def up_kernel(pos_ref, nt_ref, bias_ref, own_ref, got_ref, act_ref, slope_ref, full_ref, sems):
+def up_kernel(pos_ref, ctx_ref, out_w_ref, x_ref, vec_ref, bias_ref, own_ref, got_ref,
+              act_ref, slope_ref, mid_t_ref, unit_ref, rstd_ref, nt_t_ref, nt_ref, full_ref, sems):
     pos = pos_ref[0]
     units = own_ref.shape[1]
     count = units // CHUNK
@@ -390,38 +392,52 @@
     for pair in copies:
         for copy in pair:
             copy.start()
+    unit_ref[...] = _nn(ctx_ref[...], out_w_ref[...])
+    rows = ctx_ref.shape[0]
+    tile = 128
+    for at in range(0, rows, tile):
+        where = slice(at, at + tile)
+        middle = x_ref[where, :].astype(jnp.float32) + (unit_ref[where, :] + vec_ref[0:1, :])
+        unit, rstd = centred(middle)
+        normed = unit * vec_ref[1:2, :] + vec_ref[2:3, :]
+        unit_ref[where, :] = unit
+        rstd_ref[where, :] = rstd
+        mid_t_ref[:, where] = middle.T
+        nt_ref[where, :] = normed.astype(jnp.bfloat16)
+        nt_t_ref[:, where] = normed.T.astype(jnp.bfloat16)
+    for pair in copies:
+        for copy in pair:
+            copy.wait()
     normed = nt_ref[...]
-    early = min(3, count)
-    for j in range(early):
-        for copy in copies[j]:
-            copy.wait()
-
     for j in range(count):
-        if j == early:
-            for later in copies[early:]:
-                for copy in later:
-                    copy.wait()
         cols = pl.ds(j * CHUNK, CHUNK)
         hidden = _nn(normed, full_ref[:, cols]) + bias_ref[:, cols]
         value, slope = gelu_parts(hidden)
-        value = value.astype(jnp.bfloat16)
-        act_ref[:, cols] = value
+        act_ref[:, cols] = value.astype(jnp.bfloat16)
         slope_ref[:, cols] = slope.astype(jnp.bfloat16)
 
 
-def mlp_up(spot, normed, bias, own, got):
-    rows, width = normed.shape
+def mlp_up(spot, context, out_weight, tokens, vectors, bias, own, got):
+    rows, width = tokens.shape
     units = own.shape[1]
     any_spec = pl.BlockSpec(memory_space=pl.ANY)
     return _call(
-        up_kernel, "mlp_up", _vmem(2) + [any_spec] * 2,
+        up_kernel, "mlp_up", _vmem(5) + [any_spec] * 2,
         [
             jax.ShapeDtypeStruct((rows, units), jnp.bfloat16),
             jax.ShapeDtypeStruct((rows, units), jnp.bfloat16),
+            jax.ShapeDtypeStruct((width, rows), jnp.float32),
+            jax.ShapeDtypeStruct((rows, width), jnp.float32),
+            jax.ShapeDtypeStruct((rows, 1), jnp.float32),
+            jax.ShapeDtypeStruct((width, rows), jnp.bfloat16),
         ],
-        [pltpu.VMEM((width, units), jnp.bfloat16), pltpu.SemaphoreType.DMA((units // CHUNK, 2))],
-        2 * rows * width * units, 2 * units * (width + 3 * rows),
-    )(spot, normed, bias, own, got)
+        [
+            pltpu.VMEM((rows, width), jnp.bfloat16),
+            pltpu.VMEM((width, units), jnp.bfloat16),
+            pltpu.SemaphoreType.DMA((units // CHUNK, 2)),
+        ],
+        2 * rows * width * (units + width), 2 * units * (width + 2 * rows) + 18 * rows * width,
+    )(spot, context, out_weight, tokens, vectors, bias, own, got)
 
 
 def down_kernel(pos_ref, act_ref, own_ref, got_ref, middle_ref, bias_ref, out_ref):
@@ -452,16 +468,19 @@
         ),
         out_shape=jax.ShapeDtypeStruct((width, rows), jnp.bfloat16),
         compiler_params=pltpu.CompilerParams(vmem_limit_bytes=VMEM_LIMIT),
-        cost_estimate=pl.CostEstimate(flops=4 * rows * width * half, bytes_accessed=4 * half * (width + rows), transcendentals=0),
+        cost_estimate=QUICK,
         name="mlp_down",
     )(spot, active, own, got, middle, bias)
 
 
-def back_kernel(pos_ref, grad_ref, slope_ref, down_own, down_got, up_own, up_got,
-                hidden_ref, normed_ref, sum_ref, down_full, up_full, sems):
+def back_kernel(pos_ref, grad_ref, slope_ref, unit_ref, rstd_ref, gain_ref, out_w_ref,
+                down_own, down_got, up_own, up_got,
+                hidden_ref, middle_ref, branch_ref, context_ref, wide_sum_ref, sum_ref,
+                down_full, up_full, sems):
     pos = pos_ref[0]
     half = down_own.shape[1]
     units = up_own.shape[1]
+    rows, width = grad_ref.shape
     mine = pl.ds(pl.multiple_of(pos * half, 128), half)
     theirs = pl.ds(pl.multiple_of((1 - pos) * half, 128), half)
     first = pltpu.make_async_copy(down_own, down_full.at[:, mine], sems.at[0])
@@ -481,33 +500,52 @@
         active = _nn(grad, down_full[:, cols])
         hidden = (active * slope_ref[:, cols].astype(jnp.float32)).astype(jnp.bfloat16)
         hidden_ref[:, cols] = hidden
-        sum_ref[:, cols] = jnp.sum(hidden.astype(jnp.float32), axis=0, keepdims=True)
+        wide_sum_ref[:, cols] = jnp.sum(hidden.astype(jnp.float32), axis=0, keepdims=True)
     third.wait()
     fourth.wait()
     hidden = hidden_ref[...]
-    for at in range(0, rows_up * 2, CHUNK):
-        size = min(CHUNK, rows_up * 2 - at)
-        normed_ref[:, at : at + size] = _nt(hidden, up_full[at : at + size, :])
-
-
-def mlp_back(spot, grad, slope, down_own, down_got, up_own, up_got):
+    for at in range(0, width, CHUNK):
+        size = min(CHUNK, width - at)
+        middle_ref[:, at : at + size] = _nt(hidden, up_full[at : at + size, :])
+    sum_ref[...] = jnp.zeros_like(sum_ref)
+    branch_ref[...] = jnp.zeros_like(branch_ref)
+    tile = 128
+    for at in range(0, rows, tile):
+        where = slice(at, at + tile)
+        normed = middle_ref[where, :]
+        unit = unit_ref[where, :]
+        out = norm_pull(normed, unit, rstd_ref[where, :], gain_ref[...])
+        out = out + grad_ref[where, :].astype(jnp.float32)
+        branch = out.astype(jnp.bfloat16)
+        middle_ref[where, :] = out
+        branch_ref[where, 0:width] = branch
+        sum_ref[0:1, :] += jnp.sum(normed * unit, axis=0, keepdims=True)
+        sum_ref[1:2, :] += jnp.sum(normed, axis=0, keepdims=True)
+        sum_ref[2:3, :] += jnp.sum(branch.astype(jnp.float32), axis=0, keepdims=True)
+    context_ref[...] = _nt(branch_ref[:, 0:width], out_w_ref[...]).astype(context_ref.dtype)
+
+
+def mlp_back(spot, grad, slope, unit, rstd, gain, out_weight, down_own, down_got, up_own, up_got):
     rows, width = grad.shape
     units = up_own.shape[1]
     any_spec = pl.BlockSpec(memory_space=pl.ANY)
     return _call(
-        back_kernel, "mlp_back", _vmem(2) + [any_spec] * 4,
+        back_kernel, "mlp_back", _vmem(6) + [any_spec] * 4,
         [
             jax.ShapeDtypeStruct((rows, units), jnp.bfloat16),
             jax.ShapeDtypeStruct((rows, width), jnp.float32),
+            jax.ShapeDtypeStruct((rows, pl.cdiv(width, LANES) * LANES), jnp.bfloat16),
+            jax.ShapeDtypeStruct((rows, width), jnp.bfloat16),
             jax.ShapeDtypeStruct((1, units), jnp.float32),
+            jax.ShapeDtypeStruct((8, width), jnp.float32),
         ],
         [
             pltpu.VMEM((width, units), jnp.bfloat16),
             pltpu.VMEM((width, units), jnp.bfloat16),
             pltpu.SemaphoreType.DMA((4,)),
         ],
-        4 * rows * width * units, 4 * units * (width + rows),
-    )(spot, grad, slope, down_own, down_got, up_own, up_got)
+        4 * rows * width * units + 2 * rows * width * width, 4 * units * (width + rows) + 12 * rows * width,
+    )(spot, grad, slope, unit, rstd, gain, out_weight, down_own, down_got, up_own, up_got)
 
 
 def weight_kernel(pos_ref, left_own, left_sib, right_own, right_sib, give_ref, keep_ref, total_ref):
@@ -521,9 +559,8 @@
     keep_ref[...] = total_ref[pos]
 
 
-def weight_grads(spot, left_own, left_sib, right_own, right_sib, tile_rows, tile_cols, name):
+def weight_grads(spot, left_own, left_sib, right_own, right_sib, columns, tile_rows, tile_cols, name):
     _, rows, tokens = left_own.shape
-    columns = right_own.shape[1]
     left = pl.BlockSpec((2, tile_rows, tokens), lambda i, j, p: (0, i, 0))
     right = pl.BlockSpec((tokens, tile_cols), lambda i, j, p: (0, j))
     out = pl.BlockSpec((tile_rows, tile_cols), lambda i, j, p: (i, j))
@@ -536,7 +573,7 @@
         ),
         out_shape=[jax.ShapeDtypeStruct((rows, columns), jnp.bfloat16)] * 2,
         compiler_params=pltpu.CompilerParams(vmem_limit_bytes=VMEM_LIMIT),
-        cost_estimate=pl.CostEstimate(flops=8 * rows * tokens * columns, bytes_accessed=4 * rows * columns + 4 * tokens * columns, transcendentals=0),
+        cost_estimate=QUICK,
         name=name,
     )(spot, left_own, left_sib, right_own, right_sib)
 
@@ -572,7 +609,7 @@
         ),
         out_shape=[jax.ShapeDtypeStruct((rows, columns), jnp.bfloat16)] * 2,
         compiler_params=pltpu.CompilerParams(vmem_limit_bytes=VMEM_LIMIT),
-        cost_estimate=pl.CostEstimate(flops=8 * rows * tokens * columns, bytes_accessed=4 * rows * columns + 8 * tokens * columns, transcendentals=0),
+        cost_estimate=QUICK,
         name=name,
     )(spot, left_own, left_sib, right_own, right_sib)
 
@@ -581,7 +618,8 @@
                       give_ref, keep_ref, total_ref):
     pos = pos_ref[0]
     _, rows, length = left_own.shape
-    span, width = q_own.shape
+    span = q_own.shape[0]
+    width = total_ref.shape[2]
     mine = pl.ds(pl.multiple_of(pos * span, 128), span)
 
     def rows_of(ref, cols):
@@ -589,16 +627,15 @@
 
     whole = pl.ds(0, length)
     for at, cols, own, sib in ((0, mine, q_own, q_sib), (1, whole, k_own, k_sib), (2, whole, v_own, v_sib)):
-        total = _nn(rows_of(left_own, cols), own[...]) + _nn(rows_of(left_sib, cols), sib[...])
+        total = _nn(rows_of(left_own, cols), own[:, 0:width]) + _nn(rows_of(left_sib, cols), sib[:, 0:width])
         total_ref[...] = total.astype(total_ref.dtype).reshape(total_ref.shape)
         give_ref[:, at * width : (at + 1) * width] = total_ref[1 - pos]
         keep_ref[:, at * width : (at + 1) * width] = total_ref[pos]
 
 
-def qkv_weight_grads(spot, left_own, left_sib, *rights):
+def qkv_weight_grads(spot, width, left_own, left_sib, *rights):
     rows = left_own.shape[1]
     length = left_own.shape[2]
-    width = rights[0].shape[1]
     return _call(
         qkv_weight_kernel, "qkv_weight_grads", _vmem(8),
         [jax.ShapeDtypeStruct((rows, 3 * width), jnp.bfloat16)] * 2,
@@ -610,15 +647,18 @@
 def input_kernel(pos_ref, wq_ref, wk_ref, wv_ref, gq_ref, gk_ref, gv_ref, mine_ref, theirs_ref):
     pos = pos_ref[0]
     span = gq_ref.shape[0]
+    cols = pl.ds(0, wq_ref.shape[1])
     mine = pl.ds(pl.multiple_of(pos * span, 16), span)
     theirs = pl.ds(pl.multiple_of((1 - pos) * span, 16), span)
     wk, wv = wk_ref[...], wv_ref[...]
-    theirs_ref[...] = (_nt(wk, gk_ref[theirs, :]) + _nt(wv, gv_ref[theirs, :])).astype(theirs_ref.dtype)
-    mine_ref[...] = _nt(wq_ref[...], gq_ref[...]) + _nt(wk, gk_ref[mine, :]) + _nt(wv, gv_ref[mine, :])
+    theirs_ref[...] = (_nt(wk, gk_ref[theirs, cols]) + _nt(wv, gv_ref[theirs, cols])).astype(theirs_ref.dtype)
+    mine_ref[...] = (
+        _nt(wq_ref[...], gq_ref[:, cols]) + _nt(wk, gk_ref[mine, cols]) + _nt(wv, gv_ref[mine, cols])
+    )
 
 
 def input_grads(spot, wq, wk, wv, gq, gk, gv):
-    span, width = gq.shape
+    span, width = gq.shape[0], wq.shape[0]
     return _call(
         input_kernel, "input_grads", _vmem(6),
         [
@@ -629,6 +669,41 @@
     )(spot, wq, wk, wv, gq, gk, gv)
 
 
+def token_kernel(pos_ref, mine_ref, other_ref, x_ref, gain_ref, middle_ref, out_ref):
+    unit, rstd = centred_down(x_ref[...].astype(jnp.float32))
+    scaled = (mine_ref[...] + other_ref[...].astype(jnp.float32)) * gain_ref[...]
+    pulled = rstd * (
+        scaled - jnp.mean(scaled, axis=0, keepdims=True)
+        - unit * jnp.mean(scaled * unit, axis=0, keepdims=True)
+    )
+    out_ref[...] = (pulled + middle_ref[...].T).astype(out_ref.dtype)
+
+
+def token_grads(spot, mine, other, tokens, gain, middle):
+    width, span = mine.shape
+    tile = 128
+    cols = pl.BlockSpec((width, tile), lambda i, p: (0, i))
+    return pl.pallas_call(
+        token_kernel,
+        grid_spec=pltpu.PrefetchScalarGridSpec(
+            num_scalar_prefetch=1, grid=(span // tile,),
+            in_specs=[
+                cols, cols, cols,
+                pl.BlockSpec((width, 1), lambda i, p: (0, 0)),
+                pl.BlockSpec((tile, width), lambda i, p: (i, 0)),
+            ],
+            out_specs=cols,
+        ),
+        out_shape=jax.ShapeDtypeStruct((width, span), jnp.bfloat16),
+        compiler_params=pltpu.CompilerParams(vmem_limit_bytes=VMEM_LIMIT),
+        cost_estimate=QUICK,
+        name="token_grads",
+    )(spot, mine, other, tokens, gain, middle)
+
+
+TAIL = "udovquqtvdoquqvudoqvudoqvuq"
+
+
 def tie(values, *earlier):
     return lax.optimization_barrier((values, *earlier))[0]
 
@@ -643,16 +718,6 @@
 
 def plus(left, right):
     return low(left.astype(jnp.float32) + right.astype(jnp.float32))
-
-
-def total_of(packed):
-    position = lax.axis_index("shard")
-    kept = pick(packed, position, 0) + cross(pick(packed, 1 - position, 0))
-    bit = 1
-    while bit < lax.axis_size("replica"):
-        kept = kept + swap(kept, bit)
-        bit *= 2
-    return kept
 
 
 def spread(weight, bits):
@@ -666,15 +731,24 @@
     got = yield cross(piece), piece
     for bit in bits[::-1]:
         other = yield swap(got, bit), got
-        got = in_order(bit, got, other)
-    extra = count * size - rows
-    if extra:
-        got = jnp.concatenate([got[: (count - 1) * size], got[(count - 1) * size + extra :]], axis=0)
+        flag = has_bit(bit)
+        parts = lax.optimization_barrier((choose(flag, other, got), choose(flag, got, other)))
+        extra = count * size - rows if bit == bits[0] else 0
+        if extra:
+            kept = parts[1].shape[0] - size
+            parts = parts[0], parts[1][:kept], parts[1][kept + extra :]
+        got = jnp.concatenate(parts, axis=0)
     return got
 
 
-def reduced(keep, give, bits):
-    got = yield cross(give), give
+def reduced(keep, give, bits, cut=False):
+    if cut:
+        above, below = halves(give)
+        above = yield cross(above), give
+        below = yield cross(below), above
+        got = jnp.concatenate([above, below], axis=0)
+    else:
+        got = yield cross(give), give
     values = plus(keep, got)
     stack = []
     for bit in bits[:-1]:
@@ -696,6 +770,18 @@
     return in_order(CORE_BIT, values, got).astype(jnp.float32)
 
 
+def vector_sum(packed):
+    position = lax.axis_index("shard")
+    got = yield swap(packed, CORE_BIT), packed
+    packed = packed + got
+    got = yield cross(pick(packed, 1 - position, 0)), packed
+    kept = pick(packed, position, 0) + got
+    for bit in all_bits():
+        got = yield swap(kept, bit), kept
+        kept = kept + got
+    return kept
+
+
 class Steps:
     def __init__(self, chain):
         self.chain = chain
@@ -705,12 +791,21 @@
         got = tie(self.got, *gates) if gates else self.got
         self.got, self.latest = self.chain.send(got)
 
-    def finish(self):
+    def finish(self, *gates):
+        if gates:
+            self.got = tie(self.got, *gates)
         while True:
             try:
                 self.step()
             except StopIteration as end:
                 return end.value
+
+
+def bound(values, *chains):
+    parts = lax.optimization_barrier((*values, *[chain.got for chain in chains]))
+    for chain, got in zip(chains, parts[len(values) :]):
+        chain.got = got
+    return parts[: len(values)]
 
 
 def centred_down(values):
@@ -739,11 +834,10 @@
         [item.reshape(1, -1) for item in singles] + [up_bias.reshape(-1, singles[0].shape[0])], axis=0
     )
     way_qkv = Steps(spread(qkv_weight, fast_bits))
-    other_vectors = cross(flat_vectors)
-    way_out = Steps(spread(out_weight, turned_bits))
     other_turned = cross(tie(own_turned, way_qkv.got))
+    other_vectors = cross(tie(flat_vectors, way_qkv.got))
     way_qkv.step()
-    way_out.step()
+    way_out = Steps(spread(tie(out_weight, other_turned), turned_bits))
     way_up = Steps(spread(tie(up_weight, other_turned), turned_bits))
     way_down = Steps(spread(tie(down_turned, way_up.got), turned_bits))
     grad_turned = cotangent.reshape(span, width).T
@@ -758,6 +852,11 @@
      bias_down) = (both[i] for i in range(8))
     bias_up = jnp.concatenate([lower[8:].reshape(1, -1), upper[8:].reshape(1, -1)], axis=1)
 
+    own_tokens = own_turned.T
+    second = jnp.stack([bias_out, gain_second, shift_second])
+    bias_down = bias_down.reshape(-1, 1)
+    bias_up, own_tokens, second, bias_down, grad_out = bound((bias_up, own_tokens, second, bias_down, grad_out))
+    way_qkv.step(bias_up, own_tokens, second, bias_down, grad_out)
     all_turned = jnp.concatenate(
         [choose(first, own_turned, other_turned), choose(first, other_turned, own_turned)], axis=1
     )
@@ -770,107 +869,134 @@
         parts = turned.reshape(2, 2, turned.shape[0] // 4, turned.shape[1])
         return pick(parts, core, 1), swap(pick(parts, 1 - core, 1), CORE_BIT)
 
-    way_up.step(normed_all)
     full_qkv = both_halves(qkv_weight, way_qkv.finish())
     full_q, full_k, full_v = (full_qkv[:, i * width : (i + 1) * width] for i in range(3))
+    way_out.step(full_v)
+    way_up.step(full_v)
+    values = low(dot(tie(normed_all, way_out.latest, way_up.latest), full_v) + bias_value)
+    way_out.step(values)
+    way_down.step(values)
+    keys = low(dot(tie(normed_all, way_out.latest, way_down.latest), full_k))
+    way_out.step(keys)
+    queries = low(low(dot(tie(normed, way_out.latest), full_q) + bias_query) * SCALING)
+    (queries,) = bound((queries,), way_up)
+    way_up.step()
+    context, context_t, lse = attention_forward(spot, tie(queries, way_up.latest), keys, values, 1, span)
+    context, context_t, lse = bound((context, context_t, lse), way_up, way_down, way_out)
     full_out = both_halves(out_weight, way_out.finish())
-    normed_all = tie(normed_all, way_up.latest)
-    keys = low(dot(normed_all, full_k))
-    values = low(dot(normed_all, full_v) + bias_value)
-    queries = low(low(dot(normed, full_q) + bias_query) * SCALING)
-    way_up.step(keys, values, queries)
-    way_down.step(keys, values, queries)
-    queries = tie(queries, way_up.latest, way_down.latest, full_out)
-    context, context_t, lse = attention_forward(spot, queries, keys, values, 1, span)
-    way_up.step(context)
-    way_down.step(context)
+    way_up.step()
+    way_down.step()
     context = tie(context, way_up.latest, way_down.latest)
     normed_left = for_cores(normed_turned)
-    flat = own_turned.T.astype(jnp.float32)
-    middle = flat + dot(context, full_out) + bias_out
-    unit_second, rstd_second = centred(middle)
-    normed_two = low(unit_second * gain_second + shift_second)
     part_up = way_up.finish()
-    active, slope = mlp_up(spot, normed_two, bias_up, up_weight, part_up)
+    active, slope, middle_turned, unit_second, rstd_second, two_turned = mlp_up(
+        spot, context, full_out, own_tokens, second, bias_up, up_weight, part_up
+    )
+    active, slope, middle_turned, unit_second, rstd_second, two_turned = bound(
+        (active, slope, middle_turned, unit_second, rstd_second, two_turned), way_down
+    )
+    way_down.step()
+
     active_sib = swap(active, CORE_BIT)
-    way_down.step(active)
-    part_down = way_down.finish()
-    block_out = mlp_down(spot, active, down_turned, part_down, middle.T, bias_down.reshape(-1, 1))
-
     give, keep_down = turned_weight_grads(
-        spot, *grad_left, active, tie(active_sib, block_out), width // 4, "down_grads"
-    )
-    sum_down = Steps(reduced(keep_down, give, bits))
-
-    grad_hidden, grad_normed_two, sum_hidden = mlp_back(
-        spot, tie(grad_out, give), slope, down_turned, part_down, up_weight, part_up
-    )
+        spot, *grad_left, tie(active, way_down.latest), active_sib, width // 4, "down_grads"
+    )
+    sum_down = Steps(reduced(keep_down, give, bits, True))
+    part_down = way_down.finish(give)
+    block_out = mlp_down(
+        spot, tie(active, give), down_turned, part_down, middle_turned, bias_down
+    )
+
+    two_left = for_cores(two_turned)
+    context_left = for_cores(context_t)
+    results = mlp_back(
+        spot, tie(grad_out, block_out, *two_left, *context_left), slope, unit_second, rstd_second,
+        gain_second.reshape(1, -1), full_out, down_turned, part_down, up_weight, part_up,
+    )
+    grad_hidden, grad_middle, grad_branch, grad_context, sum_hidden, sum_rows = bound(results, sum_down)
+    sum_down.step()
     hidden_sib = swap(grad_hidden, CORE_BIT)
-    grad_middle = norm_pull(grad_normed_two, unit_second, rstd_second, gain_second)
-    grad_middle = grad_middle + grad_out.astype(jnp.float32)
-    grad_branch = low(grad_middle)
     branch_sib = swap(grad_branch, CORE_BIT)
-    grad_context = low(dot_nt(grad_branch, full_out))
-    two_left = for_cores(normed_two.T)
+    give_out, keep_out = weight_grads(
+        spot, *context_left, grad_branch, branch_sib, width, context_left[0].shape[1], grad_branch.shape[1],
+        "out_grads"
+    )
+    sum_out = Steps(reduced(keep_out, give_out, bits))
     give, keep_up = weight_grads(
-        spot, *two_left, grad_hidden, hidden_sib, two_left[0].shape[1], 2 * CHUNK, "up_grads"
-    )
+        spot, *two_left, grad_hidden, tie(hidden_sib, give_out), grad_hidden.shape[1], two_left[0].shape[1],
+        2 * CHUNK, "up_grads"
+    )
+    give, keep_up = bound((give, keep_up), sum_down)
     sum_up = Steps(reduced(keep_up, give, bits))
-    context_left = for_cores(context_t)
-    give_out, keep_out = weight_grads(
-        spot, *context_left, grad_branch, branch_sib, context_left[0].shape[1], width, "out_grads"
-    )
-    sum_down.step(give, give_out, grad_context)
-    grad_context = tie(grad_context, give, give_out, sum_down.latest)
+    sum_down.step()
+    grad_context = tie(grad_context, give, sum_down.latest)
 
     grad_q, grad_k, grad_v = attention_backward(
         spot, queries, keys, values, grad_context, context, lse, 1, span
     )
-    sum_down.step(grad_q)
+    grad_q, grad_k, grad_v = bound((grad_q, grad_k, grad_v), sum_down, sum_out)
+    sum_down.step()
+    sum_out.step()
     rights = []
     for part in (grad_q, grad_k, grad_v):
         rights += [part, swap(part, CORE_BIT)]
-    rights[0] = tie(grad_q, sum_down.latest)
-    give, keep_qkv = qkv_weight_grads(spot, *normed_left, *rights)
-    sum_down.step(give)
-    sum_up.step(give)
+    mine, theirs = input_grads(
+        spot, full_q, full_k, full_v, tie(grad_q, sum_down.latest, sum_out.latest), grad_k, grad_v
+    )
+    mine, theirs = bound((mine, theirs), sum_up, sum_down, sum_out)
+    sum_up.step()
+    sum_down.step()
+    sum_out.step()
+    rights[0] = tie(grad_q, sum_down.latest, sum_out.latest, sum_up.latest, theirs)
+    give, keep_qkv = qkv_weight_grads(spot, width, *normed_left, *rights)
+    give, keep_qkv = bound((give, keep_qkv), sum_out)
+    sum_out.step()
     sum_qkv = Steps(reduced(keep_qkv, give, bits))
 
-    mine, theirs = input_grads(
-        spot, full_q, full_k, full_v, tie(grad_q, give, sum_down.latest, sum_up.latest), grad_k, grad_v
-    )
-    sum_out = Steps(reduced(keep_out, tie(give_out, mine), bits))
-    grad_normed = mine + cross(theirs).astype(jnp.float32)
+    other_part = cross(tie(theirs, sum_qkv.got))
+    grad_middle, sum_rows, sum_hidden = bound((grad_middle, sum_rows, sum_hidden, give))[:3]
+
     unit_first, rstd_first = centred_down(own_turned.astype(jnp.float32))
-    scaled = grad_normed * gain_first[:, None]
-    pulled = rstd_first * (
-        scaled - jnp.mean(scaled, axis=0, keepdims=True)
-        - unit_first * jnp.mean(scaled * unit_first, axis=0, keepdims=True)
-    )
-    grad_tokens = low(pulled + grad_middle.T)
-
+    unit_other, _ = centred_down(other_turned.astype(jnp.float32))
+    theirs_float = theirs.astype(jnp.float32)
     sums = (
-        jnp.sum(grad_normed * unit_first, axis=1),
-        jnp.sum(grad_normed, axis=1),
-        row_sum(grad_q),
-        row_sum(grad_v),
-        row_sum(grad_branch),
-        row_sum(grad_normed_two * unit_second),
-        row_sum(grad_normed_two),
+        jnp.sum(mine * unit_first, axis=1) + jnp.sum(theirs_float * unit_other, axis=1),
+        jnp.sum(mine, axis=1) + jnp.sum(theirs_float, axis=1),
+        row_sum(grad_q)[:width],
+        row_sum(grad_v)[:width],
+        sum_rows[2],
+        sum_rows[0],
+        sum_rows[1],
         sum_hidden.reshape(-1),
-        row_sum(grad_out),
-    )
-    packed = total_of(jnp.concatenate([item.reshape(2, -1) for item in sums], axis=1))
-    outs, at = [], 0
-    for item in sums:
-        size = item.shape[0] // 2
-        outs.append(packed[at : at + size])
-        at += size
+        jnp.sum(grad_turned.astype(jnp.float32), axis=1),
+    )
+    small = jnp.stack([item.reshape(2, -1) for item in sums[:7] + sums[8:]], axis=1)
+    small = jnp.concatenate([small, sums[7].reshape(2, -1, width // 2)], axis=1)
+    sum_small = Steps(vector_sum(small))
+    grad_tokens = token_grads(
+        spot, mine, other_part, own_turned, gain_first.reshape(-1, 1), grad_middle
+    )
+
+    chains = {"d": sum_down, "u": sum_up, "q": sum_qkv, "o": sum_out, "v": sum_small}
+    done = {}
+    latest = give
+    for name in TAIL:
+        if name == "t":
+            latest = grad_tokens
+            continue
+        chain = chains[name]
+        try:
+            chain.step(latest)
+            latest = chain.latest
+        except StopIteration as end:
+            done[name] = latest = end.value
+    vectors_out = done["v"]
+    outs = [vectors_out[i] for i in range(7)] + [vectors_out[8:].reshape(-1), vectors_out[7]]
 
     return (
         block_out.T.reshape(1, span, width),
         grad_tokens.T.reshape(1, span, width),
-        sum_qkv.finish(), sum_out.finish(), sum_up.finish(), sum_down.finish().T,
+        done["q"], done["o"], done["u"], done["d"].T,
         *outs,
     )
 
@@ -975,6 +1101,7 @@
     grad_q, grad_k, grad_v = attention_backward(
         spot, queries, keys, values, grad_context, context, lse, seqs, span
     )
+    grad_q, grad_k, grad_v = grad_q[:, :width], grad_k[:, :width], grad_v[:, :width]
     normed_both = jnp.concatenate([normed_all, normed_sib], axis=0)
     own_both = jnp.concatenate([normed, own_rows(normed_sib)], axis=0)
     third = width // 2

time: 645 us -> 576 us (0.89)
  waiting for transfers between devices: 200 us -> 164 us
  local copies, waits for them, and re-layouts: 64.9 us -> 51.2 us
  Pallas kernels: 177 us -> 190 us
  other arithmetic: 97.7 us -> 84.8 us
  starting transfers between devices: 76.2 us -> 63.9 us
  matrix products: 17.3 us -> 10.8 us
    ppermute x12 -> x13, waiting for transfers between devices: 82 us -> 43.4 us  [cross(): return lax.ppermute(values, 'shard', [(0, 1), (1, 0)])]
    ppermute x50, starting transfers between devices: 69.2 us -> 51.6 us  [swap(): return lax.ppermute(values, 'replica', [(i, i ^ bit) for i in range(size)])]
    pallas_call x4 -> x0, local copies, waits for them, and re-layouts: 14 us -> none  [the longest x3 10.5 us: attention_backward(): pl.pallas_call(functools.partial(backward_kernel, span=span, width=width)...]
    pallas_call x2 -> x3, Pallas kernels: 39.4 us -> 52.3 us  [the longest x1 26 us: mlp_back(): _call(back_kernel, 'mlp_back', _vmem(6) + [any_spec] * 4, [jax.ShapeDtype...]
    ppermute x4 -> x0, local copies, waits for them, and re-layouts: 12.2 us -> none  [swap(): return lax.ppermute(values, 'replica', [(i, i ^ bit) for i in range(size)])]
    unnamed x130 -> x134, local copies, waits for them, and re-layouts: 5.69 us -> 15.6 us
    reduce_sum x5 -> x2, other arithmetic: 11 us -> 2.34 us  [row_sum(): return jnp.sum(values.astype(jnp.float32), axis=0)]
    convert_element_type x19 -> x18, other arithmetic: 20 us -> 17.9 us  [low(): return values.astype(jnp.bfloat16)]
  transfers between devices with their start and end apart: 62 -> 63, of which waited for: 29 -> 23; matrix products, arithmetic and copies ran while one was open for 24% -> 22% of each run, Pallas kernels for 22% -> 34%
where the time goes in v3:
time: 576 us; the launch traced here: 566 us
  Pallas kernels  190 us (33%)
  waiting for transfers between devices  164 us (28%)
  other arithmetic  84.8 us (15%)
  starting transfers between devices  63.9 us (11%)
  local copies, waits for them, and re-layouts  51.2 us (9%)
  matrix products  10.8 us (2%)
    ppermute x50, waiting for transfers between devices, swap(): return lax.ppermute(values, 'replica', [(i, i ^ bit) for i in range(size)])  120 us
    ppermute x50, starting transfers between devices, swap(): return lax.ppermute(values, 'replica', [(i, i ^ bit) for i in range(size)])  51.6 us
    ppermute x13, waiting for transfers between devices, cross(): return lax.ppermute(values, 'shard', [(0, 1), (1, 0)])  43.4 us
    pallas_call x1, Pallas kernels, attention_backward(): pl.pallas_call(functools.partial(backward_kernel, span=span, width=width)...  37.6 us
    pallas_call x1, Pallas kernels, attention_forward(): pl.pallas_call(functools.partial(forward_kernel, span=span, width=width),...  31.7 us
    select_n x38, other arithmetic, choose(): return jnp.where(flag, left, right)  26.8 us
    pallas_call x1, Pallas kernels, mlp_back(): _call(back_kernel, 'mlp_back', _vmem(6) + [any_spec] * 4, [jax.ShapeDtype...  26 us
    pallas_call x1, Pallas kernels, mlp_up(): _call(up_kernel, 'mlp_up', _vmem(5) + [any_spec] * 2, [jax.ShapeDtypeStru...  20.2 us
  transfers between devices with their start and end apart: 63, of which 23 were waited for; matrix products, arithmetic and copies ran while one was open for 22% of the time, Pallas kernels for 34%

profile of v3, /device:TPU:27, one launch (start us, length us, event | category | flops | bytes accessed | tf_op | source)
XLA Modules:
  0.0 566.0 jit_solution(10091675071777600492)
XLA Ops:
  8.6 5.2 collective-permute-done
  14.1 2.4 copy.44
  20.7 7.4 %collective-permute-done.4 = bf16[72,3264]{1,0:T(8,128)(2,1)S(1)} collective-permute-done((bf16[72,3264]{1,0:T(8,128)(2,1)S(1)}, bf16[72,3264]{1,0:T(8,128)(2,1)S(1)}, u32[]{:S(2)}, u32[]{:S(2)}) %collective-permute-start.4) | collective-permute-done | bytes 470048 | tf_op jit(solution)/shard_map/ppermute | solution.py:288
  29.5 11.2 %collective-permute-done.1 = bf16[1088,512]{1,0:T(8,128)(2,1)S(1)} collective-permute-done((bf16[1088,512]{1,0:T(8,128)(2,1)S(1)}, bf16[1088,512]{1,0:T(8,128)(2,1)S(1)}, u32[]{:S(2)}, u32[]{:S(2)}) %collective-permute-start.1) | collective-permute-done | bytes 1114144 | tf_op jit(solution)/shard_map/ppermute | solution.py:292
  45.5 2.5 collective-permute-done.5
  48.3 4.0 collective-permute-start.6
  61.4 6.8 %pad_maximum_fusion.2 = (bf16[1088,1088]{1,0:T(8,128)(2,1)S(1)}, bf16[1088,1088]{1,0:T(8,128)(2,1)S(1)}, bf16[1088,1088]{1,0:T(8,128)(2,1)S(1)}) fusion(bf16[544,3264]{1,0:T(8,128)(2,1)S(1)} %get-tuple-element.336, bf16[544,3264]{1,0:T(8,128)(2,1)S(1)} %get-tuple-element.337), kind=kLoop, calls=%fused_computation.41 | loop fusion | flops 14204928 | bytes 14204928 | tf_op jit(solution)/shard_map/concatenate | solution.py:310
  69.8 4.8 add_convert_fusion.2.v_ref
  75.0 4.0 convolution_convert_fusion.k_ref
  86.7 8.4 %collective-permute-start.14 = (bf16[288,1088]{1,0:T(8,128)(2,1)}, bf16[288,1088]{1,0:T(8,128)(2,1)}, u32[]{:S(2)}, u32[]{:S(2)}) collective-permute-start(bf16[288,1088]{1,0:T(8,128)(2,1)} %constant_dynamic-update-slice_fusion.6), channel_id=1, source_target_pairs={{0,2},{2,0},{4,6},{6,4},{8,10},{10,8},{12,14},{14,12},{16,18},{18,... | collective-permute-start | bytes 1880072 | tf_op jit(solution)/shard_map/ppermute | solution.py:288
  96.4 2.4 copy.48.x_ref
  98.8 31.7 %attention_forward.1 = (bf16[512,1088]{1,0:T(8,128)(2,1)S(1)}, bf16[1088,512]{1,0:T(8,128)(2,1)S(1)}, f32[9,2,512]{2,1,0:T(2,128)S(1)}) custom-call(s32[1]{0:T(128)} %bitcast.pos_ref, bf16[512,1088]{1,0:T(8,128)(2,1)S(1)} %fusion.7.q_ref, bf16[1024,1088]{1,0:T(8,128)(2,1)S(1)} %convolution_convert_fusion.k_ref, bf16[1024,1088]{1,0:T(8,128)(2,1)} %add_convert_fusion.2.v_ref), custom_call_target="tpu_custom_call" | custom-call | flops 1 | bytes 1 | tf_op jit(solution)/shard_map/attention_forward/pallas_call | solution.py:182
  140.7 2.8 pad_maximum_fusion.got_ref.up_got
  143.5 20.2 %mlp_up.1 = (bf16[512,4352]{1,0:T(8,128)(2,1)}, bf16[512,4352]{1,0:T(8,128)(2,1)}, f32[1088,512]{1,0:T(8,128)}, f32[512,1088]{1,0:T(8,128)}, f32[512,1]{1,0:T(8,128)}, /*index=5*/bf16[1088,512]{1,0:T(8,128)(2,1)}) custom-call(s32[1]{0:T(128)} %bitcast.pos_ref, bf16[512,1088]{1,0:T(8,128)(2,1)} %copy-done.5, bf16[1088,1088]{1,0:T(8,128)(2,1)} %pad_maximum_fusion.3.out_w_ref, ...), custom_call_target="tpu_custom_call" | custom-call | flops 1 | bytes 1 | tf_op jit(solution)/shard_map/mlp_up/pallas_call | solution.py:424
  165.9 2.4 dynamic-slice_bitcast_fusion.7
  172.4 3.1 collective-permute-done.17.left_sib
  175.4 11.7 %down_grads.1 = (bf16[544,2176]{1,0:T(8,128)(2,1)}, bf16[544,2176]{1,0:T(8,128)(2,1)}) custom-call(s32[1]{0:T(128)} %bitcast.pos_ref, bf16[544,512]{1,0:T(8,128)(2,1)} %get-tuple-element.385.left_own, bf16[544,512]{1,0:T(8,128)(2,1)} %collective-permute-done.17.left_sib, bf16[512,4352]{1,0:T(8,128)(2,1)} %get-tuple-element.226.right_own.act_ref, ...), custom_call_target="tpu_custom_call" | custom-call | flops 1 | bytes 1 | tf_op jit(solution)/shard_map/down_grads/pallas_call | solution.py:600
  187.1 3.2 fusion.29
  195.6 11.3 %mlp_down.1 = bf16[1088,512]{1,0:T(8,128)(2,1)} custom-call(s32[1]{0:T(128)} %bitcast.pos_ref, bf16[512,4352]{1,0:T(8,128)(2,1)} %get-tuple-element.226.right_own.act_ref, bf16[1088,2176]{1,0:T(8,128)(2,1)} %bitcast.78, bf16[1088,2176]{1,0:T(8,128)(2,1)} %constant_dynamic-update-slice_fusion.16.got_ref.down_got, f32[1088,512]{1,0:T(8,128)} %get-tuple-element.230.middle_ref, ...), custom_call_target="tpu_custom_call" | custom-call | flops 1 | bytes 1 | tf_op jit(solution)/shard_map/mlp_down/pallas_call | solution.py:456
  207.7 26.0 %mlp_back.1 = (bf16[512,4352]{1,0:T(8,128)(2,1)}, f32[512,1088]{1,0:T(8,128)}, bf16[512,1152]{1,0:T(8,128)(2,1)}, bf16[512,1088]{1,0:T(8,128)(2,1)}, f32[1,4352]{1,0:T(1,128)}, /*index=5*/f32[8,1088]{1,0:T(8,128)}) custom-call(s32[1]{0:T(128)} %bitcast.pos_ref, bf16[512,1088]{1,0:T(8,128)(2,1)} %bitcast.80, bf16[512,4352]{1,0:T(8,128)(2,1)} %get-tuple-element.234.slope_ref, ...), custom_call_target="tpu_custom_call" | custom-call | flops 1 | bytes 1 | tf_op jit(solution)/shard_map/mlp_back/pallas_call | solution.py:532
  238.7 4.6 collective-permute-done.24.right_sib
  244.3 4.7 out_grads.1
  249.0 11.9 %up_grads.1 = (bf16[272,4352]{1,0:T(8,128)(2,1)}, bf16[272,4352]{1,0:T(8,128)(2,1)}) custom-call(s32[1]{0:T(128)} %bitcast.pos_ref, bf16[2,272,512]{2,1,0:T(8,128)(2,1)} %get-tuple-element.383.left_own, bf16[2,272,512]{2,1,0:T(8,128)(2,1)} %copy-done.50, bf16[512,4352]{1,0:T(8,128)(2,1)} %get-tuple-element.244.right_own, ...), custom_call_target="tpu_custom_call" | custom-call | flops 1 | bytes 1 | tf_op jit(solution)/shard_map/up_grads/pallas_call | solution.py:567
  271.8 37.6 %attention_backward.1 = (bf16[512,1152]{1,0:T(8,128)(2,1)S(1)}, bf16[1024,1152]{1,0:T(8,128)(2,1)}, bf16[1024,1152]{1,0:T(8,128)(2,1)}) custom-call(s32[1]{0:T(128)} %bitcast.pos_ref, bf16[512,1088]{1,0:T(8,128)(2,1)S(1)} %copy-done.4, bf16[1024,1088]{1,0:T(8,128)(2,1)} %copy-done.2, bf16[1024,1088]{1,0:T(8,128)(2,1)} %add_convert_fusion.2.v_ref, ...), custom_call_target="tpu_custom_call" | custom-call | flops 1 | bytes 1 | tf_op jit(solution)/shard_map/attention_backward/pallas_call | solution.py:212
  314.9 13.7 %input_grads.1 = (f32[1088,512]{1,0:T(8,128)}, bf16[1088,512]{1,0:T(8,128)(2,1)}) custom-call(s32[1]{0:T(128)} %bitcast.pos_ref, bf16[1088,1088]{1,0:T(8,128)(2,1)} %copy-done.27, bf16[1088,1088]{1,0:T(8,128)(2,1)} %copy-done.29, bf16[1088,1088]{1,0:T(8,128)(2,1)} %copy-done.28, bf16[512,1152]{1,0:T(8,128)(2,1)} %copy-done, ...), custom_call_target="tpu_custom_call" | custom-call | flops 1 | bytes 1 | tf_op jit(solution)/shard_map/input_grads/pallas_call | solution.py:662
  331.5 5.0 collective-permute-done.28
  336.5 2.9 add_convert_fusion
  349.7 14.7 %qkv_weight_grads.1 = (bf16[272,3264]{1,0:T(8,128)(2,1)}, bf16[272,3264]{1,0:T(8,128)(2,1)}) custom-call(s32[1]{0:T(128)} %bitcast.pos_ref, bf16[2,272,1024]{2,1,0:T(8,128)(2,1)} %get-tuple-element.363.left_own, bf16[2,272,1024]{2,1,0:T(8,128)(2,1)} %collective-permute-done.31.left_sib, bf16[512,1152]{1,0:T(8,128)(2,1)} %copy-done, ...), custom_call_target="tpu_custom_call" | custom-call | flops 1 | bytes 1 | tf_op jit(solution)/shard_map/qkv_weight_grads/pallas_call | solution.py:639
  365.4 2.4 collective-permute-start.39
  374.6 7.5 %collective-permute-done.40 = bf16[136,2176]{1,0:T(8,128)(2,1)S(1)} collective-permute-done((bf16[136,2176]{1,0:T(8,128)(2,1)}, bf16[136,2176]{1,0:T(8,128)(2,1)S(1)}, u32[]{:S(2)}, u32[]{:S(2)}) %collective-permute-start.40) | collective-permute-done | bytes 591904 | tf_op jit(solution)/shard_map/ppermute | solution.py:288
  387.9 19.2 %collective-permute-done.36 = bf16[272,3264]{1,0:T(8,128)(2,1)} collective-permute-done((bf16[272,3264]{1,0:T(8,128)(2,1)}, bf16[272,3264]{1,0:T(8,128)(2,1)}, u32[]{:S(2)}, u32[]{:S(2)}) %collective-permute-start.36) | collective-permute-done | bytes 1775648 | tf_op jit(solution)/shard_map/ppermute | solution.py:292
  412.8 17.7 %collective-permute-done.42 = bf16[136,3264]{1,0:T(8,128)(2,1)S(1)} collective-permute-done((bf16[136,3264]{1,0:T(8,128)(2,1)S(1)}, bf16[136,3264]{1,0:T(8,128)(2,1)S(1)}, u32[]{:S(2)}, u32[]{:S(2)}) %collective-permute-start.42) | collective-permute-done | bytes 887840 | tf_op jit(solution)/shard_map/ppermute | solution.py:288
  432.6 6.1 %token_grads.1 = bf16[1088,512]{1,0:T(8,128)(2,1)} custom-call(s32[1]{0:T(128)} %bitcast.pos_ref, f32[1088,512]{1,0:T(8,128)} %get-tuple-element.268.mine_ref, bf16[1088,512]{1,0:T(8,128)(2,1)} %copy-done.45, bf16[1088,512]{1,0:T(8,128)(2,1)} %bitcast.73, f32[1088,1]{1,0:T(8,128)} %copy.55.gain_ref, f32[512,1088]{1,0:T(8,128)} %get-tuple-element.282.middle_ref), custom_call_target="tpu_custom_call" | custom-call | flops 1 | bytes 1 | tf_op jit(solution)/shard_map/token_grads/pallas_call | solution.py:686
  444.5 6.6 %collective-permute-done.44 = bf16[72,3264]{1,0:T(8,128)(2,1)} collective-permute-done((bf16[72,3264]{1,0:T(8,128)(2,1)}, bf16[72,3264]{1,0:T(8,128)(2,1)}, u32[]{:S(2)}, u32[]{:S(2)}) %collective-permute-start.44) | collective-permute-done | bytes 470048 | tf_op jit(solution)/shard_map/ppermute | solution.py:288
  452.7 13.5 %collective-permute-done.49 = bf16[72,4352]{1,0:T(8,128)(2,1)S(1)} collective-permute-done((bf16[72,4352]{1,0:T(8,128)(2,1)S(1)}, bf16[72,4352]{1,0:T(8,128)(2,1)S(1)}, u32[]{:S(2)}, u32[]{:S(2)}) %collective-permute-start.49) | collective-permute-done | bytes 626720 | tf_op jit(solution)/shard_map/ppermute | solution.py:288
  466.4 13.1 %collective-permute-done.48 = bf16[72,3264]{1,0:T(8,128)(2,1)S(1)} collective-permute-done((bf16[72,3264]{1,0:T(8,128)(2,1)S(1)}, bf16[72,3264]{1,0:T(8,128)(2,1)S(1)}, u32[]{:S(2)}, u32[]{:S(2)}) %collective-permute-start.48) | collective-permute-done | bytes 470048 | tf_op jit(solution)/shard_map/ppermute | solution.py:288
  481.3 9.5 %collective-permute-done.53 = bf16[72,4352]{1,0:T(8,128)(2,1)S(1)} collective-permute-done((bf16[72,4352]{1,0:T(8,128)(2,1)S(1)}, bf16[72,4352]{1,0:T(8,128)(2,1)S(1)}, u32[]{:S(2)}, u32[]{:S(2)}) %collective-permute-start.53) | collective-permute-done | bytes 626720 | tf_op jit(solution)/shard_map/ppermute | solution.py:288
  493.4 3.0 collective-permute-start.56
  496.4 4.7 collective-permute-done.50
  504.9 12.1 %collective-permute-done.58 = bf16[136,4352]{1,0:T(8,128)(2,1)S(1)} collective-permute-done((bf16[136,4352]{1,0:T(8,128)(2,1)S(1)}, bf16[136,4352]{1,0:T(8,128)(2,1)S(1)}, u32[]{:S(2)}, u32[]{:S(2)}) %collective-permute-start.58) | collective-permute-done | bytes 1183776 | tf_op jit(solution)/shard_map/ppermute | solution.py:288
  519.2 4.8 collective-permute-start.61
  524.0 12.4 %collective-permute-done.55 = bf16[136,3264]{1,0:T(8,128)(2,1)S(1)} collective-permute-done((bf16[136,3264]{1,0:T(8,128)(2,1)S(1)}, bf16[136,3264]{1,0:T(8,128)(2,1)S(1)}, u32[]{:S(2)}, u32[]{:S(2)}) %collective-permute-start.55) | collective-permute-done | bytes 887840 | tf_op jit(solution)/shard_map/ppermute | solution.py:288
  539.1 2.6 collective-permute-start.60
  546.2 2.6 broadcast_select_fusion.7
  548.8 4.4 fusion.19
  553.2 2.5 broadcast_select_fusion.5
  555.7 4.4 maximum_convert_fusion.1
  562.3 3.5 maximum_convert_fusion.2
  (384 shorter events, 144.4 us)
Async XLA Ops:
  16.5 24.2 %collective-permute-start.1 = (bf16[1088,512]{1,0:T(8,128)(2,1)S(1)}, bf16[1088,512]{1,0:T(8,128)(2,1)S(1)}, u32[]{:S(2)}, u32[]{:S(2)}) collective-permute-start(bf16[1088,512]{1,0:T(8,128)(2,1)S(1)} %bitcast.74), channel_id=1, source_target_pairs={{0,1},{1,0},{2,3},{3,2},{4,5},{5,4},{6,7},{7,6},{8,9},{9,8},{10,11... | collective-permute-start | bytes 3342344 | tf_op jit(solution)/shard_map/ppermute | solution.py:292
  28.2 19.8 %collective-permute-start.5 = (bf16[144,3264]{1,0:T(8,128)(2,1)S(1)}, bf16[144,3264]{1,0:T(8,128)(2,1)S(1)}, u32[]{:S(2)}, u32[]{:S(2)}) collective-permute-start(bf16[144,3264]{1,0:T(8,128)(2,1)S(1)} %constant_dynamic-update-slice_fusion), channel_id=1, source_target_pairs={{0,4},{2,6},{4,0},{6,2},{8,12},{10,14},{12,8},{14,10},{16,20},{18,... | collective-permute-start | bytes 2820104 | tf_op jit(solution)/shard_map/ppermute | solution.py:288
  44.6 23.6 %collective-permute-start.3 = (bf16[72,1088]{1,0:T(8,128)(2,1)S(1)}, bf16[72,1088]{1,0:T(8,128)(2,1)S(1)}, u32[]{:S(2)}, u32[]{:S(2)}) collective-permute-start(bf16[72,1088]{1,0:T(8,128)(2,1)S(1)} %constant_dynamic-slice_fusion.2), channel_id=1, source_target_pairs={{0,1},{1,0},{2,3},{3,2},{4,5},{5,4},{6,7},{7,6},{8,9},{9,8},{10,11... | collective-permute-start | bytes 470024 | tf_op jit(solution)/shard_map/ppermute | solution.py:292
  56.5 18.1 %collective-permute-start.10 = (bf16[136,2176]{1,0:T(8,128)(2,1)S(1)}, bf16[136,2176]{1,0:T(8,128)(2,1)}, u32[]{:S(2)}, u32[]{:S(2)}) collective-permute-start(bf16[136,2176]{1,0:T(8,128)(2,1)S(1)} %constant_dynamic-slice_fusion), channel_id=1, source_target_pairs={{0,1},{1,0},{2,3},{3,2},{4,5},{5,4},{6,7},{7,6},{8,9},{9,8},{10,11... | collective-permute-start | bytes 1775624 | tf_op jit(solution)/shard_map/ppermute | solution.py:292
  86.6 44.0 %collective-permute-start.12 = (bf16[144,4352]{1,0:T(8,128)(2,1)}, bf16[144,4352]{1,0:T(8,128)(2,1)}, u32[]{:S(2)}, u32[]{:S(2)}) collective-permute-start(bf16[144,4352]{1,0:T(8,128)(2,1)} %constant_dynamic-update-slice_fusion.8), channel_id=1, source_target_pairs={{0,8},{2,10},{4,12},{6,14},{8,0},{10,2},{12,4},{14,6},{16,24},{18,... | collective-permute-start | bytes 3760136 | tf_op jit(solution)/shard_map/ppermute | solution.py:288
  86.7 43.8 %collective-permute-start.14 = (bf16[288,1088]{1,0:T(8,128)(2,1)}, bf16[288,1088]{1,0:T(8,128)(2,1)}, u32[]{:S(2)}, u32[]{:S(2)}) collective-permute-start(bf16[288,1088]{1,0:T(8,128)(2,1)} %constant_dynamic-update-slice_fusion.6), channel_id=1, source_target_pairs={{0,2},{2,0},{4,6},{6,4},{8,10},{10,8},{12,14},{14,12},{16,18},{18,... | collective-permute-start | bytes 1880072 | tf_op jit(solution)/shard_map/ppermute | solution.py:288
  95.1 35.4 %collective-permute-start.13 = (bf16[136,2176]{1,0:T(8,128)(2,1)}, bf16[136,2176]{1,0:T(8,128)(2,1)}, u32[]{:S(2)}, u32[]{:S(2)}) collective-permute-start(bf16[136,2176]{1,0:T(8,128)(2,1)} %collective-permute-done.10), channel_id=1, source_target_pairs={{0,4},{2,6},{4,0},{6,2},{8,12},{10,14},{12,8},{14,10},{16,20},{18,... | collective-permute-start | bytes 1775624 | tf_op jit(solution)/shard_map/ppermute | solution.py:288
  136.7 27.4 %collective-permute-start.16 = (bf16[272,2176]{1,0:T(8,128)(2,1)S(1)}, bf16[272,2176]{1,0:T(8,128)(2,1)S(1)}, u32[]{:S(2)}, u32[]{:S(2)}) collective-permute-start(bf16[272,2176]{1,0:T(8,128)(2,1)S(1)} %constant_dynamic-update-slice_fusion.12), channel_id=1, source_target_pairs={{0,8},{2,10},{4,12},{6,14},{8,0},{10,2},{12,4},{14,6},{16,24},{18,... | collective-permute-start | bytes 3551240 | tf_op jit(solution)/shard_map/ppermute | solution.py:288
  165.8 24.5 %collective-permute-start.19 = (bf16[544,2176]{1,0:T(8,128)(2,1)S(1)}, bf16[544,2176]{1,0:T(8,128)(2,1)}, u32[]{:S(2)}, u32[]{:S(2)}) collective-permute-start(bf16[544,2176]{1,0:T(8,128)(2,1)S(1)} %constant_dynamic-update-slice_fusion.14), channel_id=1, source_target_pairs={{0,2},{2,0},{4,6},{6,4},{8,10},{10,8},{12,14},{14,12},{16,18},{18,... | collective-permute-start | bytes 7102472 | tf_op jit(solution)/shard_map/ppermute | solution.py:288
  170.8 36.0 %collective-permute-start.21 = (bf16[2,272,512]{2,1,0:T(8,128)(2,1)}, bf16[2,272,512]{2,1,0:T(8,128)(2,1)S(1)}, u32[]{:S(2)}, u32[]{:S(2)}) collective-permute-start(bf16[2,272,512]{2,1,0:T(8,128)(2,1)} %get-tuple-element.380), channel_id=1, source_target_pairs={{0,2},{2,0},{4,6},{6,4},{8,10},{10,8},{12,14},{14,12},{16,18},{18,... | collective-permute-start | bytes 1671176 | tf_op jit(solution)/shard_map/ppermute | solution.py:288
  172.3 34.6 %collective-permute-start.20 = (bf16[2,272,512]{2,1,0:T(8,128)(2,1)S(1)}, bf16[2,272,512]{2,1,0:T(8,128)(2,1)S(1)}, u32[]{:S(2)}, u32[]{:S(2)}) collective-permute-start(bf16[2,272,512]{2,1,0:T(8,128)(2,1)S(1)} %get-tuple-element.382), channel_id=1, source_target_pairs={{0,2},{2,0},{4,6},{6,4},{8,10},{10,8},{12,14},{14,12},{16,18},{18,... | collective-permute-start | bytes 1671176 | tf_op jit(solution)/shard_map/ppermute | solution.py:288
  190.3 43.4 %collective-permute-start.22 = (bf16[272,2176]{1,0:T(8,128)(2,1)}, bf16[272,2176]{1,0:T(8,128)(2,1)}, u32[]{:S(2)}, u32[]{:S(2)}) collective-permute-start(bf16[272,2176]{1,0:T(8,128)(2,1)} %get-tuple-element.359), channel_id=1, source_target_pairs={{0,1},{1,0},{2,3},{3,2},{4,5},{5,4},{6,7},{7,6},{8,9},{9,8},{10,11... | collective-permute-start | bytes 3551240 | tf_op jit(solution)/shard_map/ppermute | solution.py:292
  234.2 28.3 %collective-permute-start.25 = (bf16[272,2176]{1,0:T(8,128)(2,1)}, bf16[272,2176]{1,0:T(8,128)(2,1)}, u32[]{:S(2)}, u32[]{:S(2)}) collective-permute-start(bf16[272,2176]{1,0:T(8,128)(2,1)} %get-tuple-element.358), channel_id=1, source_target_pairs={{0,1},{1,0},{2,3},{3,2},{4,5},{5,4},{6,7},{7,6},{8,9},{9,8},{10,11... | collective-permute-start | bytes 3551240 | tf_op jit(solution)/shard_map/ppermute | solution.py:292
  264.9 44.5 %collective-permute-start.26 = (bf16[272,2176]{1,0:T(8,128)(2,1)S(1)}, bf16[272,2176]{1,0:T(8,128)(2,1)S(1)}, u32[]{:S(2)}, u32[]{:S(2)}) collective-permute-start(bf16[272,2176]{1,0:T(8,128)(2,1)S(1)} %broadcast_select_fusion.23), channel_id=1, source_target_pairs={{0,4},{2,6},{4,0},{6,2},{8,12},{10,14},{12,8},{14,10},{16,20},{18,... | collective-permute-start | bytes 3551240 | tf_op jit(solution)/shard_map/ppermute | solution.py:288
  268.8 78.0 %collective-permute-start.31 = (bf16[2,272,1024]{2,1,0:T(8,128)(2,1)}, bf16[2,272,1024]{2,1,0:T(8,128)(2,1)}, u32[]{:S(2)}, u32[]{:S(2)}) collective-permute-start(bf16[2,272,1024]{2,1,0:T(8,128)(2,1)} %get-tuple-element.362), channel_id=1, source_target_pairs={{0,2},{2,0},{4,6},{6,4},{8,10},{10,8},{12,14},{14,12},{16,18},{18,... | collective-permute-start | bytes 3342344 | tf_op jit(solution)/shard_map/ppermute | solution.py:288
  269.8 39.6 %collective-permute-start.27 = (bf16[272,1088]{1,0:T(8,128)(2,1)S(1)}, bf16[272,1088]{1,0:T(8,128)(2,1)S(1)}, u32[]{:S(2)}, u32[]{:S(2)}) collective-permute-start(bf16[272,1088]{1,0:T(8,128)(2,1)S(1)} %copy-done.61), channel_id=1, source_target_pairs={{0,1},{1,0},{2,3},{3,2},{4,5},{5,4},{6,7},{7,6},{8,9},{9,8},{10,11... | collective-permute-start | bytes 1775624 | tf_op jit(solution)/shard_map/ppermute | solution.py:292
  271.7 64.8 %collective-permute-start.28 = (bf16[272,4352]{1,0:T(8,128)(2,1)}, bf16[272,4352]{1,0:T(8,128)(2,1)}, u32[]{:S(2)}, u32[]{:S(2)}) collective-permute-start(bf16[272,4352]{1,0:T(8,128)(2,1)} %get-tuple-element.250), channel_id=1, source_target_pairs={{0,1},{1,0},{2,3},{3,2},{4,5},{5,4},{6,7},{7,6},{8,9},{9,8},{10,11... | collective-permute-start | bytes 7102472 | tf_op jit(solution)/shard_map/ppermute | solution.py:292
  310.8 20.2 %collective-permute-start.29 = (bf16[136,2176]{1,0:T(8,128)(2,1)}, bf16[136,2176]{1,0:T(8,128)(2,1)}, u32[]{:S(2)}, u32[]{:S(2)}) collective-permute-start(bf16[136,2176]{1,0:T(8,128)(2,1)} %broadcast_select_fusion.43), channel_id=1, source_target_pairs={{0,8},{2,10},{4,12},{6,14},{8,0},{10,2},{12,4},{14,6},{16,24},{18,... | collective-permute-start | bytes 1775624 | tf_op jit(solution)/shard_map/ppermute | solution.py:288
  313.1 17.8 %collective-permute-start.30 = (bf16[136,1088]{1,0:T(8,128)(2,1)}, bf16[136,1088]{1,0:T(8,128)(2,1)}, u32[]{:S(2)}, u32[]{:S(2)}) collective-permute-start(bf16[136,1088]{1,0:T(8,128)(2,1)} %broadcast_select_fusion.54), channel_id=1, source_target_pairs={{0,4},{2,6},{4,0},{6,2},{8,12},{10,14},{12,8},{14,10},{16,20},{18,... | collective-permute-start | bytes 887816 | tf_op jit(solution)/shard_map/ppermute | solution.py:288
  313.7 35.9 %collective-permute-start.33 = (bf16[1024,1152]{1,0:T(8,128)(2,1)}, bf16[1024,1152]{1,0:T(8,128)(2,1)}, u32[]{:S(2)}, u32[]{:S(2)}) collective-permute-start(bf16[1024,1152]{1,0:T(8,128)(2,1)} %get-tuple-element.264.gk_ref.k_own), channel_id=1, source_target_pairs={{0,2},{2,0},{4,6},{6,4},{8,10},{10,8},{12,14},{14,12},{16,18},{18,... | collective-permute-start | bytes 7077896 | tf_op jit(solution)/shard_map/ppermute | solution.py:288
  330.9 18.7 %collective-permute-start.34 = (bf16[1024,1152]{1,0:T(8,128)(2,1)}, bf16[1024,1152]{1,0:T(8,128)(2,1)}, u32[]{:S(2)}, u32[]{:S(2)}) collective-permute-start(bf16[1024,1152]{1,0:T(8,128)(2,1)} %get-tuple-element.265.gv_ref.v_own), channel_id=1, source_target_pairs={{0,2},{2,0},{4,6},{6,4},{8,10},{10,8},{12,14},{14,12},{16,18},{18,... | collective-permute-start | bytes 7077896 | tf_op jit(solution)/shard_map/ppermute | solution.py:288
  331.0 18.6 %collective-permute-start.32 = (bf16[512,1152]{1,0:T(8,128)(2,1)S(1)}, bf16[512,1152]{1,0:T(8,128)(2,1)}, u32[]{:S(2)}, u32[]{:S(2)}) collective-permute-start(bf16[512,1152]{1,0:T(8,128)(2,1)S(1)} %copy-done.1), channel_id=1, source_target_pairs={{0,2},{2,0},{4,6},{6,4},{8,10},{10,8},{12,14},{14,12},{16,18},{18,... | collective-permute-start | bytes 3538952 | tf_op jit(solution)/shard_map/ppermute | solution.py:288
  343.9 29.0 %collective-permute-start.41 = (bf16[136,4352]{1,0:T(8,128)(2,1)}, bf16[136,4352]{1,0:T(8,128)(2,1)}, u32[]{:S(2)}, u32[]{:S(2)}) collective-permute-start(bf16[136,4352]{1,0:T(8,128)(2,1)} %broadcast_select_fusion.20), channel_id=1, source_target_pairs={{0,4},{2,6},{4,0},{6,2},{8,12},{10,14},{12,8},{14,10},{16,20},{18,... | collective-permute-start | bytes 3551240 | tf_op jit(solution)/shard_map/ppermute | solution.py:288
  346.8 17.6 %collective-permute-start.35 = (bf16[72,1088]{1,0:T(8,128)(2,1)}, bf16[72,1088]{1,0:T(8,128)(2,1)}, u32[]{:S(2)}, u32[]{:S(2)}) collective-permute-start(bf16[72,1088]{1,0:T(8,128)(2,1)} %broadcast_select_fusion.56), channel_id=1, source_target_pairs={{0,8},{2,10},{4,12},{6,14},{8,0},{10,2},{12,4},{14,6},{16,24},{18,... | collective-permute-start | bytes 470024 | tf_op jit(solution)/shard_map/ppermute | solution.py:288
  349.6 32.6 %collective-permute-start.40 = (bf16[136,2176]{1,0:T(8,128)(2,1)}, bf16[136,2176]{1,0:T(8,128)(2,1)S(1)}, u32[]{:S(2)}, u32[]{:S(2)}) collective-permute-start(bf16[136,2176]{1,0:T(8,128)(2,1)} %add_convert_fusion.12), channel_id=1, source_target_pairs={{0,16},{2,18},{4,20},{6,22},{8,24},{10,26},{12,28},{14,30},{16,0},... | collective-permute-start | bytes 1775624 | tf_op jit(solution)/shard_map/ppermute | solution.py:288
  365.4 20.3 %collective-permute-start.39 = (bf16[72,1088]{1,0:T(8,128)(2,1)S(1)}, bf16[72,1088]{1,0:T(8,128)(2,1)S(1)}, u32[]{:S(2)}, u32[]{:S(2)}) collective-permute-start(bf16[72,1088]{1,0:T(8,128)(2,1)S(1)} %add_convert_fusion.17), channel_id=1, source_target_pairs={{0,16},{2,18},{4,20},{6,22},{8,24},{10,26},{12,28},{14,30},{16,0},... | collective-permute-start | bytes 470024 | tf_op jit(solution)/shard_map/ppermute | solution.py:288
  367.7 39.4 %collective-permute-start.36 = (bf16[272,3264]{1,0:T(8,128)(2,1)}, bf16[272,3264]{1,0:T(8,128)(2,1)}, u32[]{:S(2)}, u32[]{:S(2)}) collective-permute-start(bf16[272,3264]{1,0:T(8,128)(2,1)} %get-tuple-element.277), channel_id=1, source_target_pairs={{0,1},{1,0},{2,3},{3,2},{4,5},{5,4},{6,7},{7,6},{8,9},{9,8},{10,11... | collective-permute-start | bytes 5326856 | tf_op jit(solution)/shard_map/ppermute | solution.py:292
  382.3 57.2 %collective-permute-start.46 = (bf16[136,2176]{1,0:T(8,128)(2,1)S(1)}, bf16[136,2176]{1,0:T(8,128)(2,1)}, u32[]{:S(2)}, u32[]{:S(2)}) collective-permute-start(bf16[136,2176]{1,0:T(8,128)(2,1)S(1)} %add_convert_fusion.11), channel_id=1, source_target_pairs={{0,8},{2,10},{4,12},{6,14},{8,0},{10,2},{12,4},{14,6},{16,24},{18,... | collective-permute-start | bytes 1775624 | tf_op jit(solution)/shard_map/ppermute | solution.py:288
  382.4 29.2 %collective-permute-start.43 = (bf16[72,4352]{1,0:T(8,128)(2,1)S(1)}, bf16[72,4352]{1,0:T(8,128)(2,1)S(1)}, u32[]{:S(2)}, u32[]{:S(2)}) collective-permute-start(bf16[72,4352]{1,0:T(8,128)(2,1)S(1)} %broadcast_select_fusion.38), channel_id=1, source_target_pairs={{0,8},{2,10},{4,12},{6,14},{8,0},{10,2},{12,4},{14,6},{16,24},{18,... | collective-permute-start | bytes 1880072 | tf_op jit(solution)/shard_map/ppermute | solution.py:288
  385.8 55.1 %collective-permute-start.45 = (bf16[72,1088]{1,0:T(8,128)(2,1)S(1)}, bf16[72,1088]{1,0:T(8,128)(2,1)}, u32[]{:S(2)}, u32[]{:S(2)}) collective-permute-start(bf16[72,1088]{1,0:T(8,128)(2,1)S(1)} %add_convert_fusion.16), channel_id=1, source_target_pairs={{0,8},{2,10},{4,12},{6,14},{8,0},{10,2},{12,4},{14,6},{16,24},{18,... | collective-permute-start | bytes 470024 | tf_op jit(solution)/shard_map/ppermute | solution.py:288
  386.5 52.3 %collective-permute-start.47 = (f32[12,544]{1,0:T(8,128)}, f32[12,544]{1,0:T(8,128)}, u32[]{:S(2)}, u32[]{:S(2)}) collective-permute-start(f32[12,544]{1,0:T(8,128)} %dynamic-slice_bitcast_fusion.9), channel_id=1, source_target_pairs={{0,1},{1,0},{2,3},{3,2},{4,5},{5,4},{6,7},{7,6},{8,9},{9,8},{10,11... | collective-permute-start | bytes 78344 | tf_op jit(solution)/shard_map/ppermute | solution.py:292
  407.2 24.5 %collective-permute-start.37 = (bf16[1088,512]{1,0:T(8,128)(2,1)S(1)}, bf16[1088,512]{1,0:T(8,128)(2,1)S(1)}, u32[]{:S(2)}, u32[]{:S(2)}) collective-permute-start(bf16[1088,512]{1,0:T(8,128)(2,1)S(1)} %copy-done.47), channel_id=1, source_target_pairs={{0,1},{1,0},{2,3},{3,2},{4,5},{5,4},{6,7},{7,6},{8,9},{9,8},{10,11... | collective-permute-start | bytes 3342344 | tf_op jit(solution)/shard_map/ppermute | solution.py:292
  411.6 18.9 %collective-permute-start.42 = (bf16[136,3264]{1,0:T(8,128)(2,1)S(1)}, bf16[136,3264]{1,0:T(8,128)(2,1)S(1)}, u32[]{:S(2)}, u32[]{:S(2)}) collective-permute-start(bf16[136,3264]{1,0:T(8,128)(2,1)S(1)} %broadcast_select_fusion.32), channel_id=1, source_target_pairs={{0,4},{2,6},{4,0},{6,2},{8,12},{10,14},{12,8},{14,10},{16,20},{18,... | collective-permute-start | bytes 2663432 | tf_op jit(solution)/shard_map/ppermute | solution.py:288
  430.5 35.7 %collective-permute-start.49 = (bf16[72,4352]{1,0:T(8,128)(2,1)S(1)}, bf16[72,4352]{1,0:T(8,128)(2,1)S(1)}, u32[]{:S(2)}, u32[]{:S(2)}) collective-permute-start(bf16[72,4352]{1,0:T(8,128)(2,1)S(1)} %add_convert_fusion.9), channel_id=1, source_target_pairs={{0,16},{2,18},{4,20},{6,22},{8,24},{10,26},{12,28},{14,30},{16,0},... | collective-permute-start | bytes 1880072 | tf_op jit(solution)/shard_map/ppermute | solution.py:288
  431.7 19.4 %collective-permute-start.44 = (bf16[72,3264]{1,0:T(8,128)(2,1)}, bf16[72,3264]{1,0:T(8,128)(2,1)}, u32[]{:S(2)}, u32[]{:S(2)}) collective-permute-start(bf16[72,3264]{1,0:T(8,128)(2,1)} %broadcast_select_fusion.47), channel_id=1, source_target_pairs={{0,8},{2,10},{4,12},{6,14},{8,0},{10,2},{12,4},{14,6},{16,24},{18,... | collective-permute-start | bytes 1410056 | tf_op jit(solution)/shard_map/ppermute | solution.py:288
  441.8 37.9 %collective-permute-start.54 = (f32[12,544]{1,0:T(8,128)S(1)}, f32[12,544]{1,0:T(8,128)S(1)}, u32[]{:S(2)}, u32[]{:S(2)}) collective-permute-start(f32[12,544]{1,0:T(8,128)S(1)} %bitcast_add_fusion), channel_id=1, source_target_pairs={{0,4},{2,6},{4,0},{6,2},{8,12},{10,14},{12,8},{14,10},{16,20},{18,... | collective-permute-start | bytes 78344 | tf_op jit(solution)/shard_map/ppermute | solution.py:288
  442.9 48.2 %collective-permute-start.52 = (bf16[272,2176]{1,0:T(8,128)(2,1)S(1)}, bf16[272,2176]{1,0:T(8,128)(2,1)S(1)}, u32[]{:S(2)}, u32[]{:S(2)}) collective-permute-start(bf16[272,2176]{1,0:T(8,128)(2,1)S(1)} %pad_maximum_fusion.9), channel_id=1, source_target_pairs={{0,4},{2,6},{4,0},{6,2},{8,12},{10,14},{12,8},{14,10},{16,20},{18,... | collective-permute-start | bytes 3551240 | tf_op jit(solution)/shard_map/ppermute | solution.py:288
  443.4 49.8 %collective-permute-start.51 = (bf16[136,1088]{1,0:T(8,128)(2,1)S(1)}, bf16[136,1088]{1,0:T(8,128)(2,1)S(1)}, u32[]{:S(2)}, u32[]{:S(2)}) collective-permute-start(bf16[136,1088]{1,0:T(8,128)(2,1)S(1)} %pad_maximum_fusion.13), channel_id=1, source_target_pairs={{0,4},{2,6},{4,0},{6,2},{8,12},{10,14},{12,8},{14,10},{16,20},{18,... | collective-permute-start | bytes 887816 | tf_op jit(solution)/shard_map/ppermute | solution.py:288
  452.3 27.3 %collective-permute-start.48 = (bf16[72,3264]{1,0:T(8,128)(2,1)S(1)}, bf16[72,3264]{1,0:T(8,128)(2,1)S(1)}, u32[]{:S(2)}, u32[]{:S(2)}) collective-permute-start(bf16[72,3264]{1,0:T(8,128)(2,1)S(1)} %add_convert_fusion.14), channel_id=1, source_target_pairs={{0,16},{2,18},{4,20},{6,22},{8,24},{10,26},{12,28},{14,30},{16,0},... | collective-permute-start | bytes 1410056 | tf_op jit(solution)/shard_map/ppermute | solution.py:288
  466.4 24.5 %collective-permute-start.53 = (bf16[72,4352]{1,0:T(8,128)(2,1)S(1)}, bf16[72,4352]{1,0:T(8,128)(2,1)S(1)}, u32[]{:S(2)}, u32[]{:S(2)}) collective-permute-start(bf16[72,4352]{1,0:T(8,128)(2,1)S(1)} %add_convert_fusion.8), channel_id=1, source_target_pairs={{0,8},{2,10},{4,12},{6,14},{8,0},{10,2},{12,4},{14,6},{16,24},{18,... | collective-permute-start | bytes 1880072 | tf_op jit(solution)/shard_map/ppermute | solution.py:288
  479.7 21.4 %collective-permute-start.50 = (bf16[72,3264]{1,0:T(8,128)(2,1)S(1)}, bf16[72,3264]{1,0:T(8,128)(2,1)S(1)}, u32[]{:S(2)}, u32[]{:S(2)}) collective-permute-start(bf16[72,3264]{1,0:T(8,128)(2,1)S(1)} %add_convert_fusion.13), channel_id=1, source_target_pairs={{0,8},{2,10},{4,12},{6,14},{8,0},{10,2},{12,4},{14,6},{16,24},{18,... | collective-permute-start | bytes 1410056 | tf_op jit(solution)/shard_map/ppermute | solution.py:288
  479.8 23.1 %collective-permute-start.59 = (f32[12,544]{1,0:T(8,128)S(1)}, f32[12,544]{1,0:T(8,128)S(1)}, u32[]{:S(2)}, u32[]{:S(2)}) collective-permute-start(f32[12,544]{1,0:T(8,128)S(1)} %add.256), channel_id=1, source_target_pairs={{0,8},{2,10},{4,12},{6,14},{8,0},{10,2},{12,4},{14,6},{16,24},{18,... | collective-permute-start | bytes 78344 | tf_op jit(solution)/shard_map/ppermute | solution.py:288
  491.1 25.9 %collective-permute-start.58 = (bf16[136,4352]{1,0:T(8,128)(2,1)S(1)}, bf16[136,4352]{1,0:T(8,128)(2,1)S(1)}, u32[]{:S(2)}, u32[]{:S(2)}) collective-permute-start(bf16[136,4352]{1,0:T(8,128)(2,1)S(1)} %pad_maximum_fusion.10), channel_id=1, source_target_pairs={{0,4},{2,6},{4,0},{6,2},{8,12},{10,14},{12,8},{14,10},{16,20},{18,... | collective-permute-start | bytes 3551240 | tf_op jit(solution)/shard_map/ppermute | solution.py:288
  501.2 45.0 %collective-permute-start.57 = (bf16[544,2176]{1,0:T(8,128)(2,1)}, bf16[544,2176]{1,0:T(8,128)(2,1)}, u32[]{:S(2)}, u32[]{:S(2)}) collective-permute-start(bf16[544,2176]{1,0:T(8,128)(2,1)} %pad_maximum_fusion.4), channel_id=1, source_target_pairs={{0,2},{2,0},{4,6},{6,4},{8,10},{10,8},{12,14},{14,12},{16,18},{18,... | collective-permute-start | bytes 7102472 | tf_op jit(solution)/shard_map/ppermute | solution.py:288
  502.8 33.6 %collective-permute-start.55 = (bf16[136,3264]{1,0:T(8,128)(2,1)S(1)}, bf16[136,3264]{1,0:T(8,128)(2,1)S(1)}, u32[]{:S(2)}, u32[]{:S(2)}) collective-permute-start(bf16[136,3264]{1,0:T(8,128)(2,1)S(1)} %pad_maximum_fusion.11), channel_id=1, source_target_pairs={{0,4},{2,6},{4,0},{6,2},{8,12},{10,14},{12,8},{14,10},{16,20},{18,... | collective-permute-start | bytes 2663432 | tf_op jit(solution)/shard_map/ppermute | solution.py:288
  502.9 38.8 %collective-permute-start.62 = (f32[12,544]{1,0:T(8,128)S(1)}, f32[12,544]{1,0:T(8,128)S(1)}, u32[]{:S(2)}, u32[]{:S(2)}) collective-permute-start(f32[12,544]{1,0:T(8,128)S(1)} %add.257), channel_id=1, source_target_pairs={{0,16},{2,18},{4,20},{6,22},{8,24},{10,26},{12,28},{14,30},{16,0},... | collective-permute-start | bytes 78344 | tf_op jit(solution)/shard_map/ppermute | solution.py:288
  519.2 34.0 %collective-permute-start.61 = (bf16[272,4352]{1,0:T(8,128)(2,1)}, bf16[272,4352]{1,0:T(8,128)(2,1)}, u32[]{:S(2)}, u32[]{:S(2)}) collective-permute-start(bf16[272,4352]{1,0:T(8,128)(2,1)} %pad_maximum_fusion.5), channel_id=1, source_target_pairs={{0,2},{2,0},{4,6},{6,4},{8,10},{10,8},{12,14},{14,12},{16,18},{18,... | collective-permute-start | bytes 7102472 | tf_op jit(solution)/shard_map/ppermute | solution.py:288
  539.1 21.0 %collective-permute-start.60 = (bf16[272,3264]{1,0:T(8,128)(2,1)}, bf16[272,3264]{1,0:T(8,128)(2,1)}, u32[]{:S(2)}, u32[]{:S(2)}) collective-permute-start(bf16[272,3264]{1,0:T(8,128)(2,1)} %pad_maximum_fusion.7), channel_id=1, source_target_pairs={{0,2},{2,0},{4,6},{6,4},{8,10},{10,8},{12,14},{14,12},{16,18},{18,... | collective-permute-start | bytes 5326856 | tf_op jit(solution)/shard_map/ppermute | solution.py:288
  (77 other events, 608.7 us)

commit v4 on v3

--- a/solution.py
+++ b/solution.py
@@ -701,7 +701,7 @@
     )(spot, mine, other, tokens, gain, middle)
 
 
-TAIL = "udovquqtvdoquqvudoqvudoqvuq"
+TAIL = "udovudoqququdotvqvqvudovquq"
 
 
 def tie(values, *earlier):
@@ -743,7 +743,8 @@
 
 def reduced(keep, give, bits, cut=False):
     if cut:
-        above, below = halves(give)
+        most = give.shape[0] // 32 * 24
+        above, below = give[:most], give[most:]
         above = yield cross(above), give
         below = yield cross(below), above
         got = jnp.concatenate([above, below], axis=0)
@@ -839,7 +840,6 @@
     way_qkv.step()
     way_out = Steps(spread(tie(out_weight, other_turned), turned_bits))
     way_up = Steps(spread(tie(up_weight, other_turned), turned_bits))
-    way_down = Steps(spread(tie(down_turned, way_up.got), turned_bits))
     grad_turned = cotangent.reshape(span, width).T
     grad_out = grad_turned.T
     grad_halves = grad_turned.reshape(2, width // 2, span)
@@ -872,16 +872,19 @@
     full_qkv = both_halves(qkv_weight, way_qkv.finish())
     full_q, full_k, full_v = (full_qkv[:, i * width : (i + 1) * width] for i in range(3))
     way_out.step(full_v)
-    way_up.step(full_v)
-    values = low(dot(tie(normed_all, way_out.latest, way_up.latest), full_v) + bias_value)
+    values = low(dot(tie(normed_all, way_out.latest), full_v) + bias_value)
+    way_up.step(values)
     way_out.step(values)
-    way_down.step(values)
-    keys = low(dot(tie(normed_all, way_out.latest, way_down.latest), full_k))
+    way_down = Steps(spread(tie(down_turned, way_up.latest), turned_bits))
+    keys = low(dot(tie(normed_all, way_out.latest, way_up.latest), full_k))
     way_out.step(keys)
     queries = low(low(dot(tie(normed, way_out.latest), full_q) + bias_query) * SCALING)
-    (queries,) = bound((queries,), way_up)
+    (queries,) = bound((queries,), way_up, way_down)
     way_up.step()
-    context, context_t, lse = attention_forward(spot, tie(queries, way_up.latest), keys, values, 1, span)
+    way_down.step()
+    context, context_t, lse = attention_forward(
+        spot, tie(queries, way_up.latest, way_down.latest), keys, values, 1, span
+    )
     context, context_t, lse = bound((context, context_t, lse), way_up, way_down, way_out)
     full_out = both_halves(out_weight, way_out.finish())
     way_up.step()
@@ -899,7 +902,7 @@
 
     active_sib = swap(active, CORE_BIT)
     give, keep_down = turned_weight_grads(
-        spot, *grad_left, tie(active, way_down.latest), active_sib, width // 4, "down_grads"
+        spot, *grad_left, tie(active, way_down.latest), active_sib, width // 2, "down_grads"
     )
     sum_down = Steps(reduced(keep_down, give, bits, True))
     part_down = way_down.finish(give)
@@ -924,24 +927,25 @@
     sum_out = Steps(reduced(keep_out, give_out, bits))
     give, keep_up = weight_grads(
         spot, *two_left, grad_hidden, tie(hidden_sib, give_out), grad_hidden.shape[1], two_left[0].shape[1],
-        2 * CHUNK, "up_grads"
+        grad_hidden.shape[1] // 2, "up_grads"
     )
     give, keep_up = bound((give, keep_up), sum_down)
-    sum_up = Steps(reduced(keep_up, give, bits))
+    sum_up = Steps(reduced(keep_up, give, bits, True))
     sum_down.step()
     grad_context = tie(grad_context, give, sum_down.latest)
 
     grad_q, grad_k, grad_v = attention_backward(
         spot, queries, keys, values, grad_context, context, lse, 1, span
     )
-    grad_q, grad_k, grad_v = bound((grad_q, grad_k, grad_v), sum_down, sum_out)
+    grad_q, grad_k, grad_v = bound((grad_q, grad_k, grad_v), sum_down, sum_out, sum_up)
     sum_down.step()
     sum_out.step()
+    sum_up.step()
     rights = []
     for part in (grad_q, grad_k, grad_v):
         rights += [part, swap(part, CORE_BIT)]
     mine, theirs = input_grads(
-        spot, full_q, full_k, full_v, tie(grad_q, sum_down.latest, sum_out.latest), grad_k, grad_v
+        spot, full_q, full_k, full_v, tie(grad_q, sum_down.latest, sum_out.latest, sum_up.latest), grad_k, grad_v
     )
     mine, theirs = bound((mine, theirs), sum_up, sum_down, sum_out)
     sum_up.step()
@@ -989,7 +993,10 @@
             chain.step(latest)
             latest = chain.latest
         except StopIteration as end:
-            done[name] = latest = end.value
+            value = end.value
+            if name in "do":
+                (value,) = bound((value,), sum_qkv)
+            done[name] = latest = value
     vectors_out = done["v"]
     outs = [vectors_out[i] for i in range(7)] + [vectors_out[8:].reshape(-1), vectors_out[7]]
 

time: 576 us -> 555 us (0.964)
  waiting for transfers between devices: 164 us -> 141 us
    ppermute x13 -> x14, waiting for transfers between devices: 43.4 us -> 24.7 us  [cross(): return lax.ppermute(values, 'shard', [(0, 1), (1, 0)])]
    convert_element_type x3 -> x4, other arithmetic: 9.61 us -> 14 us  [reduced(): return in_order(CORE_BIT, values, got).astype(jnp.float32)]
    ppermute x13 -> x14, starting transfers between devices: 12.3 us -> 14.8 us  [cross(): return lax.ppermute(values, 'shard', [(0, 1), (1, 0)])]
    unnamed x134 -> x132, local copies, waits for them, and re-layouts: 15.6 us -> 13.7 us
  transfers between devices with their start and end apart: 63 -> 64, of which waited for: 23 -> 25; matrix products, arithmetic and copies ran while one was open for 22% -> 23% of each run, Pallas kernels for 34% -> 34%
where the time goes in v4:
time: 555 us; the launch traced here: 544 us
  Pallas kernels  187 us (34%)
  waiting for transfers between devices  141 us (25%)
  other arithmetic  87.9 us (16%)
  starting transfers between devices  63.9 us (12%)
  local copies, waits for them, and re-layouts  51.3 us (9%)
  matrix products  11 us (2%)
    ppermute x50, waiting for transfers between devices, swap(): return lax.ppermute(values, 'replica', [(i, i ^ bit) for i in range(size)])  117 us
    ppermute x50, starting transfers between devices, swap(): return lax.ppermute(values, 'replica', [(i, i ^ bit) for i in range(size)])  49.1 us
    pallas_call x1, Pallas kernels, attention_backward(): pl.pallas_call(functools.partial(backward_kernel, span=span, width=width)...  37.4 us
    pallas_call x1, Pallas kernels, attention_forward(): pl.pallas_call(functools.partial(forward_kernel, span=span, width=width),...  31.7 us
    pallas_call x1, Pallas kernels, mlp_back(): _call(back_kernel, 'mlp_back', _vmem(6) + [any_spec] * 4, [jax.ShapeDtype...  26 us
    select_n x38, other arithmetic, choose(): return jnp.where(flag, left, right)  26 us
    ppermute x14, waiting for transfers between devices, cross(): return lax.ppermute(values, 'shard', [(0, 1), (1, 0)])  24.7 us
    convert_element_type x18, other arithmetic, low(): return values.astype(jnp.bfloat16)  21.4 us
  transfers between devices with their start and end apart: 64, of which 25 were waited for; matrix products, arithmetic and copies ran while one was open for 23% of the time, Pallas kernels for 34%

profile of v4, /device:TPU:27, one launch (start us, length us, event | category | flops | bytes accessed | tf_op | source)
XLA Modules:
  0.0 544.4 jit_solution(7113862270852210175)
XLA Ops:
  8.6 5.2 collective-permute-done
  20.6 7.4 %collective-permute-done.4 = bf16[72,3264]{1,0:T(8,128)(2,1)S(1)} collective-permute-done((bf16[72,3264]{1,0:T(8,128)(2,1)S(1)}, bf16[72,3264]{1,0:T(8,128)(2,1)S(1)}, u32[]{:S(2)}, u32[]{:S(2)}) %collective-permute-start.4) | collective-permute-done | bytes 470048 | tf_op jit(solution)/shard_map/ppermute | solution.py:288
  29.4 11.3 %collective-permute-done.1 = bf16[1088,512]{1,0:T(8,128)(2,1)S(1)} collective-permute-done((bf16[1088,512]{1,0:T(8,128)(2,1)S(1)}, bf16[1088,512]{1,0:T(8,128)(2,1)S(1)}, u32[]{:S(2)}, u32[]{:S(2)}) %collective-permute-start.1) | collective-permute-done | bytes 1114144 | tf_op jit(solution)/shard_map/ppermute | solution.py:292
  44.8 3.3 collective-permute-done.5
  49.5 4.0 collective-permute-start.6
  60.7 6.8 %pad_maximum_fusion.2 = (bf16[1088,1088]{1,0:T(8,128)(2,1)S(1)}, bf16[1088,1088]{1,0:T(8,128)(2,1)S(1)}, bf16[1088,1088]{1,0:T(8,128)(2,1)S(1)}) fusion(bf16[544,3264]{1,0:T(8,128)(2,1)S(1)} %get-tuple-element.346, bf16[544,3264]{1,0:T(8,128)(2,1)S(1)} %get-tuple-element.347), kind=kLoop, calls=%fused_computation.41 | loop fusion | flops 14204928 | bytes 14204928 | tf_op jit(solution)/shard_map/concatenate | solution.py:310
  68.8 4.8 add_convert_fusion.2.v_ref
  75.8 4.3 convolution_convert_fusion.k_ref
  80.1 3.7 collective-permute-done.8
  94.6 2.4 copy.48.x_ref
  97.0 31.7 %attention_forward.1 = (bf16[512,1088]{1,0:T(8,128)(2,1)S(1)}, bf16[1088,512]{1,0:T(8,128)(2,1)S(1)}, f32[9,2,512]{2,1,0:T(2,128)S(1)}) custom-call(s32[1]{0:T(128)} %bitcast.pos_ref, bf16[512,1088]{1,0:T(8,128)(2,1)S(1)} %fusion.7.q_ref, bf16[1024,1088]{1,0:T(8,128)(2,1)S(1)} %convolution_convert_fusion.k_ref, bf16[1024,1088]{1,0:T(8,128)(2,1)} %add_convert_fusion.2.v_ref), custom_call_target="tpu_custom_call" | custom-call | flops 1 | bytes 1 | tf_op jit(solution)/shard_map/attention_forward/pallas_call | solution.py:182
  138.9 2.5 pad_maximum_fusion.got_ref.up_got
  141.4 20.2 %mlp_up.1 = (bf16[512,4352]{1,0:T(8,128)(2,1)}, bf16[512,4352]{1,0:T(8,128)(2,1)}, f32[1088,512]{1,0:T(8,128)}, f32[512,1088]{1,0:T(8,128)}, f32[512,1]{1,0:T(8,128)}, /*index=5*/bf16[1088,512]{1,0:T(8,128)(2,1)}) custom-call(s32[1]{0:T(128)} %bitcast.pos_ref, bf16[512,1088]{1,0:T(8,128)(2,1)} %copy-done.5, bf16[1088,1088]{1,0:T(8,128)(2,1)} %pad_maximum_fusion.3.out_w_ref, ...), custom_call_target="tpu_custom_call" | custom-call | flops 1 | bytes 1 | tf_op jit(solution)/shard_map/mlp_up/pallas_call | solution.py:424
  164.1 2.4 dynamic-slice_bitcast_fusion.7
  170.6 3.0 collective-permute-done.17.left_sib
  173.7 10.8 %down_grads.1 = (bf16[544,2176]{1,0:T(8,128)(2,1)}, bf16[544,2176]{1,0:T(8,128)(2,1)}) custom-call(s32[1]{0:T(128)} %bitcast.pos_ref, bf16[544,512]{1,0:T(8,128)(2,1)} %get-tuple-element.393.left_own, bf16[544,512]{1,0:T(8,128)(2,1)} %collective-permute-done.17.left_sib, bf16[512,4352]{1,0:T(8,128)(2,1)} %get-tuple-element.231.right_own.act_ref, ...), custom_call_target="tpu_custom_call" | custom-call | flops 1 | bytes 1 | tf_op jit(solution)/shard_map/down_grads/pallas_call | solution.py:600
  184.5 2.8 slice.185
  192.6 11.5 %mlp_down.1 = bf16[1088,512]{1,0:T(8,128)(2,1)} custom-call(s32[1]{0:T(128)} %bitcast.pos_ref, bf16[512,4352]{1,0:T(8,128)(2,1)} %get-tuple-element.231.right_own.act_ref, bf16[1088,2176]{1,0:T(8,128)(2,1)} %bitcast.77, bf16[1088,2176]{1,0:T(8,128)(2,1)} %constant_dynamic-update-slice_fusion.16.got_ref.down_got, f32[1088,512]{1,0:T(8,128)} %get-tuple-element.235.middle_ref, ...), custom_call_target="tpu_custom_call" | custom-call | flops 1 | bytes 1 | tf_op jit(solution)/shard_map/mlp_down/pallas_call | solution.py:456
  204.9 26.0 %mlp_back.1 = (bf16[512,4352]{1,0:T(8,128)(2,1)}, f32[512,1088]{1,0:T(8,128)}, bf16[512,1152]{1,0:T(8,128)(2,1)}, bf16[512,1088]{1,0:T(8,128)(2,1)}, f32[1,4352]{1,0:T(1,128)}, /*index=5*/f32[8,1088]{1,0:T(8,128)}) custom-call(s32[1]{0:T(128)} %bitcast.pos_ref, bf16[512,1088]{1,0:T(8,128)(2,1)} %bitcast.79, bf16[512,4352]{1,0:T(8,128)(2,1)} %get-tuple-element.239.slope_ref, ...), custom_call_target="tpu_custom_call" | custom-call | flops 1 | bytes 1 | tf_op jit(solution)/shard_map/mlp_back/pallas_call | solution.py:532
  235.6 3.8 collective-permute-done.24.right_sib
  240.4 4.7 out_grads.1
  245.1 9.8 %up_grads.1 = (bf16[272,4352]{1,0:T(8,128)(2,1)}, bf16[272,4352]{1,0:T(8,128)(2,1)}) custom-call(s32[1]{0:T(128)} %bitcast.pos_ref, bf16[2,272,512]{2,1,0:T(8,128)(2,1)} %get-tuple-element.391.left_own, bf16[2,272,512]{2,1,0:T(8,128)(2,1)} %copy-done.50, bf16[512,4352]{1,0:T(8,128)(2,1)} %get-tuple-element.249.right_own, ...), custom_call_target="tpu_custom_call" | custom-call | flops 1 | bytes 1 | tf_op jit(solution)/shard_map/up_grads/pallas_call | solution.py:567
  256.6 2.7 collective-permute-start.28
  270.5 37.4 %attention_backward.1 = (bf16[512,1152]{1,0:T(8,128)(2,1)S(1)}, bf16[1024,1152]{1,0:T(8,128)(2,1)}, bf16[1024,1152]{1,0:T(8,128)(2,1)}) custom-call(s32[1]{0:T(128)} %bitcast.pos_ref, bf16[512,1088]{1,0:T(8,128)(2,1)S(1)} %copy-done.4, bf16[1024,1088]{1,0:T(8,128)(2,1)} %copy-done.2, bf16[1024,1088]{1,0:T(8,128)(2,1)} %add_convert_fusion.2.v_ref, ...), custom_call_target="tpu_custom_call" | custom-call | flops 1 | bytes 1 | tf_op jit(solution)/shard_map/attention_backward/pallas_call | solution.py:212
  317.3 13.7 %input_grads.1 = (f32[1088,512]{1,0:T(8,128)}, bf16[1088,512]{1,0:T(8,128)(2,1)}) custom-call(s32[1]{0:T(128)} %bitcast.pos_ref, bf16[1088,1088]{1,0:T(8,128)(2,1)} %copy-done.25, bf16[1088,1088]{1,0:T(8,128)(2,1)} %copy-done.27, bf16[1088,1088]{1,0:T(8,128)(2,1)} %copy-done.26, bf16[512,1152]{1,0:T(8,128)(2,1)} %copy-done, ...), custom_call_target="tpu_custom_call" | custom-call | flops 1 | bytes 1 | tf_op jit(solution)/shard_map/input_grads/pallas_call | solution.py:662
  333.8 2.9 add_convert_fusion
  345.6 14.9 %qkv_weight_grads.1 = (bf16[272,3264]{1,0:T(8,128)(2,1)}, bf16[272,3264]{1,0:T(8,128)(2,1)}) custom-call(s32[1]{0:T(128)} %bitcast.pos_ref, bf16[2,272,1024]{2,1,0:T(8,128)(2,1)} %get-tuple-element.371.left_own, bf16[2,272,1024]{2,1,0:T(8,128)(2,1)} %collective-permute-done.32.left_sib, bf16[512,1152]{1,0:T(8,128)(2,1)} %copy-done, ...), custom_call_target="tpu_custom_call" | custom-call | flops 1 | bytes 1 | tf_op jit(solution)/shard_map/qkv_weight_grads/pallas_call | solution.py:639
  364.9 3.5 collective-permute-done.41
  370.2 3.5 collective-permute-done.40
  376.5 7.1 %collective-permute-done.39 = bf16[72,1088]{1,0:T(8,128)(2,1)S(1)} collective-permute-done((bf16[72,1088]{1,0:T(8,128)(2,1)S(1)}, bf16[72,1088]{1,0:T(8,128)(2,1)S(1)}, u32[]{:S(2)}, u32[]{:S(2)}) %collective-permute-start.39) | collective-permute-done | bytes 156704 | tf_op jit(solution)/shard_map/ppermute | solution.py:288
  384.4 8.4 %collective-permute-done.44 = bf16[72,4352]{1,0:T(8,128)(2,1)S(1)} collective-permute-done((bf16[72,4352]{1,0:T(8,128)(2,1)S(1)}, bf16[72,4352]{1,0:T(8,128)(2,1)S(1)}, u32[]{:S(2)}, u32[]{:S(2)}) %collective-permute-start.44) | collective-permute-done | bytes 626720 | tf_op jit(solution)/shard_map/ppermute | solution.py:288
  393.8 11.5 %collective-permute-done.43 = bf16[136,2176]{1,0:T(8,128)(2,1)S(1)} collective-permute-done((bf16[136,2176]{1,0:T(8,128)(2,1)S(1)}, bf16[136,2176]{1,0:T(8,128)(2,1)S(1)}, u32[]{:S(2)}, u32[]{:S(2)}) %collective-permute-start.43) | collective-permute-done | bytes 591904 | tf_op jit(solution)/shard_map/ppermute | solution.py:288
  417.6 13.8 %collective-permute-done.49 = bf16[136,3264]{1,0:T(8,128)(2,1)} collective-permute-done((bf16[136,3264]{1,0:T(8,128)(2,1)S(1)}, bf16[136,3264]{1,0:T(8,128)(2,1)}, u32[]{:S(2)}, u32[]{:S(2)}) %collective-permute-start.49) | collective-permute-done | bytes 887840 | tf_op jit(solution)/shard_map/ppermute | solution.py:288
  434.6 11.8 %collective-permute-done.48 = bf16[72,4352]{1,0:T(8,128)(2,1)S(1)} collective-permute-done((bf16[72,4352]{1,0:T(8,128)(2,1)}, bf16[72,4352]{1,0:T(8,128)(2,1)S(1)}, u32[]{:S(2)}, u32[]{:S(2)}) %collective-permute-start.48) | collective-permute-done | bytes 626720 | tf_op jit(solution)/shard_map/ppermute | solution.py:288
  447.7 4.6 collective-permute-done.38.other_ref
  453.1 6.3 %token_grads.1 = bf16[1088,512]{1,0:T(8,128)(2,1)} custom-call(s32[1]{0:T(128)} %bitcast.pos_ref, f32[1088,512]{1,0:T(8,128)} %get-tuple-element.274.mine_ref, bf16[1088,512]{1,0:T(8,128)(2,1)} %collective-permute-done.38.other_ref, bf16[1088,512]{1,0:T(8,128)(2,1)} %bitcast.72, f32[1088,1]{1,0:T(8,128)} %copy.55.gain_ref, ...), custom_call_target="tpu_custom_call" | custom-call | flops 1 | bytes 1 | tf_op jit(solution)/shard_map/token_grads/pallas_call | solution.py:686
  462.3 15.2 %collective-permute-done.50 = bf16[72,4352]{1,0:T(8,128)(2,1)S(1)} collective-permute-done((bf16[72,4352]{1,0:T(8,128)(2,1)S(1)}, bf16[72,4352]{1,0:T(8,128)(2,1)S(1)}, u32[]{:S(2)}, u32[]{:S(2)}) %collective-permute-start.50) | collective-permute-done | bytes 626720 | tf_op jit(solution)/shard_map/ppermute | solution.py:288
  481.0 2.7 collective-permute-start.53
  485.1 2.6 collective-permute-start.52
  489.5 4.4 collective-permute-done.59
  495.0 7.3 %collective-permute-done.54 = bf16[136,4352]{1,0:T(8,128)(2,1)S(1)} collective-permute-done((bf16[136,4352]{1,0:T(8,128)(2,1)S(1)}, bf16[136,4352]{1,0:T(8,128)(2,1)S(1)}, u32[]{:S(2)}, u32[]{:S(2)}) %collective-permute-start.54) | collective-permute-done | bytes 1183776 | tf_op jit(solution)/shard_map/ppermute | solution.py:288
  504.3 7.6 %collective-permute-start.63 = (bf16[272,4352]{1,0:T(8,128)(2,1)}, bf16[272,4352]{1,0:T(8,128)(2,1)}, u32[]{:S(2)}, u32[]{:S(2)}) collective-permute-start(bf16[272,4352]{1,0:T(8,128)(2,1)} %pad_maximum_fusion.5), channel_id=1, source_target_pairs={{0,2},{2,0},{4,6},{6,4},{8,10},{10,8},{12,14},{14,12},{16,18},{18,... | collective-permute-start | bytes 7102472 | tf_op jit(solution)/shard_map/ppermute | solution.py:288
  512.8 4.4 maximum_convert_fusion
  517.2 4.5 collective-permute-done.60
  526.2 4.0 collective-permute-start.62
  531.6 2.5 broadcast_select_fusion.5
  534.1 4.4 maximum_convert_fusion.1
  540.7 3.5 maximum_convert_fusion.2
  (387 shorter events, 154.6 us)
Async XLA Ops:
  16.4 24.3 %collective-permute-start.1 = (bf16[1088,512]{1,0:T(8,128)(2,1)S(1)}, bf16[1088,512]{1,0:T(8,128)(2,1)S(1)}, u32[]{:S(2)}, u32[]{:S(2)}) collective-permute-start(bf16[1088,512]{1,0:T(8,128)(2,1)S(1)} %bitcast.73), channel_id=1, source_target_pairs={{0,1},{1,0},{2,3},{3,2},{4,5},{5,4},{6,7},{7,6},{8,9},{9,8},{10,11... | collective-permute-start | bytes 3342344 | tf_op jit(solution)/shard_map/ppermute | solution.py:292
  28.2 19.9 %collective-permute-start.5 = (bf16[144,3264]{1,0:T(8,128)(2,1)S(1)}, bf16[144,3264]{1,0:T(8,128)(2,1)}, u32[]{:S(2)}, u32[]{:S(2)}) collective-permute-start(bf16[144,3264]{1,0:T(8,128)(2,1)S(1)} %constant_dynamic-update-slice_fusion), channel_id=1, source_target_pairs={{0,4},{2,6},{4,0},{6,2},{8,12},{10,14},{12,8},{14,10},{16,20},{18,... | collective-permute-start | bytes 2820104 | tf_op jit(solution)/shard_map/ppermute | solution.py:288
  41.9 25.6 %collective-permute-start.3 = (bf16[72,1088]{1,0:T(8,128)(2,1)S(1)}, bf16[72,1088]{1,0:T(8,128)(2,1)S(1)}, u32[]{:S(2)}, u32[]{:S(2)}) collective-permute-start(bf16[72,1088]{1,0:T(8,128)(2,1)S(1)} %constant_dynamic-slice_fusion.2), channel_id=1, source_target_pairs={{0,1},{1,0},{2,3},{3,2},{4,5},{5,4},{6,7},{7,6},{8,9},{9,8},{10,11... | collective-permute-start | bytes 470024 | tf_op jit(solution)/shard_map/ppermute | solution.py:292
  44.5 29.1 %collective-permute-start.9 = (bf16[72,4352]{1,0:T(8,128)(2,1)S(1)}, bf16[72,4352]{1,0:T(8,128)(2,1)S(1)}, u32[]{:S(2)}, u32[]{:S(2)}) collective-permute-start(bf16[72,4352]{1,0:T(8,128)(2,1)S(1)} %constant_dynamic-slice_fusion.1), channel_id=1, source_target_pairs={{0,1},{1,0},{2,3},{3,2},{4,5},{5,4},{6,7},{7,6},{8,9},{9,8},{10,11... | collective-permute-start | bytes 1880072 | tf_op jit(solution)/shard_map/ppermute | solution.py:292
  73.6 15.6 %collective-permute-start.10 = (bf16[72,4352]{1,0:T(8,128)(2,1)S(1)}, bf16[72,4352]{1,0:T(8,128)(2,1)S(1)}, u32[]{:S(2)}, u32[]{:S(2)}) collective-permute-start(bf16[72,4352]{1,0:T(8,128)(2,1)S(1)} %collective-permute-done.9), channel_id=1, source_target_pairs={{0,4},{2,6},{4,0},{6,2},{8,12},{10,14},{12,8},{14,10},{16,20},{18,... | collective-permute-start | bytes 1880072 | tf_op jit(solution)/shard_map/ppermute | solution.py:288
  75.1 14.1 %collective-permute-start.11 = (bf16[136,2176]{1,0:T(8,128)(2,1)S(1)}, bf16[136,2176]{1,0:T(8,128)(2,1)}, u32[]{:S(2)}, u32[]{:S(2)}) collective-permute-start(bf16[136,2176]{1,0:T(8,128)(2,1)S(1)} %constant_dynamic-slice_fusion), channel_id=1, source_target_pairs={{0,1},{1,0},{2,3},{3,2},{4,5},{5,4},{6,7},{7,6},{8,9},{9,8},{10,11... | collective-permute-start | bytes 1775624 | tf_op jit(solution)/shard_map/ppermute | solution.py:292
  91.1 37.7 %collective-permute-start.12 = (bf16[144,4352]{1,0:T(8,128)(2,1)}, bf16[144,4352]{1,0:T(8,128)(2,1)}, u32[]{:S(2)}, u32[]{:S(2)}) collective-permute-start(bf16[144,4352]{1,0:T(8,128)(2,1)} %constant_dynamic-update-slice_fusion.8), channel_id=1, source_target_pairs={{0,8},{2,10},{4,12},{6,14},{8,0},{10,2},{12,4},{14,6},{16,24},{18,... | collective-permute-start | bytes 3760136 | tf_op jit(solution)/shard_map/ppermute | solution.py:288
  91.2 37.5 %collective-permute-start.14 = (bf16[288,1088]{1,0:T(8,128)(2,1)}, bf16[288,1088]{1,0:T(8,128)(2,1)}, u32[]{:S(2)}, u32[]{:S(2)}) collective-permute-start(bf16[288,1088]{1,0:T(8,128)(2,1)} %constant_dynamic-update-slice_fusion.6), channel_id=1, source_target_pairs={{0,2},{2,0},{4,6},{6,4},{8,10},{10,8},{12,14},{14,12},{16,18},{18,... | collective-permute-start | bytes 1880072 | tf_op jit(solution)/shard_map/ppermute | solution.py:288
  93.4 35.4 %collective-permute-start.13 = (bf16[136,2176]{1,0:T(8,128)(2,1)}, bf16[136,2176]{1,0:T(8,128)(2,1)}, u32[]{:S(2)}, u32[]{:S(2)}) collective-permute-start(bf16[136,2176]{1,0:T(8,128)(2,1)} %collective-permute-done.11), channel_id=1, source_target_pairs={{0,4},{2,6},{4,0},{6,2},{8,12},{10,14},{12,8},{14,10},{16,20},{18,... | collective-permute-start | bytes 1775624 | tf_op jit(solution)/shard_map/ppermute | solution.py:288
  135.0 27.4 %collective-permute-start.16 = (bf16[272,2176]{1,0:T(8,128)(2,1)S(1)}, bf16[272,2176]{1,0:T(8,128)(2,1)S(1)}, u32[]{:S(2)}, u32[]{:S(2)}) collective-permute-start(bf16[272,2176]{1,0:T(8,128)(2,1)S(1)} %constant_dynamic-update-slice_fusion.12), channel_id=1, source_target_pairs={{0,8},{2,10},{4,12},{6,14},{8,0},{10,2},{12,4},{14,6},{16,24},{18,... | collective-permute-start | bytes 3551240 | tf_op jit(solution)/shard_map/ppermute | solution.py:288
  164.0 23.3 %collective-permute-start.19 = (bf16[544,2176]{1,0:T(8,128)(2,1)S(1)}, bf16[544,2176]{1,0:T(8,128)(2,1)}, u32[]{:S(2)}, u32[]{:S(2)}) collective-permute-start(bf16[544,2176]{1,0:T(8,128)(2,1)S(1)} %constant_dynamic-update-slice_fusion.14), channel_id=1, source_target_pairs={{0,2},{2,0},{4,6},{6,4},{8,10},{10,8},{12,14},{14,12},{16,18},{18,... | collective-permute-start | bytes 7102472 | tf_op jit(solution)/shard_map/ppermute | solution.py:288
  169.1 35.0 %collective-permute-start.21 = (bf16[2,272,512]{2,1,0:T(8,128)(2,1)}, bf16[2,272,512]{2,1,0:T(8,128)(2,1)S(1)}, u32[]{:S(2)}, u32[]{:S(2)}) collective-permute-start(bf16[2,272,512]{2,1,0:T(8,128)(2,1)} %get-tuple-element.388), channel_id=1, source_target_pairs={{0,2},{2,0},{4,6},{6,4},{8,10},{10,8},{12,14},{14,12},{16,18},{18,... | collective-permute-start | bytes 1671176 | tf_op jit(solution)/shard_map/ppermute | solution.py:288
  170.6 33.5 %collective-permute-start.20 = (bf16[2,272,512]{2,1,0:T(8,128)(2,1)S(1)}, bf16[2,272,512]{2,1,0:T(8,128)(2,1)S(1)}, u32[]{:S(2)}, u32[]{:S(2)}) collective-permute-start(bf16[2,272,512]{2,1,0:T(8,128)(2,1)S(1)} %get-tuple-element.390), channel_id=1, source_target_pairs={{0,2},{2,0},{4,6},{6,4},{8,10},{10,8},{12,14},{14,12},{16,18},{18,... | collective-permute-start | bytes 1671176 | tf_op jit(solution)/shard_map/ppermute | solution.py:288
  187.3 43.6 %collective-permute-start.22 = (bf16[408,2176]{1,0:T(8,128)(2,1)}, bf16[408,2176]{1,0:T(8,128)(2,1)}, u32[]{:S(2)}, u32[]{:S(2)}) collective-permute-start(bf16[408,2176]{1,0:T(8,128)(2,1)} %slice.185), channel_id=1, source_target_pairs={{0,1},{1,0},{2,3},{3,2},{4,5},{5,4},{6,7},{7,6},{8,9},{9,8},{10,11... | collective-permute-start | bytes 5326856 | tf_op jit(solution)/shard_map/ppermute | solution.py:292
  230.9 14.2 %collective-permute-start.23 = (bf16[512,4352]{1,0:T(8,128)(2,1)}, bf16[512,4352]{1,0:T(8,128)(2,1)}, u32[]{:S(2)}, u32[]{:S(2)}) collective-permute-start(bf16[512,4352]{1,0:T(8,128)(2,1)} %get-tuple-element.249.right_own), channel_id=1, source_target_pairs={{0,2},{2,0},{4,6},{6,4},{8,10},{10,8},{12,14},{14,12},{16,18},{18,... | collective-permute-start | bytes 13369352 | tf_op jit(solution)/shard_map/ppermute | solution.py:288
  233.2 21.8 %collective-permute-start.25 = (bf16[136,2176]{1,0:T(8,128)(2,1)S(1)}, bf16[136,2176]{1,0:T(8,128)(2,1)}, u32[]{:S(2)}, u32[]{:S(2)}) collective-permute-start(bf16[136,2176]{1,0:T(8,128)(2,1)S(1)} %slice.186), channel_id=1, source_target_pairs={{0,1},{1,0},{2,3},{3,2},{4,5},{5,4},{6,7},{7,6},{8,9},{9,8},{10,11... | collective-permute-start | bytes 1775624 | tf_op jit(solution)/shard_map/ppermute | solution.py:292
  256.6 52.8 %collective-permute-start.28 = (bf16[192,4352]{1,0:T(8,128)(2,1)S(1)}, bf16[192,4352]{1,0:T(8,128)(2,1)S(1)}, u32[]{:S(2)}, u32[]{:S(2)}) collective-permute-start(bf16[192,4352]{1,0:T(8,128)(2,1)S(1)} %slice.189), channel_id=1, source_target_pairs={{0,1},{1,0},{2,3},{3,2},{4,5},{5,4},{6,7},{7,6},{8,9},{9,8},{10,11... | collective-permute-start | bytes 5013512 | tf_op jit(solution)/shard_map/ppermute | solution.py:292
  261.8 47.7 %collective-permute-start.26 = (bf16[272,2176]{1,0:T(8,128)(2,1)S(1)}, bf16[272,2176]{1,0:T(8,128)(2,1)S(1)}, u32[]{:S(2)}, u32[]{:S(2)}) collective-permute-start(bf16[272,2176]{1,0:T(8,128)(2,1)S(1)} %broadcast_select_fusion.23), channel_id=1, source_target_pairs={{0,4},{2,6},{4,0},{6,2},{8,12},{10,14},{12,8},{14,10},{16,20},{18,... | collective-permute-start | bytes 3551240 | tf_op jit(solution)/shard_map/ppermute | solution.py:288
  265.7 78.0 %collective-permute-start.32 = (bf16[2,272,1024]{2,1,0:T(8,128)(2,1)}, bf16[2,272,1024]{2,1,0:T(8,128)(2,1)}, u32[]{:S(2)}, u32[]{:S(2)}) collective-permute-start(bf16[2,272,1024]{2,1,0:T(8,128)(2,1)} %get-tuple-element.370), channel_id=1, source_target_pairs={{0,2},{2,0},{4,6},{6,4},{8,10},{10,8},{12,14},{14,12},{16,18},{18,... | collective-permute-start | bytes 3342344 | tf_op jit(solution)/shard_map/ppermute | solution.py:288
  266.5 43.0 %collective-permute-start.27 = (bf16[272,1088]{1,0:T(8,128)(2,1)}, bf16[272,1088]{1,0:T(8,128)(2,1)S(1)}, u32[]{:S(2)}, u32[]{:S(2)}) collective-permute-start(bf16[272,1088]{1,0:T(8,128)(2,1)} %get-tuple-element.251), channel_id=1, source_target_pairs={{0,1},{1,0},{2,3},{3,2},{4,5},{5,4},{6,7},{7,6},{8,9},{9,8},{10,11... | collective-permute-start | bytes 1775624 | tf_op jit(solution)/shard_map/ppermute | solution.py:292
  269.1 64.2 %collective-permute-start.29 = (bf16[80,4352]{1,0:T(8,128)(2,1)}, bf16[80,4352]{1,0:T(8,128)(2,1)}, u32[]{:S(2)}, u32[]{:S(2)}) collective-permute-start(bf16[80,4352]{1,0:T(8,128)(2,1)} %slice.190), channel_id=1, source_target_pairs={{0,1},{1,0},{2,3},{3,2},{4,5},{5,4},{6,7},{7,6},{8,9},{9,8},{10,11... | collective-permute-start | bytes 2088968 | tf_op jit(solution)/shard_map/ppermute | solution.py:292
  311.8 22.0 %collective-permute-start.30 = (bf16[136,2176]{1,0:T(8,128)(2,1)}, bf16[136,2176]{1,0:T(8,128)(2,1)}, u32[]{:S(2)}, u32[]{:S(2)}) collective-permute-start(bf16[136,2176]{1,0:T(8,128)(2,1)} %broadcast_select_fusion.43), channel_id=1, source_target_pairs={{0,8},{2,10},{4,12},{6,14},{8,0},{10,2},{12,4},{14,6},{16,24},{18,... | collective-permute-start | bytes 1775624 | tf_op jit(solution)/shard_map/ppermute | solution.py:288
  315.1 18.2 %collective-permute-start.31 = (bf16[136,1088]{1,0:T(8,128)(2,1)}, bf16[136,1088]{1,0:T(8,128)(2,1)}, u32[]{:S(2)}, u32[]{:S(2)}) collective-permute-start(bf16[136,1088]{1,0:T(8,128)(2,1)} %broadcast_select_fusion.54), channel_id=1, source_target_pairs={{0,4},{2,6},{4,0},{6,2},{8,12},{10,14},{12,8},{14,10},{16,20},{18,... | collective-permute-start | bytes 887816 | tf_op jit(solution)/shard_map/ppermute | solution.py:288
  315.6 30.0 %collective-permute-start.34 = (bf16[1024,1152]{1,0:T(8,128)(2,1)}, bf16[1024,1152]{1,0:T(8,128)(2,1)}, u32[]{:S(2)}, u32[]{:S(2)}) collective-permute-start(bf16[1024,1152]{1,0:T(8,128)(2,1)} %get-tuple-element.270.gk_ref.k_own), channel_id=1, source_target_pairs={{0,2},{2,0},{4,6},{6,4},{8,10},{10,8},{12,14},{14,12},{16,18},{18,... | collective-permute-start | bytes 7077896 | tf_op jit(solution)/shard_map/ppermute | solution.py:288
  340.4 27.9 %collective-permute-start.41 = (bf16[136,4352]{1,0:T(8,128)(2,1)}, bf16[136,4352]{1,0:T(8,128)(2,1)}, u32[]{:S(2)}, u32[]{:S(2)}) collective-permute-start(bf16[136,4352]{1,0:T(8,128)(2,1)} %broadcast_select_fusion.20), channel_id=1, source_target_pairs={{0,4},{2,6},{4,0},{6,2},{8,12},{10,14},{12,8},{14,10},{16,20},{18,... | collective-permute-start | bytes 3551240 | tf_op jit(solution)/shard_map/ppermute | solution.py:288
  343.8 16.8 %collective-permute-start.36 = (bf16[72,1088]{1,0:T(8,128)(2,1)}, bf16[72,1088]{1,0:T(8,128)(2,1)}, u32[]{:S(2)}, u32[]{:S(2)}) collective-permute-start(bf16[72,1088]{1,0:T(8,128)(2,1)} %broadcast_select_fusion.56), channel_id=1, source_target_pairs={{0,8},{2,10},{4,12},{6,14},{8,0},{10,2},{12,4},{14,6},{16,24},{18,... | collective-permute-start | bytes 470024 | tf_op jit(solution)/shard_map/ppermute | solution.py:288
  345.5 28.2 %collective-permute-start.40 = (bf16[136,2176]{1,0:T(8,128)(2,1)}, bf16[136,2176]{1,0:T(8,128)(2,1)S(1)}, u32[]{:S(2)}, u32[]{:S(2)}) collective-permute-start(bf16[136,2176]{1,0:T(8,128)(2,1)} %add_convert_fusion.12), channel_id=1, source_target_pairs={{0,16},{2,18},{4,20},{6,22},{8,24},{10,26},{12,28},{14,30},{16,0},... | collective-permute-start | bytes 1775624 | tf_op jit(solution)/shard_map/ppermute | solution.py:288
  360.5 49.2 %collective-permute-start.37 = (bf16[272,3264]{1,0:T(8,128)(2,1)}, bf16[272,3264]{1,0:T(8,128)(2,1)}, u32[]{:S(2)}, u32[]{:S(2)}) collective-permute-start(bf16[272,3264]{1,0:T(8,128)(2,1)} %get-tuple-element.283), channel_id=1, source_target_pairs={{0,1},{1,0},{2,3},{3,2},{4,5},{5,4},{6,7},{7,6},{8,9},{9,8},{10,11... | collective-permute-start | bytes 5326856 | tf_op jit(solution)/shard_map/ppermute | solution.py:292
  363.6 20.1 %collective-permute-start.45 = (f32[2,12,544]{2,1,0:T(8,128)S(1)}, f32[2,12,544]{2,1,0:T(8,128)S(1)}, u32[]{:S(2)}, u32[]{:S(2)}) collective-permute-start(f32[2,12,544]{2,1,0:T(8,128)S(1)} %concatenate.129), channel_id=1, source_target_pairs={{0,2},{2,0},{4,6},{6,4},{8,10},{10,8},{12,14},{14,12},{16,18},{18,... | collective-permute-start | bytes 156680 | tf_op jit(solution)/shard_map/ppermute | solution.py:288
  374.8 18.0 %collective-permute-start.44 = (bf16[72,4352]{1,0:T(8,128)(2,1)S(1)}, bf16[72,4352]{1,0:T(8,128)(2,1)S(1)}, u32[]{:S(2)}, u32[]{:S(2)}) collective-permute-start(bf16[72,4352]{1,0:T(8,128)(2,1)S(1)} %broadcast_select_fusion.36), channel_id=1, source_target_pairs={{0,8},{2,10},{4,12},{6,14},{8,0},{10,2},{12,4},{14,6},{16,24},{18,... | collective-permute-start | bytes 1880072 | tf_op jit(solution)/shard_map/ppermute | solution.py:288
  376.1 29.3 %collective-permute-start.43 = (bf16[136,2176]{1,0:T(8,128)(2,1)S(1)}, bf16[136,2176]{1,0:T(8,128)(2,1)S(1)}, u32[]{:S(2)}, u32[]{:S(2)}) collective-permute-start(bf16[136,2176]{1,0:T(8,128)(2,1)S(1)} %add_convert_fusion.11), channel_id=1, source_target_pairs={{0,8},{2,10},{4,12},{6,14},{8,0},{10,2},{12,4},{14,6},{16,24},{18,... | collective-permute-start | bytes 1775624 | tf_op jit(solution)/shard_map/ppermute | solution.py:288
  383.7 25.2 %collective-permute-start.42 = (bf16[72,1088]{1,0:T(8,128)(2,1)S(1)}, bf16[72,1088]{1,0:T(8,128)(2,1)S(1)}, u32[]{:S(2)}, u32[]{:S(2)}) collective-permute-start(bf16[72,1088]{1,0:T(8,128)(2,1)S(1)} %add_convert_fusion.16), channel_id=1, source_target_pairs={{0,8},{2,10},{4,12},{6,14},{8,0},{10,2},{12,4},{14,6},{16,24},{18,... | collective-permute-start | bytes 470024 | tf_op jit(solution)/shard_map/ppermute | solution.py:288
  411.8 19.5 %collective-permute-start.49 = (bf16[136,3264]{1,0:T(8,128)(2,1)S(1)}, bf16[136,3264]{1,0:T(8,128)(2,1)}, u32[]{:S(2)}, u32[]{:S(2)}) collective-permute-start(bf16[136,3264]{1,0:T(8,128)(2,1)S(1)} %broadcast_select_fusion.32), channel_id=1, source_target_pairs={{0,4},{2,6},{4,0},{6,2},{8,12},{10,14},{12,8},{14,10},{16,20},{18,... | collective-permute-start | bytes 2663432 | tf_op jit(solution)/shard_map/ppermute | solution.py:288
  414.2 45.2 %collective-permute-start.55 = (f32[12,544]{1,0:T(8,128)S(1)}, f32[12,544]{1,0:T(8,128)}, u32[]{:S(2)}, u32[]{:S(2)}) collective-permute-start(f32[12,544]{1,0:T(8,128)S(1)} %dynamic-slice_bitcast_fusion.9), channel_id=1, source_target_pairs={{0,1},{1,0},{2,3},{3,2},{4,5},{5,4},{6,7},{7,6},{8,9},{9,8},{10,11... | collective-permute-start | bytes 78344 | tf_op jit(solution)/shard_map/ppermute | solution.py:292
  415.9 30.5 %collective-permute-start.48 = (bf16[72,4352]{1,0:T(8,128)(2,1)}, bf16[72,4352]{1,0:T(8,128)(2,1)S(1)}, u32[]{:S(2)}, u32[]{:S(2)}) collective-permute-start(bf16[72,4352]{1,0:T(8,128)(2,1)} %add_convert_fusion.9), channel_id=1, source_target_pairs={{0,16},{2,18},{4,20},{6,22},{8,24},{10,26},{12,28},{14,30},{16,0},... | collective-permute-start | bytes 1880072 | tf_op jit(solution)/shard_map/ppermute | solution.py:288
  416.1 63.0 %collective-permute-start.47 = (bf16[272,2176]{1,0:T(8,128)(2,1)}, bf16[272,2176]{1,0:T(8,128)(2,1)}, u32[]{:S(2)}, u32[]{:S(2)}) collective-permute-start(bf16[272,2176]{1,0:T(8,128)(2,1)} %pad_maximum_fusion.9), channel_id=1, source_target_pairs={{0,4},{2,6},{4,0},{6,2},{8,12},{10,14},{12,8},{14,10},{16,20},{18,... | collective-permute-start | bytes 3551240 | tf_op jit(solution)/shard_map/ppermute | solution.py:288
  417.1 66.6 %collective-permute-start.46 = (bf16[136,1088]{1,0:T(8,128)(2,1)}, bf16[136,1088]{1,0:T(8,128)(2,1)}, u32[]{:S(2)}, u32[]{:S(2)}) collective-permute-start(bf16[136,1088]{1,0:T(8,128)(2,1)} %pad_maximum_fusion.13), channel_id=1, source_target_pairs={{0,4},{2,6},{4,0},{6,2},{8,12},{10,14},{12,8},{14,10},{16,20},{18,... | collective-permute-start | bytes 887816 | tf_op jit(solution)/shard_map/ppermute | solution.py:288
  431.3 20.9 %collective-permute-start.38 = (bf16[1088,512]{1,0:T(8,128)(2,1)}, bf16[1088,512]{1,0:T(8,128)(2,1)}, u32[]{:S(2)}, u32[]{:S(2)}) collective-permute-start(bf16[1088,512]{1,0:T(8,128)(2,1)} %get-tuple-element.284), channel_id=1, source_target_pairs={{0,1},{1,0},{2,3},{3,2},{4,5},{5,4},{6,7},{7,6},{8,9},{9,8},{10,11... | collective-permute-start | bytes 3342344 | tf_op jit(solution)/shard_map/ppermute | solution.py:292
  446.4 13.8 %collective-permute-start.51 = (bf16[72,3264]{1,0:T(8,128)(2,1)S(1)}, bf16[72,3264]{1,0:T(8,128)(2,1)S(1)}, u32[]{:S(2)}, u32[]{:S(2)}) collective-permute-start(bf16[72,3264]{1,0:T(8,128)(2,1)S(1)} %broadcast_select_fusion.47), channel_id=1, source_target_pairs={{0,8},{2,10},{4,12},{6,14},{8,0},{10,2},{12,4},{14,6},{16,24},{18,... | collective-permute-start | bytes 1410056 | tf_op jit(solution)/shard_map/ppermute | solution.py:288
  452.2 25.3 %collective-permute-start.50 = (bf16[72,4352]{1,0:T(8,128)(2,1)S(1)}, bf16[72,4352]{1,0:T(8,128)(2,1)S(1)}, u32[]{:S(2)}, u32[]{:S(2)}) collective-permute-start(bf16[72,4352]{1,0:T(8,128)(2,1)S(1)} %add_convert_fusion.8), channel_id=1, source_target_pairs={{0,8},{2,10},{4,12},{6,14},{8,0},{10,2},{12,4},{14,6},{16,24},{18,... | collective-permute-start | bytes 1880072 | tf_op jit(solution)/shard_map/ppermute | solution.py:288
  460.2 27.5 %collective-permute-start.56 = (f32[12,544]{1,0:T(8,128)S(1)}, f32[12,544]{1,0:T(8,128)S(1)}, u32[]{:S(2)}, u32[]{:S(2)}) collective-permute-start(f32[12,544]{1,0:T(8,128)S(1)} %bitcast_add_fusion), channel_id=1, source_target_pairs={{0,4},{2,6},{4,0},{6,2},{8,12},{10,14},{12,8},{14,10},{16,20},{18,... | collective-permute-start | bytes 78344 | tf_op jit(solution)/shard_map/ppermute | solution.py:288
  460.4 23.3 %collective-permute-start.57 = (bf16[72,3264]{1,0:T(8,128)(2,1)S(1)}, bf16[72,3264]{1,0:T(8,128)(2,1)S(1)}, u32[]{:S(2)}, u32[]{:S(2)}) collective-permute-start(bf16[72,3264]{1,0:T(8,128)(2,1)S(1)} %add_convert_fusion.14), channel_id=1, source_target_pairs={{0,16},{2,18},{4,20},{6,22},{8,24},{10,26},{12,28},{14,30},{16,0},... | collective-permute-start | bytes 1410056 | tf_op jit(solution)/shard_map/ppermute | solution.py:288
  477.8 24.5 %collective-permute-start.54 = (bf16[136,4352]{1,0:T(8,128)(2,1)S(1)}, bf16[136,4352]{1,0:T(8,128)(2,1)S(1)}, u32[]{:S(2)}, u32[]{:S(2)}) collective-permute-start(bf16[136,4352]{1,0:T(8,128)(2,1)S(1)} %pad_maximum_fusion.10), channel_id=1, source_target_pairs={{0,4},{2,6},{4,0},{6,2},{8,12},{10,14},{12,8},{14,10},{16,20},{18,... | collective-permute-start | bytes 3551240 | tf_op jit(solution)/shard_map/ppermute | solution.py:288
  481.0 30.9 %collective-permute-start.53 = (bf16[544,2176]{1,0:T(8,128)(2,1)S(1)}, bf16[544,2176]{1,0:T(8,128)(2,1)S(1)}, u32[]{:S(2)}, u32[]{:S(2)}) collective-permute-start(bf16[544,2176]{1,0:T(8,128)(2,1)S(1)} %pad_maximum_fusion.4), channel_id=1, source_target_pairs={{0,2},{2,0},{4,6},{6,4},{8,10},{10,8},{12,14},{14,12},{16,18},{18,... | collective-permute-start | bytes 7102472 | tf_op jit(solution)/shard_map/ppermute | solution.py:288
  485.1 36.6 %collective-permute-start.52 = (bf16[272,1088]{1,0:T(8,128)(2,1)S(1)}, bf16[272,1088]{1,0:T(8,128)(2,1)S(1)}, u32[]{:S(2)}, u32[]{:S(2)}) collective-permute-start(bf16[272,1088]{1,0:T(8,128)(2,1)S(1)} %pad_maximum_fusion.12), channel_id=1, source_target_pairs={{0,2},{2,0},{4,6},{6,4},{8,10},{10,8},{12,14},{14,12},{16,18},{18,... | collective-permute-start | bytes 1775624 | tf_op jit(solution)/shard_map/ppermute | solution.py:288
  494.0 27.6 %collective-permute-start.60 = (bf16[136,3264]{1,0:T(8,128)(2,1)S(1)}, bf16[136,3264]{1,0:T(8,128)(2,1)S(1)}, u32[]{:S(2)}, u32[]{:S(2)}) collective-permute-start(bf16[136,3264]{1,0:T(8,128)(2,1)S(1)} %pad_maximum_fusion.11), channel_id=1, source_target_pairs={{0,4},{2,6},{4,0},{6,2},{8,12},{10,14},{12,8},{14,10},{16,20},{18,... | collective-permute-start | bytes 2663432 | tf_op jit(solution)/shard_map/ppermute | solution.py:288
  494.7 28.8 %collective-permute-start.61 = (f32[12,544]{1,0:T(8,128)S(1)}, f32[12,544]{1,0:T(8,128)S(1)}, u32[]{:S(2)}, u32[]{:S(2)}) collective-permute-start(f32[12,544]{1,0:T(8,128)S(1)} %add.257), channel_id=1, source_target_pairs={{0,16},{2,18},{4,20},{6,22},{8,24},{10,26},{12,28},{14,30},{16,0},... | collective-permute-start | bytes 78344 | tf_op jit(solution)/shard_map/ppermute | solution.py:288
  504.3 27.3 %collective-permute-start.63 = (bf16[272,4352]{1,0:T(8,128)(2,1)}, bf16[272,4352]{1,0:T(8,128)(2,1)}, u32[]{:S(2)}, u32[]{:S(2)}) collective-permute-start(bf16[272,4352]{1,0:T(8,128)(2,1)} %pad_maximum_fusion.5), channel_id=1, source_target_pairs={{0,2},{2,0},{4,6},{6,4},{8,10},{10,8},{12,14},{14,12},{16,18},{18,... | collective-permute-start | bytes 7102472 | tf_op jit(solution)/shard_map/ppermute | solution.py:288
  (77 other events, 520.4 us)

commit v5 on v4

--- a/solution.py
+++ b/solution.py
@@ -45,7 +45,7 @@
 
 def forward_kernel(pos_ref, q_ref, k_ref, v_ref, ctx_ref, ctx_t_ref, lse_ref, kc_ref, vt_ref, *, span, width):
     pos = pos_ref[0]
-    block = min(256, span)
+    block = min(512, span)
     queries = _clean(q_ref, width)
     kc_ref[...] = _clean(k_ref, width)
     length = k_ref.shape[0]
@@ -101,7 +101,7 @@
 def backward_kernel(pos_ref, q_ref, k_ref, v_ref, g_ref, ctx_ref, lse_ref, dq_ref, dk_ref, dv_ref,
                     kc_ref, vc_ref, kt_ref, dk_acc, dv_acc, *, span, width):
     pos = pos_ref[0]
-    block = min(256, span)
+    block = min(512, span)
     queries = _clean(q_ref, width)
     grads = _clean(g_ref, width)
     context = _clean(ctx_ref, width)
@@ -890,7 +890,6 @@
     way_up.step()
     way_down.step()
     context = tie(context, way_up.latest, way_down.latest)
-    normed_left = for_cores(normed_turned)
     part_up = way_up.finish()
     active, slope, middle_turned, unit_second, rstd_second, two_turned = mlp_up(
         spot, context, full_out, own_tokens, second, bias_up, up_weight, part_up
@@ -901,8 +900,9 @@
     way_down.step()
 
     active_sib = swap(active, CORE_BIT)
+    normed_left = for_cores(normed_turned)
     give, keep_down = turned_weight_grads(
-        spot, *grad_left, tie(active, way_down.latest), active_sib, width // 2, "down_grads"
+        spot, *grad_left, tie(active, way_down.latest, normed_left[0]), active_sib, width // 2, "down_grads"
     )
     sum_down = Steps(reduced(keep_down, give, bits, True))
     part_down = way_down.finish(give)

time: 555 us -> 549 us (0.989)
  the two profiles are of different devices: /device:TPU:27 before, /device:TPU:1 now
where the time goes in v5:
time: 549 us; the launch traced here: 540 us
  waiting for transfers between devices  156 us (28%)
  Pallas kernels  151 us (28%)
  other arithmetic  88 us (16%)
  starting transfers between devices  79.7 us (15%)
  local copies, waits for them, and re-layouts  51.6 us (9%)
  matrix products  10.8 us (2%)
    ppermute x50, waiting for transfers between devices, swap(): return lax.ppermute(values, 'replica', [(i, i ^ bit) for i in range(size)])  112 us
    ppermute x50, starting transfers between devices, swap(): return lax.ppermute(values, 'replica', [(i, i ^ bit) for i in range(size)])  62.7 us
    ppermute x14, waiting for transfers between devices, cross(): return lax.ppermute(values, 'shard', [(0, 1), (1, 0)])  44.5 us
    pallas_call x1, Pallas kernels, mlp_back(): _call(back_kernel, 'mlp_back', _vmem(6) + [any_spec] * 4, [jax.ShapeDtype...  25.9 us
    select_n x38, other arithmetic, choose(): return jnp.where(flag, left, right)  25.8 us
    convert_element_type x18, other arithmetic, low(): return values.astype(jnp.bfloat16)  21.6 us
    pallas_call x1, Pallas kernels, attention_backward(): pl.pallas_call(functools.partial(backward_kernel, span=span, width=width)...  20.5 us
    pallas_call x1, Pallas kernels, mlp_up(): _call(up_kernel, 'mlp_up', _vmem(5) + [any_spec] * 2, [jax.ShapeDtypeStru...  20.2 us
  transfers between devices with their start and end apart: 64, of which 25 were waited for; matrix products, arithmetic and copies ran while one was open for 24% of the time, Pallas kernels for 28%

profile of v5, /device:TPU:1, one launch (start us, length us, event | category | flops | bytes accessed | tf_op | source)
XLA Modules:
  0.0 539.5 jit_solution(4065958803014908115)
XLA Ops:
  10.4 4.3 collective-permute-done
  22.6 6.6 %collective-permute-done.4 = bf16[72,3264]{1,0:T(8,128)(2,1)S(1)} collective-permute-done((bf16[72,3264]{1,0:T(8,128)(2,1)S(1)}, bf16[72,3264]{1,0:T(8,128)(2,1)S(1)}, u32[]{:S(2)}, u32[]{:S(2)}) %collective-permute-start.4) | collective-permute-done | bytes 470048 | tf_op jit(solution)/shard_map/ppermute | solution.py:288
  30.3 12.2 %collective-permute-done.1 = bf16[1088,512]{1,0:T(8,128)(2,1)S(1)} collective-permute-done((bf16[1088,512]{1,0:T(8,128)(2,1)S(1)}, bf16[1088,512]{1,0:T(8,128)(2,1)S(1)}, u32[]{:S(2)}, u32[]{:S(2)}) %collective-permute-start.1) | collective-permute-done | bytes 1114144 | tf_op jit(solution)/shard_map/ppermute | solution.py:292
  46.6 3.0 collective-permute-done.5
  51.1 3.7 collective-permute-start.6
  61.9 6.8 %pad_maximum_fusion.2 = (bf16[1088,1088]{1,0:T(8,128)(2,1)S(1)}, bf16[1088,1088]{1,0:T(8,128)(2,1)S(1)}, bf16[1088,1088]{1,0:T(8,128)(2,1)S(1)}) fusion(bf16[544,3264]{1,0:T(8,128)(2,1)S(1)} %get-tuple-element.346, bf16[544,3264]{1,0:T(8,128)(2,1)S(1)} %get-tuple-element.347), kind=kLoop, calls=%fused_computation.41 | loop fusion | flops 14204928 | bytes 14204928 | tf_op jit(solution)/shard_map/concatenate | solution.py:310
  69.7 4.8 add_convert_fusion.2.v_ref
  78.7 4.0 convolution_convert_fusion.k_ref
  82.8 2.8 collective-permute-done.8
  98.8 12.8 %attention_forward.1 = (bf16[512,1088]{1,0:T(8,128)(2,1)S(1)}, bf16[1088,512]{1,0:T(8,128)(2,1)S(1)}, f32[9,2,512]{2,1,0:T(2,128)S(1)}) custom-call(s32[1]{0:T(128)} %bitcast.pos_ref, bf16[512,1088]{1,0:T(8,128)(2,1)S(1)} %fusion.7.q_ref, bf16[1024,1088]{1,0:T(8,128)(2,1)S(1)} %convolution_convert_fusion.k_ref, bf16[1024,1088]{1,0:T(8,128)(2,1)} %add_convert_fusion.2.v_ref), custom_call_target="tpu_custom_call" | custom-call | flops 1 | bytes 1 | tf_op jit(solution)/shard_map/attention_forward/pallas_call | solution.py:182
  111.7 8.1 %collective-permute-done.12 = bf16[144,4352]{1,0:T(8,128)(2,1)} collective-permute-done((bf16[144,4352]{1,0:T(8,128)(2,1)}, bf16[144,4352]{1,0:T(8,128)(2,1)}, u32[]{:S(2)}, u32[]{:S(2)}) %collective-permute-start.12) | collective-permute-done | bytes 1253408 | tf_op jit(solution)/shard_map/ppermute | solution.py:288
  123.4 2.8 collective-permute-start.15
  131.3 2.8 pad_maximum_fusion.got_ref.up_got
  134.1 20.2 %mlp_up.1 = (bf16[512,4352]{1,0:T(8,128)(2,1)}, bf16[512,4352]{1,0:T(8,128)(2,1)}, f32[1088,512]{1,0:T(8,128)}, f32[512,1088]{1,0:T(8,128)}, f32[512,1]{1,0:T(8,128)}, /*index=5*/bf16[1088,512]{1,0:T(8,128)(2,1)}) custom-call(s32[1]{0:T(128)} %bitcast.pos_ref, bf16[512,1088]{1,0:T(8,128)(2,1)} %copy-done.5, bf16[1088,1088]{1,0:T(8,128)(2,1)} %pad_maximum_fusion.3.out_w_ref, ...), custom_call_target="tpu_custom_call" | custom-call | flops 1 | bytes 1 | tf_op jit(solution)/shard_map/mlp_up/pallas_call | solution.py:424
  167.4 10.7 %down_grads.1 = (bf16[544,2176]{1,0:T(8,128)(2,1)}, bf16[544,2176]{1,0:T(8,128)(2,1)}) custom-call(s32[1]{0:T(128)} %bitcast.pos_ref, bf16[544,512]{1,0:T(8,128)(2,1)} %get-tuple-element.393.left_own, bf16[544,512]{1,0:T(8,128)(2,1)} %copy-done.52, bf16[512,4352]{1,0:T(8,128)(2,1)} %get-tuple-element.231.right_own.act_ref, ...), custom_call_target="tpu_custom_call" | custom-call | flops 1 | bytes 1 | tf_op jit(solution)/shard_map/down_grads/pallas_call | solution.py:600
  178.1 2.8 slice.185
  180.9 2.7 collective-permute-start.22
  183.7 2.8 broadcast_select_fusion.8
  189.6 11.1 %mlp_down.1 = bf16[1088,512]{1,0:T(8,128)(2,1)} custom-call(s32[1]{0:T(128)} %bitcast.pos_ref, bf16[512,4352]{1,0:T(8,128)(2,1)} %get-tuple-element.231.right_own.act_ref, bf16[1088,2176]{1,0:T(8,128)(2,1)} %bitcast.77, bf16[1088,2176]{1,0:T(8,128)(2,1)} %constant_dynamic-update-slice_fusion.16.got_ref.down_got, f32[1088,512]{1,0:T(8,128)} %get-tuple-element.235.middle_ref, ...), custom_call_target="tpu_custom_call" | custom-call | flops 1 | bytes 1 | tf_op jit(solution)/shard_map/mlp_down/pallas_call | solution.py:456
  201.6 25.9 %mlp_back.1 = (bf16[512,4352]{1,0:T(8,128)(2,1)}, f32[512,1088]{1,0:T(8,128)}, bf16[512,1152]{1,0:T(8,128)(2,1)}, bf16[512,1088]{1,0:T(8,128)(2,1)}, f32[1,4352]{1,0:T(1,128)}, /*index=5*/f32[8,1088]{1,0:T(8,128)}) custom-call(s32[1]{0:T(128)} %bitcast.pos_ref, bf16[512,1088]{1,0:T(8,128)(2,1)} %bitcast.79, bf16[512,4352]{1,0:T(8,128)(2,1)} %get-tuple-element.239.slope_ref, ...), custom_call_target="tpu_custom_call" | custom-call | flops 1 | bytes 1 | tf_op jit(solution)/shard_map/mlp_back/pallas_call | solution.py:532
  230.6 4.6 collective-permute-done.24.right_sib
  236.3 5.1 out_grads.1
  241.3 9.8 %up_grads.1 = (bf16[272,4352]{1,0:T(8,128)(2,1)}, bf16[272,4352]{1,0:T(8,128)(2,1)}) custom-call(s32[1]{0:T(128)} %bitcast.pos_ref, bf16[2,272,512]{2,1,0:T(8,128)(2,1)} %get-tuple-element.391.left_own, bf16[2,272,512]{2,1,0:T(8,128)(2,1)} %copy-done.51, bf16[512,4352]{1,0:T(8,128)(2,1)} %get-tuple-element.249.right_own, ...), custom_call_target="tpu_custom_call" | custom-call | flops 1 | bytes 1 | tf_op jit(solution)/shard_map/up_grads/pallas_call | solution.py:567
  262.8 20.5 %attention_backward.1 = (bf16[512,1152]{1,0:T(8,128)(2,1)S(1)}, bf16[1024,1152]{1,0:T(8,128)(2,1)}, bf16[1024,1152]{1,0:T(8,128)(2,1)}) custom-call(s32[1]{0:T(128)} %bitcast.pos_ref, bf16[512,1088]{1,0:T(8,128)(2,1)S(1)} %copy-done.4, bf16[1024,1088]{1,0:T(8,128)(2,1)} %copy-done.2, bf16[1024,1088]{1,0:T(8,128)(2,1)} %add_convert_fusion.2.v_ref, ...), custom_call_target="tpu_custom_call" | custom-call | flops 1 | bytes 1 | tf_op jit(solution)/shard_map/attention_backward/pallas_call | solution.py:212
  283.3 21.1 %collective-permute-done.27 = bf16[272,1088]{1,0:T(8,128)(2,1)S(1)} collective-permute-done((bf16[272,1088]{1,0:T(8,128)(2,1)}, bf16[272,1088]{1,0:T(8,128)(2,1)S(1)}, u32[]{:S(2)}, u32[]{:S(2)}) %collective-permute-start.27) | collective-permute-done | bytes 591904 | tf_op jit(solution)/shard_map/ppermute | solution.py:292
  311.6 13.7 %input_grads.1 = (f32[1088,512]{1,0:T(8,128)}, bf16[1088,512]{1,0:T(8,128)(2,1)}) custom-call(s32[1]{0:T(128)} %bitcast.pos_ref, bf16[1088,1088]{1,0:T(8,128)(2,1)} %copy-done.25, bf16[1088,1088]{1,0:T(8,128)(2,1)} %copy-done.27, bf16[1088,1088]{1,0:T(8,128)(2,1)} %copy-done.26, bf16[512,1152]{1,0:T(8,128)(2,1)} %copy-done, ...), custom_call_target="tpu_custom_call" | custom-call | flops 1 | bytes 1 | tf_op jit(solution)/shard_map/input_grads/pallas_call | solution.py:662
  328.2 2.9 add_convert_fusion
  343.2 14.6 %qkv_weight_grads.1 = (bf16[272,3264]{1,0:T(8,128)(2,1)}, bf16[272,3264]{1,0:T(8,128)(2,1)}) custom-call(s32[1]{0:T(128)} %bitcast.pos_ref, bf16[2,272,1024]{2,1,0:T(8,128)(2,1)} %get-tuple-element.371.left_own, bf16[2,272,1024]{2,1,0:T(8,128)(2,1)} %collective-permute-done.32.left_sib, bf16[512,1152]{1,0:T(8,128)(2,1)} %copy-done, ...), custom_call_target="tpu_custom_call" | custom-call | flops 1 | bytes 1 | tf_op jit(solution)/shard_map/qkv_weight_grads/pallas_call | solution.py:639
  364.5 4.5 collective-permute-done.40
  370.1 2.5 collective-permute-start.44
  372.8 7.8 %collective-permute-done.39 = bf16[72,1088]{1,0:T(8,128)(2,1)S(1)} collective-permute-done((bf16[72,1088]{1,0:T(8,128)(2,1)S(1)}, bf16[72,1088]{1,0:T(8,128)(2,1)S(1)}, u32[]{:S(2)}, u32[]{:S(2)}) %collective-permute-start.39) | collective-permute-done | bytes 156704 | tf_op jit(solution)/shard_map/ppermute | solution.py:288
  381.4 7.7 %collective-permute-done.44 = bf16[72,4352]{1,0:T(8,128)(2,1)S(1)} collective-permute-done((bf16[72,4352]{1,0:T(8,128)(2,1)S(1)}, bf16[72,4352]{1,0:T(8,128)(2,1)S(1)}, u32[]{:S(2)}, u32[]{:S(2)}) %collective-permute-start.44) | collective-permute-done | bytes 626720 | tf_op jit(solution)/shard_map/ppermute | solution.py:288
  390.2 11.5 %collective-permute-done.43 = bf16[136,2176]{1,0:T(8,128)(2,1)S(1)} collective-permute-done((bf16[136,2176]{1,0:T(8,128)(2,1)S(1)}, bf16[136,2176]{1,0:T(8,128)(2,1)S(1)}, u32[]{:S(2)}, u32[]{:S(2)}) %collective-permute-start.43) | collective-permute-done | bytes 591904 | tf_op jit(solution)/shard_map/ppermute | solution.py:288
  414.2 13.5 %collective-permute-done.49 = bf16[136,3264]{1,0:T(8,128)(2,1)} collective-permute-done((bf16[136,3264]{1,0:T(8,128)(2,1)S(1)}, bf16[136,3264]{1,0:T(8,128)(2,1)}, u32[]{:S(2)}, u32[]{:S(2)}) %collective-permute-start.49) | collective-permute-done | bytes 887840 | tf_op jit(solution)/shard_map/ppermute | solution.py:288
  431.0 11.1 %collective-permute-done.48 = bf16[72,4352]{1,0:T(8,128)(2,1)S(1)} collective-permute-done((bf16[72,4352]{1,0:T(8,128)(2,1)}, bf16[72,4352]{1,0:T(8,128)(2,1)S(1)}, u32[]{:S(2)}, u32[]{:S(2)}) %collective-permute-start.48) | collective-permute-done | bytes 626720 | tf_op jit(solution)/shard_map/ppermute | solution.py:288
  443.3 5.4 %collective-permute-done.38.other_ref = bf16[1088,512]{1,0:T(8,128)(2,1)} collective-permute-done((bf16[1088,512]{1,0:T(8,128)(2,1)}, bf16[1088,512]{1,0:T(8,128)(2,1)}, u32[]{:S(2)}, u32[]{:S(2)}) %collective-permute-start.38) | collective-permute-done | bytes 1114144 | tf_op jit(solution)/shard_map/ppermute | solution.py:292
  448.7 6.4 %token_grads.1 = bf16[1088,512]{1,0:T(8,128)(2,1)} custom-call(s32[1]{0:T(128)} %bitcast.pos_ref, f32[1088,512]{1,0:T(8,128)} %get-tuple-element.274.mine_ref, bf16[1088,512]{1,0:T(8,128)(2,1)} %collective-permute-done.38.other_ref, bf16[1088,512]{1,0:T(8,128)(2,1)} %bitcast.72, f32[1088,1]{1,0:T(8,128)} %copy.55.gain_ref, ...), custom_call_target="tpu_custom_call" | custom-call | flops 1 | bytes 1 | tf_op jit(solution)/shard_map/token_grads/pallas_call | solution.py:686
  458.9 13.5 %collective-permute-done.50 = bf16[72,4352]{1,0:T(8,128)(2,1)S(1)} collective-permute-done((bf16[72,4352]{1,0:T(8,128)(2,1)S(1)}, bf16[72,4352]{1,0:T(8,128)(2,1)S(1)}, u32[]{:S(2)}, u32[]{:S(2)}) %collective-permute-start.50) | collective-permute-done | bytes 626720 | tf_op jit(solution)/shard_map/ppermute | solution.py:288
  476.1 3.7 collective-permute-start.53
  481.2 3.0 collective-permute-start.52
  486.0 3.6 collective-permute-done.59
  491.0 5.4 collective-permute-done.54
  498.4 9.1 %collective-permute-start.63 = (bf16[272,4352]{1,0:T(8,128)(2,1)}, bf16[272,4352]{1,0:T(8,128)(2,1)}, u32[]{:S(2)}, u32[]{:S(2)}) collective-permute-start(bf16[272,4352]{1,0:T(8,128)(2,1)} %pad_maximum_fusion.5), channel_id=1, source_target_pairs={{0,2},{2,0},{4,6},{6,4},{8,10},{10,8},{12,14},{14,12},{16,18},{18,... | collective-permute-start | bytes 7102472 | tf_op jit(solution)/shard_map/ppermute | solution.py:288
  508.5 4.4 maximum_convert_fusion
  512.8 3.0 collective-permute-done.60
  520.4 4.8 collective-permute-start.62
  529.0 4.4 maximum_convert_fusion.1
  535.5 3.5 maximum_convert_fusion.2
  (391 shorter events, 164.9 us)
Async XLA Ops:
  18.2 24.3 %collective-permute-start.1 = (bf16[1088,512]{1,0:T(8,128)(2,1)S(1)}, bf16[1088,512]{1,0:T(8,128)(2,1)S(1)}, u32[]{:S(2)}, u32[]{:S(2)}) collective-permute-start(bf16[1088,512]{1,0:T(8,128)(2,1)S(1)} %bitcast.73), channel_id=1, source_target_pairs={{0,1},{1,0},{2,3},{3,2},{4,5},{5,4},{6,7},{7,6},{8,9},{9,8},{10,11... | collective-permute-start | bytes 3342344 | tf_op jit(solution)/shard_map/ppermute | solution.py:292
  29.4 20.2 %collective-permute-start.5 = (bf16[144,3264]{1,0:T(8,128)(2,1)S(1)}, bf16[144,3264]{1,0:T(8,128)(2,1)}, u32[]{:S(2)}, u32[]{:S(2)}) collective-permute-start(bf16[144,3264]{1,0:T(8,128)(2,1)S(1)} %constant_dynamic-update-slice_fusion), channel_id=1, source_target_pairs={{0,4},{2,6},{4,0},{6,2},{8,12},{10,14},{12,8},{14,10},{16,20},{18,... | collective-permute-start | bytes 2820104 | tf_op jit(solution)/shard_map/ppermute | solution.py:288
  43.7 25.0 %collective-permute-start.3 = (bf16[72,1088]{1,0:T(8,128)(2,1)S(1)}, bf16[72,1088]{1,0:T(8,128)(2,1)S(1)}, u32[]{:S(2)}, u32[]{:S(2)}) collective-permute-start(bf16[72,1088]{1,0:T(8,128)(2,1)S(1)} %constant_dynamic-slice_fusion.2), channel_id=1, source_target_pairs={{0,1},{1,0},{2,3},{3,2},{4,5},{5,4},{6,7},{7,6},{8,9},{9,8},{10,11... | collective-permute-start | bytes 470024 | tf_op jit(solution)/shard_map/ppermute | solution.py:292
  45.7 28.8 %collective-permute-start.9 = (bf16[72,4352]{1,0:T(8,128)(2,1)S(1)}, bf16[72,4352]{1,0:T(8,128)(2,1)S(1)}, u32[]{:S(2)}, u32[]{:S(2)}) collective-permute-start(bf16[72,4352]{1,0:T(8,128)(2,1)S(1)} %constant_dynamic-slice_fusion.1), channel_id=1, source_target_pairs={{0,1},{1,0},{2,3},{3,2},{4,5},{5,4},{6,7},{7,6},{8,9},{9,8},{10,11... | collective-permute-start | bytes 1880072 | tf_op jit(solution)/shard_map/ppermute | solution.py:292
  74.5 15.9 %collective-permute-start.10 = (bf16[72,4352]{1,0:T(8,128)(2,1)S(1)}, bf16[72,4352]{1,0:T(8,128)(2,1)S(1)}, u32[]{:S(2)}, u32[]{:S(2)}) collective-permute-start(bf16[72,4352]{1,0:T(8,128)(2,1)S(1)} %collective-permute-done.9), channel_id=1, source_target_pairs={{0,4},{2,6},{4,0},{6,2},{8,12},{10,14},{12,8},{14,10},{16,20},{18,... | collective-permute-start | bytes 1880072 | tf_op jit(solution)/shard_map/ppermute | solution.py:288
  76.4 14.1 %collective-permute-start.11 = (bf16[136,2176]{1,0:T(8,128)(2,1)S(1)}, bf16[136,2176]{1,0:T(8,128)(2,1)}, u32[]{:S(2)}, u32[]{:S(2)}) collective-permute-start(bf16[136,2176]{1,0:T(8,128)(2,1)S(1)} %constant_dynamic-slice_fusion), channel_id=1, source_target_pairs={{0,1},{1,0},{2,3},{3,2},{4,5},{5,4},{6,7},{7,6},{8,9},{9,8},{10,11... | collective-permute-start | bytes 1775624 | tf_op jit(solution)/shard_map/ppermute | solution.py:292
  92.3 27.5 %collective-permute-start.12 = (bf16[144,4352]{1,0:T(8,128)(2,1)}, bf16[144,4352]{1,0:T(8,128)(2,1)}, u32[]{:S(2)}, u32[]{:S(2)}) collective-permute-start(bf16[144,4352]{1,0:T(8,128)(2,1)} %constant_dynamic-update-slice_fusion.8), channel_id=1, source_target_pairs={{0,8},{2,10},{4,12},{6,14},{8,0},{10,2},{12,4},{14,6},{16,24},{18,... | collective-permute-start | bytes 3760136 | tf_op jit(solution)/shard_map/ppermute | solution.py:288
  93.2 18.5 %collective-permute-start.14 = (bf16[288,1088]{1,0:T(8,128)(2,1)}, bf16[288,1088]{1,0:T(8,128)(2,1)}, u32[]{:S(2)}, u32[]{:S(2)}) collective-permute-start(bf16[288,1088]{1,0:T(8,128)(2,1)} %constant_dynamic-update-slice_fusion.6), channel_id=1, source_target_pairs={{0,2},{2,0},{4,6},{6,4},{8,10},{10,8},{12,14},{14,12},{16,18},{18,... | collective-permute-start | bytes 1880072 | tf_op jit(solution)/shard_map/ppermute | solution.py:288
  95.3 16.4 %collective-permute-start.13 = (bf16[136,2176]{1,0:T(8,128)(2,1)}, bf16[136,2176]{1,0:T(8,128)(2,1)}, u32[]{:S(2)}, u32[]{:S(2)}) collective-permute-start(bf16[136,2176]{1,0:T(8,128)(2,1)} %collective-permute-done.11), channel_id=1, source_target_pairs={{0,4},{2,6},{4,0},{6,2},{8,12},{10,14},{12,8},{14,10},{16,20},{18,... | collective-permute-start | bytes 1775624 | tf_op jit(solution)/shard_map/ppermute | solution.py:288
  127.6 27.7 %collective-permute-start.16 = (bf16[272,2176]{1,0:T(8,128)(2,1)S(1)}, bf16[272,2176]{1,0:T(8,128)(2,1)S(1)}, u32[]{:S(2)}, u32[]{:S(2)}) collective-permute-start(bf16[272,2176]{1,0:T(8,128)(2,1)S(1)} %constant_dynamic-update-slice_fusion.12), channel_id=1, source_target_pairs={{0,8},{2,10},{4,12},{6,14},{8,0},{10,2},{12,4},{14,6},{16,24},{18,... | collective-permute-start | bytes 3551240 | tf_op jit(solution)/shard_map/ppermute | solution.py:288
  158.7 22.2 %collective-permute-start.19 = (bf16[544,2176]{1,0:T(8,128)(2,1)}, bf16[544,2176]{1,0:T(8,128)(2,1)}, u32[]{:S(2)}, u32[]{:S(2)}) collective-permute-start(bf16[544,2176]{1,0:T(8,128)(2,1)} %constant_dynamic-update-slice_fusion.14), channel_id=1, source_target_pairs={{0,2},{2,0},{4,6},{6,4},{8,10},{10,8},{12,14},{14,12},{16,18},{18,... | collective-permute-start | bytes 7102472 | tf_op jit(solution)/shard_map/ppermute | solution.py:288
  165.1 35.6 %collective-permute-start.21 = (bf16[2,272,512]{2,1,0:T(8,128)(2,1)S(1)}, bf16[2,272,512]{2,1,0:T(8,128)(2,1)S(1)}, u32[]{:S(2)}, u32[]{:S(2)}) collective-permute-start(bf16[2,272,512]{2,1,0:T(8,128)(2,1)S(1)} %get-tuple-element.388), channel_id=1, source_target_pairs={{0,2},{2,0},{4,6},{6,4},{8,10},{10,8},{12,14},{14,12},{16,18},{18,... | collective-permute-start | bytes 1671176 | tf_op jit(solution)/shard_map/ppermute | solution.py:288
  166.1 34.7 %collective-permute-start.20 = (bf16[2,272,512]{2,1,0:T(8,128)(2,1)S(1)}, bf16[2,272,512]{2,1,0:T(8,128)(2,1)S(1)}, u32[]{:S(2)}, u32[]{:S(2)}) collective-permute-start(bf16[2,272,512]{2,1,0:T(8,128)(2,1)S(1)} %get-tuple-element.390), channel_id=1, source_target_pairs={{0,2},{2,0},{4,6},{6,4},{8,10},{10,8},{12,14},{14,12},{16,18},{18,... | collective-permute-start | bytes 1671176 | tf_op jit(solution)/shard_map/ppermute | solution.py:288
  180.9 46.6 %collective-permute-start.22 = (bf16[408,2176]{1,0:T(8,128)(2,1)}, bf16[408,2176]{1,0:T(8,128)(2,1)}, u32[]{:S(2)}, u32[]{:S(2)}) collective-permute-start(bf16[408,2176]{1,0:T(8,128)(2,1)} %slice.185), channel_id=1, source_target_pairs={{0,1},{1,0},{2,3},{3,2},{4,5},{5,4},{6,7},{7,6},{8,9},{9,8},{10,11... | collective-permute-start | bytes 5326856 | tf_op jit(solution)/shard_map/ppermute | solution.py:292
  230.1 21.1 %collective-permute-start.25 = (bf16[136,2176]{1,0:T(8,128)(2,1)}, bf16[136,2176]{1,0:T(8,128)(2,1)}, u32[]{:S(2)}, u32[]{:S(2)}) collective-permute-start(bf16[136,2176]{1,0:T(8,128)(2,1)} %slice.186), channel_id=1, source_target_pairs={{0,1},{1,0},{2,3},{3,2},{4,5},{5,4},{6,7},{7,6},{8,9},{9,8},{10,11... | collective-permute-start | bytes 1775624 | tf_op jit(solution)/shard_map/ppermute | solution.py:292
  252.9 51.5 %collective-permute-start.28 = (bf16[192,4352]{1,0:T(8,128)(2,1)S(1)}, bf16[192,4352]{1,0:T(8,128)(2,1)S(1)}, u32[]{:S(2)}, u32[]{:S(2)}) collective-permute-start(bf16[192,4352]{1,0:T(8,128)(2,1)S(1)} %slice.189), channel_id=1, source_target_pairs={{0,1},{1,0},{2,3},{3,2},{4,5},{5,4},{6,7},{7,6},{8,9},{9,8},{10,11... | collective-permute-start | bytes 5013512 | tf_op jit(solution)/shard_map/ppermute | solution.py:292
  256.9 47.4 %collective-permute-start.26 = (bf16[272,2176]{1,0:T(8,128)(2,1)S(1)}, bf16[272,2176]{1,0:T(8,128)(2,1)S(1)}, u32[]{:S(2)}, u32[]{:S(2)}) collective-permute-start(bf16[272,2176]{1,0:T(8,128)(2,1)S(1)} %broadcast_select_fusion.23), channel_id=1, source_target_pairs={{0,4},{2,6},{4,0},{6,2},{8,12},{10,14},{12,8},{14,10},{16,20},{18,... | collective-permute-start | bytes 3551240 | tf_op jit(solution)/shard_map/ppermute | solution.py:288
  257.6 80.5 %collective-permute-start.32 = (bf16[2,272,1024]{2,1,0:T(8,128)(2,1)}, bf16[2,272,1024]{2,1,0:T(8,128)(2,1)}, u32[]{:S(2)}, u32[]{:S(2)}) collective-permute-start(bf16[2,272,1024]{2,1,0:T(8,128)(2,1)} %get-tuple-element.370), channel_id=1, source_target_pairs={{0,2},{2,0},{4,6},{6,4},{8,10},{10,8},{12,14},{14,12},{16,18},{18,... | collective-permute-start | bytes 3342344 | tf_op jit(solution)/shard_map/ppermute | solution.py:288
  258.8 45.5 %collective-permute-start.27 = (bf16[272,1088]{1,0:T(8,128)(2,1)}, bf16[272,1088]{1,0:T(8,128)(2,1)S(1)}, u32[]{:S(2)}, u32[]{:S(2)}) collective-permute-start(bf16[272,1088]{1,0:T(8,128)(2,1)} %get-tuple-element.251), channel_id=1, source_target_pairs={{0,1},{1,0},{2,3},{3,2},{4,5},{5,4},{6,7},{7,6},{8,9},{9,8},{10,11... | collective-permute-start | bytes 1775624 | tf_op jit(solution)/shard_map/ppermute | solution.py:292
  261.4 66.2 %collective-permute-start.29 = (bf16[80,4352]{1,0:T(8,128)(2,1)}, bf16[80,4352]{1,0:T(8,128)(2,1)}, u32[]{:S(2)}, u32[]{:S(2)}) collective-permute-start(bf16[80,4352]{1,0:T(8,128)(2,1)} %slice.190), channel_id=1, source_target_pairs={{0,1},{1,0},{2,3},{3,2},{4,5},{5,4},{6,7},{7,6},{8,9},{9,8},{10,11... | collective-permute-start | bytes 2088968 | tf_op jit(solution)/shard_map/ppermute | solution.py:292
  306.7 21.5 %collective-permute-start.30 = (bf16[136,2176]{1,0:T(8,128)(2,1)}, bf16[136,2176]{1,0:T(8,128)(2,1)}, u32[]{:S(2)}, u32[]{:S(2)}) collective-permute-start(bf16[136,2176]{1,0:T(8,128)(2,1)} %broadcast_select_fusion.43), channel_id=1, source_target_pairs={{0,8},{2,10},{4,12},{6,14},{8,0},{10,2},{12,4},{14,6},{16,24},{18,... | collective-permute-start | bytes 1775624 | tf_op jit(solution)/shard_map/ppermute | solution.py:288
  309.0 18.7 %collective-permute-start.31 = (bf16[136,1088]{1,0:T(8,128)(2,1)}, bf16[136,1088]{1,0:T(8,128)(2,1)}, u32[]{:S(2)}, u32[]{:S(2)}) collective-permute-start(bf16[136,1088]{1,0:T(8,128)(2,1)} %broadcast_select_fusion.54), channel_id=1, source_target_pairs={{0,4},{2,6},{4,0},{6,2},{8,12},{10,14},{12,8},{14,10},{16,20},{18,... | collective-permute-start | bytes 887816 | tf_op jit(solution)/shard_map/ppermute | solution.py:288
  309.5 33.7 %collective-permute-start.34 = (bf16[1024,1152]{1,0:T(8,128)(2,1)}, bf16[1024,1152]{1,0:T(8,128)(2,1)}, u32[]{:S(2)}, u32[]{:S(2)}) collective-permute-start(bf16[1024,1152]{1,0:T(8,128)(2,1)} %get-tuple-element.270.gk_ref.k_own), channel_id=1, source_target_pairs={{0,2},{2,0},{4,6},{6,4},{8,10},{10,8},{12,14},{14,12},{16,18},{18,... | collective-permute-start | bytes 7077896 | tf_op jit(solution)/shard_map/ppermute | solution.py:288
  327.6 15.6 %collective-permute-start.35 = (bf16[1024,1152]{1,0:T(8,128)(2,1)}, bf16[1024,1152]{1,0:T(8,128)(2,1)}, u32[]{:S(2)}, u32[]{:S(2)}) collective-permute-start(bf16[1024,1152]{1,0:T(8,128)(2,1)} %get-tuple-element.271.gv_ref.v_own), channel_id=1, source_target_pairs={{0,2},{2,0},{4,6},{6,4},{8,10},{10,8},{12,14},{14,12},{16,18},{18,... | collective-permute-start | bytes 7077896 | tf_op jit(solution)/shard_map/ppermute | solution.py:288
  334.8 27.9 %collective-permute-start.41 = (bf16[136,4352]{1,0:T(8,128)(2,1)}, bf16[136,4352]{1,0:T(8,128)(2,1)}, u32[]{:S(2)}, u32[]{:S(2)}) collective-permute-start(bf16[136,4352]{1,0:T(8,128)(2,1)} %broadcast_select_fusion.20), channel_id=1, source_target_pairs={{0,4},{2,6},{4,0},{6,2},{8,12},{10,14},{12,8},{14,10},{16,20},{18,... | collective-permute-start | bytes 3551240 | tf_op jit(solution)/shard_map/ppermute | solution.py:288
  338.1 19.7 %collective-permute-start.36 = (bf16[72,1088]{1,0:T(8,128)(2,1)}, bf16[72,1088]{1,0:T(8,128)(2,1)}, u32[]{:S(2)}, u32[]{:S(2)}) collective-permute-start(bf16[72,1088]{1,0:T(8,128)(2,1)} %broadcast_select_fusion.56), channel_id=1, source_target_pairs={{0,8},{2,10},{4,12},{6,14},{8,0},{10,2},{12,4},{14,6},{16,24},{18,... | collective-permute-start | bytes 470024 | tf_op jit(solution)/shard_map/ppermute | solution.py:288
  340.8 28.2 %collective-permute-start.40 = (bf16[136,2176]{1,0:T(8,128)(2,1)}, bf16[136,2176]{1,0:T(8,128)(2,1)S(1)}, u32[]{:S(2)}, u32[]{:S(2)}) collective-permute-start(bf16[136,2176]{1,0:T(8,128)(2,1)} %add_convert_fusion.12), channel_id=1, source_target_pairs={{0,16},{2,18},{4,20},{6,22},{8,24},{10,26},{12,28},{14,30},{16,0},... | collective-permute-start | bytes 1775624 | tf_op jit(solution)/shard_map/ppermute | solution.py:288
  357.8 48.3 %collective-permute-start.37 = (bf16[272,3264]{1,0:T(8,128)(2,1)}, bf16[272,3264]{1,0:T(8,128)(2,1)}, u32[]{:S(2)}, u32[]{:S(2)}) collective-permute-start(bf16[272,3264]{1,0:T(8,128)(2,1)} %get-tuple-element.283), channel_id=1, source_target_pairs={{0,1},{1,0},{2,3},{3,2},{4,5},{5,4},{6,7},{7,6},{8,9},{9,8},{10,11... | collective-permute-start | bytes 5326856 | tf_op jit(solution)/shard_map/ppermute | solution.py:292
  360.9 19.8 %collective-permute-start.45 = (f32[2,12,544]{2,1,0:T(8,128)S(1)}, f32[2,12,544]{2,1,0:T(8,128)S(1)}, u32[]{:S(2)}, u32[]{:S(2)}) collective-permute-start(f32[2,12,544]{2,1,0:T(8,128)S(1)} %concatenate.129), channel_id=1, source_target_pairs={{0,2},{2,0},{4,6},{6,4},{8,10},{10,8},{12,14},{14,12},{16,18},{18,... | collective-permute-start | bytes 156680 | tf_op jit(solution)/shard_map/ppermute | solution.py:288
  370.1 19.0 %collective-permute-start.44 = (bf16[72,4352]{1,0:T(8,128)(2,1)S(1)}, bf16[72,4352]{1,0:T(8,128)(2,1)S(1)}, u32[]{:S(2)}, u32[]{:S(2)}) collective-permute-start(bf16[72,4352]{1,0:T(8,128)(2,1)S(1)} %broadcast_select_fusion.36), channel_id=1, source_target_pairs={{0,8},{2,10},{4,12},{6,14},{8,0},{10,2},{12,4},{14,6},{16,24},{18,... | collective-permute-start | bytes 1880072 | tf_op jit(solution)/shard_map/ppermute | solution.py:288
  372.7 28.9 %collective-permute-start.43 = (bf16[136,2176]{1,0:T(8,128)(2,1)S(1)}, bf16[136,2176]{1,0:T(8,128)(2,1)S(1)}, u32[]{:S(2)}, u32[]{:S(2)}) collective-permute-start(bf16[136,2176]{1,0:T(8,128)(2,1)S(1)} %add_convert_fusion.11), channel_id=1, source_target_pairs={{0,8},{2,10},{4,12},{6,14},{8,0},{10,2},{12,4},{14,6},{16,24},{18,... | collective-permute-start | bytes 1775624 | tf_op jit(solution)/shard_map/ppermute | solution.py:288
  380.7 24.6 %collective-permute-start.42 = (bf16[72,1088]{1,0:T(8,128)(2,1)S(1)}, bf16[72,1088]{1,0:T(8,128)(2,1)S(1)}, u32[]{:S(2)}, u32[]{:S(2)}) collective-permute-start(bf16[72,1088]{1,0:T(8,128)(2,1)S(1)} %add_convert_fusion.16), channel_id=1, source_target_pairs={{0,8},{2,10},{4,12},{6,14},{8,0},{10,2},{12,4},{14,6},{16,24},{18,... | collective-permute-start | bytes 470024 | tf_op jit(solution)/shard_map/ppermute | solution.py:288
  408.2 19.5 %collective-permute-start.49 = (bf16[136,3264]{1,0:T(8,128)(2,1)S(1)}, bf16[136,3264]{1,0:T(8,128)(2,1)}, u32[]{:S(2)}, u32[]{:S(2)}) collective-permute-start(bf16[136,3264]{1,0:T(8,128)(2,1)S(1)} %broadcast_select_fusion.32), channel_id=1, source_target_pairs={{0,4},{2,6},{4,0},{6,2},{8,12},{10,14},{12,8},{14,10},{16,20},{18,... | collective-permute-start | bytes 2663432 | tf_op jit(solution)/shard_map/ppermute | solution.py:288
  410.6 44.5 %collective-permute-start.55 = (f32[12,544]{1,0:T(8,128)S(1)}, f32[12,544]{1,0:T(8,128)}, u32[]{:S(2)}, u32[]{:S(2)}) collective-permute-start(f32[12,544]{1,0:T(8,128)S(1)} %dynamic-slice_bitcast_fusion.9), channel_id=1, source_target_pairs={{0,1},{1,0},{2,3},{3,2},{4,5},{5,4},{6,7},{7,6},{8,9},{9,8},{10,11... | collective-permute-start | bytes 78344 | tf_op jit(solution)/shard_map/ppermute | solution.py:292
  412.3 29.8 %collective-permute-start.48 = (bf16[72,4352]{1,0:T(8,128)(2,1)}, bf16[72,4352]{1,0:T(8,128)(2,1)S(1)}, u32[]{:S(2)}, u32[]{:S(2)}) collective-permute-start(bf16[72,4352]{1,0:T(8,128)(2,1)} %add_convert_fusion.9), channel_id=1, source_target_pairs={{0,16},{2,18},{4,20},{6,22},{8,24},{10,26},{12,28},{14,30},{16,0},... | collective-permute-start | bytes 1880072 | tf_op jit(solution)/shard_map/ppermute | solution.py:288
  412.7 61.5 %collective-permute-start.47 = (bf16[272,2176]{1,0:T(8,128)(2,1)}, bf16[272,2176]{1,0:T(8,128)(2,1)}, u32[]{:S(2)}, u32[]{:S(2)}) collective-permute-start(bf16[272,2176]{1,0:T(8,128)(2,1)} %pad_maximum_fusion.9), channel_id=1, source_target_pairs={{0,4},{2,6},{4,0},{6,2},{8,12},{10,14},{12,8},{14,10},{16,20},{18,... | collective-permute-start | bytes 3551240 | tf_op jit(solution)/shard_map/ppermute | solution.py:288
  413.4 66.4 %collective-permute-start.46 = (bf16[136,1088]{1,0:T(8,128)(2,1)}, bf16[136,1088]{1,0:T(8,128)(2,1)}, u32[]{:S(2)}, u32[]{:S(2)}) collective-permute-start(bf16[136,1088]{1,0:T(8,128)(2,1)} %pad_maximum_fusion.13), channel_id=1, source_target_pairs={{0,4},{2,6},{4,0},{6,2},{8,12},{10,14},{12,8},{14,10},{16,20},{18,... | collective-permute-start | bytes 887816 | tf_op jit(solution)/shard_map/ppermute | solution.py:288
  427.7 21.0 %collective-permute-start.38 = (bf16[1088,512]{1,0:T(8,128)(2,1)}, bf16[1088,512]{1,0:T(8,128)(2,1)}, u32[]{:S(2)}, u32[]{:S(2)}) collective-permute-start(bf16[1088,512]{1,0:T(8,128)(2,1)} %get-tuple-element.284), channel_id=1, source_target_pairs={{0,1},{1,0},{2,3},{3,2},{4,5},{5,4},{6,7},{7,6},{8,9},{9,8},{10,11... | collective-permute-start | bytes 3342344 | tf_op jit(solution)/shard_map/ppermute | solution.py:292
  442.0 14.7 %collective-permute-start.51 = (bf16[72,3264]{1,0:T(8,128)(2,1)S(1)}, bf16[72,3264]{1,0:T(8,128)(2,1)S(1)}, u32[]{:S(2)}, u32[]{:S(2)}) collective-permute-start(bf16[72,3264]{1,0:T(8,128)(2,1)S(1)} %broadcast_select_fusion.47), channel_id=1, source_target_pairs={{0,8},{2,10},{4,12},{6,14},{8,0},{10,2},{12,4},{14,6},{16,24},{18,... | collective-permute-start | bytes 1410056 | tf_op jit(solution)/shard_map/ppermute | solution.py:288
  448.7 23.7 %collective-permute-start.50 = (bf16[72,4352]{1,0:T(8,128)(2,1)S(1)}, bf16[72,4352]{1,0:T(8,128)(2,1)S(1)}, u32[]{:S(2)}, u32[]{:S(2)}) collective-permute-start(bf16[72,4352]{1,0:T(8,128)(2,1)S(1)} %add_convert_fusion.8), channel_id=1, source_target_pairs={{0,8},{2,10},{4,12},{6,14},{8,0},{10,2},{12,4},{14,6},{16,24},{18,... | collective-permute-start | bytes 1880072 | tf_op jit(solution)/shard_map/ppermute | solution.py:288
  455.9 28.3 %collective-permute-start.56 = (f32[12,544]{1,0:T(8,128)S(1)}, f32[12,544]{1,0:T(8,128)S(1)}, u32[]{:S(2)}, u32[]{:S(2)}) collective-permute-start(f32[12,544]{1,0:T(8,128)S(1)} %bitcast_add_fusion), channel_id=1, source_target_pairs={{0,4},{2,6},{4,0},{6,2},{8,12},{10,14},{12,8},{14,10},{16,20},{18,... | collective-permute-start | bytes 78344 | tf_op jit(solution)/shard_map/ppermute | solution.py:288
  456.9 22.9 %collective-permute-start.57 = (bf16[72,3264]{1,0:T(8,128)(2,1)S(1)}, bf16[72,3264]{1,0:T(8,128)(2,1)S(1)}, u32[]{:S(2)}, u32[]{:S(2)}) collective-permute-start(bf16[72,3264]{1,0:T(8,128)(2,1)S(1)} %add_convert_fusion.14), channel_id=1, source_target_pairs={{0,16},{2,18},{4,20},{6,22},{8,24},{10,26},{12,28},{14,30},{16,0},... | collective-permute-start | bytes 1410056 | tf_op jit(solution)/shard_map/ppermute | solution.py:288
  472.6 23.8 %collective-permute-start.54 = (bf16[136,4352]{1,0:T(8,128)(2,1)S(1)}, bf16[136,4352]{1,0:T(8,128)(2,1)S(1)}, u32[]{:S(2)}, u32[]{:S(2)}) collective-permute-start(bf16[136,4352]{1,0:T(8,128)(2,1)S(1)} %pad_maximum_fusion.10), channel_id=1, source_target_pairs={{0,4},{2,6},{4,0},{6,2},{8,12},{10,14},{12,8},{14,10},{16,20},{18,... | collective-permute-start | bytes 3551240 | tf_op jit(solution)/shard_map/ppermute | solution.py:288
  476.1 31.4 %collective-permute-start.53 = (bf16[544,2176]{1,0:T(8,128)(2,1)S(1)}, bf16[544,2176]{1,0:T(8,128)(2,1)S(1)}, u32[]{:S(2)}, u32[]{:S(2)}) collective-permute-start(bf16[544,2176]{1,0:T(8,128)(2,1)S(1)} %pad_maximum_fusion.4), channel_id=1, source_target_pairs={{0,2},{2,0},{4,6},{6,4},{8,10},{10,8},{12,14},{14,12},{16,18},{18,... | collective-permute-start | bytes 7102472 | tf_op jit(solution)/shard_map/ppermute | solution.py:288
  481.2 34.6 %collective-permute-start.52 = (bf16[272,1088]{1,0:T(8,128)(2,1)S(1)}, bf16[272,1088]{1,0:T(8,128)(2,1)S(1)}, u32[]{:S(2)}, u32[]{:S(2)}) collective-permute-start(bf16[272,1088]{1,0:T(8,128)(2,1)S(1)} %pad_maximum_fusion.12), channel_id=1, source_target_pairs={{0,2},{2,0},{4,6},{6,4},{8,10},{10,8},{12,14},{14,12},{16,18},{18,... | collective-permute-start | bytes 1775624 | tf_op jit(solution)/shard_map/ppermute | solution.py:288
  489.8 26.1 %collective-permute-start.60 = (bf16[136,3264]{1,0:T(8,128)(2,1)S(1)}, bf16[136,3264]{1,0:T(8,128)(2,1)S(1)}, u32[]{:S(2)}, u32[]{:S(2)}) collective-permute-start(bf16[136,3264]{1,0:T(8,128)(2,1)S(1)} %pad_maximum_fusion.11), channel_id=1, source_target_pairs={{0,4},{2,6},{4,0},{6,2},{8,12},{10,14},{12,8},{14,10},{16,20},{18,... | collective-permute-start | bytes 2663432 | tf_op jit(solution)/shard_map/ppermute | solution.py:288
  490.5 27.2 %collective-permute-start.61 = (f32[12,544]{1,0:T(8,128)S(1)}, f32[12,544]{1,0:T(8,128)S(1)}, u32[]{:S(2)}, u32[]{:S(2)}) collective-permute-start(f32[12,544]{1,0:T(8,128)S(1)} %add.257), channel_id=1, source_target_pairs={{0,16},{2,18},{4,20},{6,22},{8,24},{10,26},{12,28},{14,30},{16,0},... | collective-permute-start | bytes 78344 | tf_op jit(solution)/shard_map/ppermute | solution.py:288
  498.4 28.0 %collective-permute-start.63 = (bf16[272,4352]{1,0:T(8,128)(2,1)}, bf16[272,4352]{1,0:T(8,128)(2,1)}, u32[]{:S(2)}, u32[]{:S(2)}) collective-permute-start(bf16[272,4352]{1,0:T(8,128)(2,1)} %pad_maximum_fusion.5), channel_id=1, source_target_pairs={{0,2},{2,0},{4,6},{6,4},{8,10},{10,8},{12,14},{14,12},{16,18},{18,... | collective-permute-start | bytes 7102472 | tf_op jit(solution)/shard_map/ppermute | solution.py:288
  (79 other events, 567.1 us)
